TPU v7x, 256 devices: a whole 4x4x8 slice. The times are simulated.
256 devices in a mesh: row: 8 (over y, core), col: 32 (over x, z).
Axes of the slice: x: 4, y: 4, z: 8, core: 2. Of those that a mesh axis runs over, the one named last changes fastest.
Arguments:
- matrix: float32 [8, 8, 256, 2, 32, 256], P(None, 'row', None, None, 'col'), may hold values from -1.2 to 2.5, as said below
Outputs:
- factored: float32 [8, 8, 256, 2, 32, 256], P(None, 'row', None, None, 'col')
Inputs may be any that keep to these rules, and one draw needn't show every extreme that they name: `matrix`: the leading 2 * 256 rows and columns, read from the lower triangle and mirrored, form a symmetric positive definite block.
All inputs are finite; a program needn't handle non-finite values.
Results may differ from a plain program's by a relative error of at most 0.00019.
Values sent between devices are 32-bit elements; how exact they have to be, the bound alone decides.
No kernel may reach another device: no remote copies, remote signals or barrier semaphores. Data moves between devices by JAX's collectives and lax.ppermute only.
A program may use at most 64 MiB of HBM per device.

v0:
```python
import jax
import jax.numpy as jnp
from jax import lax
from jax.sharding import PartitionSpec as P


def spread(value, axis, source):
    kept = jnp.where(lax.axis_index(axis) == source, value, 0).astype(value.dtype)
    return lax.psum(kept, axis)


def factor_diag(blocks, step, row_count, col_count):
    diag_tile = blocks[step // row_count, :, step // col_count, :]
    symmetric = jnp.tril(diag_tile) + jnp.tril(diag_tile, -1).T
    factor_tile = jnp.linalg.cholesky(symmetric)
    identity = jnp.eye(diag_tile.shape[0], dtype=jnp.float32)
    inverse = lax.linalg.triangular_solve(factor_tile, identity, left_side=True, lower=True)
    return (factor_tile, inverse)


def apply_update(blocks, rows_panel, cols_panel, tile_rows, tile_cols, step):
    product = jnp.einsum("aik,bjk->aibj", rows_panel, cols_panel, precision=lax.Precision.HIGHEST)
    keep_mask = (tile_rows[:, None] >= tile_cols[None, :]) & (tile_cols[None, :] > step)
    return jnp.where(keep_mask[:, None, :, None], blocks - product, blocks)


def on_device(matrix):
    shard_rows, _, width, shard_cols, _, _ = matrix.shape
    blocks = matrix.reshape(shard_rows, width, shard_cols, width)
    row_count = lax.axis_size("row")
    col_count = lax.axis_size("col")
    row_index = lax.axis_index("row")
    col_index = lax.axis_index("col")
    tile_rows = jnp.arange(shard_rows, dtype=jnp.int32) * row_count + row_index
    tile_cols = jnp.arange(shard_cols, dtype=jnp.int32) * col_count + col_index

    def panel_step(blocks, step):
        local_col = step // col_count
        column = blocks[:, :, local_col, :]
        factor_tile, inverse = factor_diag(blocks, step, row_count, col_count)
        inverse = spread(inverse, "row", step % row_count)
        local_panel = jnp.einsum("aik,jk->aij", column, inverse, precision=lax.Precision.HIGHEST)
        row_panel = spread(local_panel, "col", step % col_count)
        rowsel = tile_rows[:, None, None]
        new_column = jnp.where(
            rowsel > step, local_panel, jnp.where(rowsel == step, factor_tile[None], column)
        )
        new_column = jnp.where(col_index == step % col_count, new_column, column)
        blocks = blocks.at[:, :, local_col, :].set(new_column)
        grouped = row_panel.reshape(shard_cols, col_count // row_count, width, width)
        chosen = lax.dynamic_index_in_dim(grouped, col_index // row_count, 1, keepdims=False)
        col_panel = spread(chosen, "row", col_index % row_count)
        return (blocks, row_panel, col_panel)

    blocks, rows_first, cols_first = panel_step(blocks, 0)
    blocks = apply_update(blocks, rows_first, cols_first, tile_rows, tile_cols, 0)
    blocks, rows_second, cols_second = panel_step(blocks, 1)
    blocks = apply_update(blocks, rows_second, cols_second, tile_rows, tile_cols, 1)
    return blocks.reshape(matrix.shape)


def solution(mesh):
    return jax.shard_map(
        on_device,
        mesh=mesh,
        in_specs=(P(None, "row", None, None, "col", None),),
        out_specs=P(None, "row", None, None, "col", None),
        check_vma=False,
    )
```

profile of v0, /device:TPU:1, one launch (start us, length us, event | category | flops | bytes accessed | tf_op | source)
XLA Modules:
  0.0 758.2 jit_solution(4472650771389267089)
XLA Ops:
  6.6 2.7 copy.33
  9.3 2.0 copy-done
  11.4 1.1 bitcast_add_fusion.3
  12.7 11.7 %cholesky.130 = f32[128,128]{1,0:T(8,128)S(1)} custom-call(f32[128,128]{1,0:T(8,128)S(1)} %cholesky.194), custom_call_target="Cholesky" | custom-call | tf_op jit(solution)/shard_map/jit(cholesky)/cholesky | solution.py:15
  24.4 9.8 %custom-call.13 = f32[1,128,128]{1,2,0:T(8,128)S(1)} custom-call(f32[1,128,128]{2,1,0:T(8,128)S(1)} %get-tuple-element.78), custom_call_target="InvertDiagBlocksLowerTriangular" | custom-call | tf_op jit(solution)/shard_map/jit(cholesky)/cholesky | solution.py:15
  34.8 11.7 %cholesky.147 = f32[128,128]{1,0:T(8,128)S(1)} custom-call(f32[128,128]{1,0:T(8,128)S(1)} %convolution_subtract_fusion.4), custom_call_target="Cholesky" | custom-call | tf_op jit(solution)/shard_map/jit(cholesky)/cholesky | solution.py:15
  46.5 0.7 compare_reduce_fusion.2
  48.5 15.9 %while.6 = (s32[]{:T(128)}, f32[256,256]{1,0:T(8,128)S(1)}, s32[2,2]{1,0:T(2,128)S(1)}, f32[2,128,128]{2,1,0:T(8,128)S(1)}, s32[]{:T(128)}) while((s32[]{:T(128)}, f32[256,256]{1,0:T(8,128)S(1)}, s32[2,2]{1,0:T(2,128)S(1)}, f32[2,128,128]{2,1,0:T(8,128)S(1)}, s32[]{:T(128)}) %tuple.59), condition=%wide.while_cond.2, body=%wide.while_body.2.sunk | while | flops 2 | bytes 131181 | solution.py:17
  60.7 0.6 fusion.46
  61.2 1.3 bitcast_dynamic-update-slice_fusion.6
  62.6 0.6 fusion.46
  63.1 1.3 bitcast_dynamic-update-slice_fusion.6
  64.4 19.7 %custom-call.14 = f32[2,128,128]{1,2,0:T(8,128)S(1)} custom-call(f32[2,128,128]{2,1,0:T(8,128)S(1)} %get-tuple-element.45), custom_call_target="InvertDiagBlocksLowerTriangular" | custom-call | tf_op jit(solution)/shard_map/triangular_solve/custom-call.0 | solution.py:17
  84.7 0.3 fusion.28
  85.0 0.7 maximum_select_fusion
  85.8 66.9 %all-reduce.8.cloned.1.call-done = f32[256,256]{1,0:T(8,128)} async-done(((f32[256,256]{1,0:T(8,128)}), f32[256,256]{1,0:T(8,128)}) %all-reduce.8.cloned.1.call-update) | async-done | bytes 262160 | tf_op jit(solution)/shard_map/psum | solution.py:9
  152.7 4.9 bitcast_select_fusion
  158.0 3.0 slice_bitcast_fusion.1
  161.0 147.7 %all-reduce.10.cloned.1.call-done = f32[8,256,256]{2,1,0:T(8,128)} async-done(((f32[8,256,256]{2,1,0:T(8,128)}), f32[8,256,256]{2,1,0:T(8,128)}) %all-reduce.10.cloned.1.call-update) | async-done | bytes 2097168 | tf_op jit(solution)/shard_map/psum | solution.py:9
  308.7 1.9 fusion.5
  310.6 3.3 bitcast_dynamic-update-slice_fusion.3
  313.9 62.5 %all-reduce.12.cloned.1.call-done = f32[2,256,256]{2,1,0:T(8,128)} async-done(((f32[2,256,256]{2,1,0:T(8,128)}), f32[2,256,256]{2,1,0:T(8,128)}) %all-reduce.12.cloned.1.call-update) | async-done | bytes 524304 | tf_op jit(solution)/shard_map/psum | solution.py:9
  376.4 7.0 convolution_subtract_fusion
  383.5 0.7 copy_select_fusion
  384.2 2.0 copy-done.2
  386.4 1.1 bitcast_add_fusion.1
  387.6 11.7 %cholesky.164 = f32[128,128]{1,0:T(8,128)S(1)} custom-call(f32[128,128]{1,0:T(8,128)S(1)} %cholesky.197), custom_call_target="Cholesky" | custom-call | tf_op jit(solution)/shard_map/jit(cholesky)/cholesky | solution.py:15
  399.4 9.8 %custom-call.15 = f32[1,128,128]{1,2,0:T(8,128)S(1)} custom-call(f32[1,128,128]{2,1,0:T(8,128)S(1)} %get-tuple-element.74), custom_call_target="InvertDiagBlocksLowerTriangular" | custom-call | tf_op jit(solution)/shard_map/jit(cholesky)/cholesky | solution.py:15
  409.7 11.9 %cholesky.181 = f32[128,128]{1,0:T(8,128)S(1)} custom-call(f32[128,128]{1,0:T(8,128)S(1)} %convolution_subtract_fusion.3), custom_call_target="Cholesky" | custom-call | tf_op jit(solution)/shard_map/jit(cholesky)/cholesky | solution.py:15
  421.6 0.6 compare_reduce_fusion
  422.2 0.7 compare_reduce_fusion.1
  424.2 4.1 while.7
  424.3 0.7 fusion.47
  424.9 1.3 bitcast_dynamic-update-slice_fusion.7
  426.3 0.7 fusion.47
  427.0 1.3 bitcast_dynamic-update-slice_fusion.7
  428.3 19.7 %custom-call.16 = f32[2,128,128]{1,2,0:T(8,128)S(1)} custom-call(f32[2,128,128]{2,1,0:T(8,128)S(1)} %get-tuple-element.46), custom_call_target="InvertDiagBlocksLowerTriangular" | custom-call | tf_op jit(solution)/shard_map/triangular_solve/custom-call.0 | solution.py:17
  448.0 0.3 fusion.19
  448.9 0.7 maximum_select_fusion.1
  449.7 64.3 %all-reduce.14.cloned.1.call-done = f32[256,256]{1,0:T(8,128)} async-done(((f32[256,256]{1,0:T(8,128)}), f32[256,256]{1,0:T(8,128)}) %all-reduce.14.cloned.1.call-update) | async-done | bytes 262160 | tf_op jit(solution)/shard_map/psum | solution.py:9
  514.0 4.8 broadcast_select_fusion
  519.1 3.0 slice_bitcast_fusion
  522.1 147.8 %all-reduce.16.cloned.1.call-done = f32[8,256,256]{2,1,0:T(8,128)} async-done(((f32[8,256,256]{2,1,0:T(8,128)}), f32[8,256,256]{2,1,0:T(8,128)}) %all-reduce.16.cloned.1.call-update) | async-done | bytes 2097168 | tf_op jit(solution)/shard_map/psum | solution.py:9
  669.9 1.9 fusion.4
  671.8 3.3 bitcast_dynamic-update-slice_fusion.2
  675.1 62.5 %all-reduce.18.cloned.1.call-done = f32[2,256,256]{2,1,0:T(8,128)} async-done(((f32[2,256,256]{2,1,0:T(8,128)}), f32[2,256,256]{2,1,0:T(8,128)}) %all-reduce.18.cloned.1.call-update) | async-done | bytes 524304 | tf_op jit(solution)/shard_map/psum | solution.py:9
  737.6 6.9 fusion
  744.6 6.3 copy.16
  (60 shorter events, 4.0 us)
Async XLA Ops:
  6.5 146.1 %all-reduce.8.cloned.1.call-start = ((), (), s32[]{:S(2)}) async-start(), calls=%async_computation | async-start | bytes 524288 | tf_op jit(solution)/shard_map/psum | solution.py:9
  9.3 2.0 copy-start
  85.8 222.9 %all-reduce.10.cloned.1.call-start = ((), (), s32[]{:S(2)}) async-start(), calls=%async_computation.1 | async-start | bytes 4194304 | tf_op jit(solution)/shard_map/psum | solution.py:9
  157.6 218.9 %all-reduce.12.cloned.1.call-start = ((), (), s32[]{:S(2)}) async-start(), calls=%async_computation.2 | async-start | bytes 1048576 | tf_op jit(solution)/shard_map/psum | solution.py:9
  310.6 203.4 %all-reduce.14.cloned.1.call-start = ((), (), s32[]{:S(2)}) async-start(), calls=%async_computation.3 | async-start | bytes 524288 | tf_op jit(solution)/shard_map/psum | solution.py:9
  376.4 7.0 copy-start.1
  384.2 2.0 copy-start.2
  449.6 220.2 %all-reduce.16.cloned.1.call-start = ((), (), s32[]{:S(2)}) async-start(), calls=%async_computation.4 | async-start | bytes 4194304 | tf_op jit(solution)/shard_map/psum | solution.py:9
  518.8 218.8 %all-reduce.18.cloned.1.call-start = ((), (), s32[]{:S(2)}) async-start(), calls=%async_computation.5 | async-start | bytes 1048576 | tf_op jit(solution)/shard_map/psum | solution.py:9
Sparse Core Ops, SparseCore 0:
  85.9 66.7 all-reduce.7
  157.7 150.9 all-reduce.9
  311.0 65.3 all-reduce.11
  449.8 64.1 all-reduce.13
  518.9 150.9 all-reduce.15
  672.2 65.3 all-reduce.17
where the time goes:
time: 768 us; the launch traced here: 758 us
  waiting for transfers between devices  552 us (72%)
  other arithmetic  123 us (16%)
  local copies, waits for them, and re-layouts  27.7 us (4%)
  matrix products  26.3 us (3%)
  between operations  16.8 us (2%)
  loops' own time  12.2 us (2%)
    psum x6, waiting for transfers between devices, spread(): return lax.psum(kept, axis)  552 us
    another operation x13, other arithmetic, factor_diag(): factor_tile = jnp.linalg.cholesky(symmetric)  68.8 us
    another operation x5, other arithmetic, factor_diag(): lax.linalg.triangular_solve(factor_tile, identity, left_side=True, lower=...  39.4 us
  transfers between devices with their start and end apart: 6, of which 6 were waited for; matrix products, arithmetic and copies ran while one was open for 2% of the time, Pallas kernels for 0%

commit v1 on v0

v1 whole, which is shorter than its diff:
```python
import jax
import jax.numpy as jnp
from jax import lax
from jax.experimental import pallas as pl
from jax.experimental.pallas import tpu as pltpu
from jax.sharding import PartitionSpec as P

F32 = jnp.float32
BF16 = jnp.bfloat16
N = 256
SLAB = 64
NY, NC, NX, NZ = 4, 2, 4, 8


def flat(y, c, x, z):
    return ((y * NC + c) * NX + x) * NZ + z


def pairs(fn):
    found = []
    for y in range(NY):
        for c in range(NC):
            for x in range(NX):
                for z in range(NZ):
                    to = fn(y, c, x, z)
                    if to is not None:
                        found.append((flat(y, c, x, z), flat(*to)))
    return found


def send(value, fn):
    return lax.ppermute(value, ("row", "col"), pairs(fn))


def sweep_slab(slab):
    left = [g[:, :128] for g in slab]
    right = [g[:, 128:] for g in slab]
    lane = lax.broadcasted_iota(jnp.int32, (8, 128), 1)
    sub = lax.broadcasted_iota(jnp.int32, (8, 128), 0)

    def splat(v):
        return jnp.broadcast_to(v, (8, 128))

    def assemble(rows):
        out = rows[0]
        for i in range(1, 8):
            out = jnp.where(sub == i, rows[i], out)
        return out

    z_left, z_right, u_left = [], [], []
    for s in range(len(slab)):
        a0, a1 = left[s], right[s]
        o = 8 * s
        cols = [splat(a0[:, o + j : o + j + 1]) for j in range(8)]
        d = [[splat(cols[j][i : i + 1, :]) for j in range(i + 1)] for i in range(8)]
        r0 = [splat(a0[i : i + 1, :]) for i in range(8)]
        r1 = [splat(a1[i : i + 1, :]) for i in range(8)]
        in_block = (lane >= o) & (lane < o + 8)
        r = []
        l = [[None] * 8 for _ in range(8)]
        zl, zr, ul = [], [], []
        for k in range(8):
            rk = lax.rsqrt(d[k][k])
            r.append(rk)
            for i in range(k + 1, 8):
                l[i][k] = d[i][k] * rk
            for j in range(k + 1, 8):
                for i in range(j, 8):
                    d[i][j] = d[i][j] - l[i][k] * l[j][k]
            x0 = jnp.where(in_block, jnp.where(lane == o + k, 1.0, 0.0).astype(F32), r0[k])
            x1 = r1[k]
            x2 = r0[k]
            for m in range(k):
                x0 = x0 - l[k][m] * zl[m]
                x1 = x1 - l[k][m] * zr[m]
                x2 = x2 - l[k][m] * ul[m]
            zl.append(x0 * rk)
            zr.append(x1 * rk)
            ul.append(x2 * rk)
        z_left.append(assemble(zl))
        z_right.append(assemble(zr))
        u_left.append(assemble(ul))
        for t in range(s + 1, len(slab)):
            coef = []
            for k in range(8):
                c = splat(left[t][:, o + k : o + k + 1])
                for m in range(k):
                    c = c - l[k][m] * coef[m]
                coef.append(c * r[k])
            x0 = jnp.where(in_block, 0.0, left[t])
            x1 = right[t]
            for k in range(8):
                x0 = x0 - coef[k] * zl[k]
                x1 = x1 - coef[k] * zr[k]
            left[t] = x0
            right[t] = x1
    return z_left, z_right, u_left


def factor_tile(m_ref, u_ref):
    row = lax.broadcasted_iota(jnp.int32, (N, N), 0)
    lan = lax.broadcasted_iota(jnp.int32, (N, N), 1)
    row_s = lax.broadcasted_iota(jnp.int32, (SLAB, N), 0)
    lan_s = lax.broadcasted_iota(jnp.int32, (SLAB, N), 1)

    @pl.loop(0, N // SLAB)
    def _(b):
        o = b * SLAB
        rows = pl.ds(pl.multiple_of(o, SLAB), SLAB)
        slab = pltpu.roll(m_ref[rows, :], N - o, 1)
        zl, zr, ul = sweep_slab([slab[8 * g : 8 * g + 8, :] for g in range(SLAB // 8)])
        zr = jnp.concatenate(zr, 0)
        z = jnp.concatenate([jnp.concatenate(zl, 0), zr], 1)
        u = jnp.concatenate([jnp.concatenate(ul, 0), zr], 1)
        z = jnp.where((lan_s < SLAB) & (lan_s > row_s), 0.0, z)
        z = pltpu.roll(z, o, 1)
        u = pltpu.roll(u, o, 1)
        u_ref[rows, :] = u

        @pl.when(b < N // SLAB - 1)
        def _():
            coef = jnp.where(lan_s >= o + SLAB, u, 0.0)
            update = lax.dot_general(
                coef, z, (((0,), (0,)), ((), ())), precision=lax.Precision.HIGHEST, preferred_element_type=F32
            )
            m = m_ref[...]
            m = jnp.where((row >= o + SLAB) & (lan >= o) & (lan < o + SLAB), 0.0, m)
            m_ref[...] = m - update

        m_ref[rows, :] = z


def dot_nt(a, b):
    return lax.dot_general(a, b, (((1,), (1,)), ((), ())), precision=lax.Precision.HIGHEST, preferred_element_type=F32)


def factor_kernel(packed_ref, a10_ref, l0_ref, w0_ref, p10_ref, l1_ref, w1_ref, m_ref, u_ref):
    row = lax.broadcasted_iota(jnp.int32, (N, N), 0)
    lan = lax.broadcasted_iota(jnp.int32, (N, N), 1)

    def read_out(l_ref, w_ref):
        l_ref[...] = jnp.where(row >= lan, u_ref[...].T, 0.0)
        w_ref[...] = jnp.where(row >= lan, m_ref[...], 0.0)

    packed = packed_ref[:N, :]
    turned = packed.T
    m_ref[...] = jnp.where(row >= lan, packed, turned)
    factor_tile(m_ref, u_ref)
    read_out(l0_ref, w0_ref)
    p10 = dot_nt(a10_ref[:N, :], w0_ref[...])
    p10_ref[...] = p10
    packed = packed_ref[:N, :]
    diag = jnp.broadcast_to(packed_ref[N : N + 1, :], (N, N))
    second = jnp.where(row == lan, diag, jnp.where(row < lan, packed, packed.T))
    m_ref[...] = second - dot_nt(p10, p10)
    factor_tile(m_ref, u_ref)
    read_out(l1_ref, w1_ref)


def factor(packed, a10):
    return pl.pallas_call(
        factor_kernel,
        out_shape=[jax.ShapeDtypeStruct((N, N), F32)] * 5,
        in_specs=[pl.BlockSpec(memory_space=pltpu.VMEM)] * 2,
        out_specs=[pl.BlockSpec(memory_space=pltpu.VMEM)] * 5,
        scratch_shapes=[pltpu.VMEM((N, N), F32)] * 2,
        compiler_params=pltpu.CompilerParams(vmem_limit_bytes=24 << 20),
        cost_estimate=pl.CostEstimate(flops=10**9, bytes_accessed=60 << 20, transcendentals=0),
        name="factor",
    )(packed, a10)


def order_kernel(z_ref, *refs):
    pieces, out_ref, sem = refs[:NZ], refs[NZ], refs[NZ + 1]
    z = z_ref[0]
    copies = []
    for d in range(NZ):
        slot = lax.rem(z + (NZ - d), NZ)
        for c in range(2):
            copies.append(
                pltpu.make_async_copy(
                    pieces[d].at[c],
                    out_ref.at[pl.ds(pl.multiple_of(slot * 64, 64), 64), pl.ds(c * N, N)],
                    sem.at[d, c],
                )
            )
    for copy in copies:
        copy.start()
    for copy in copies:
        copy.wait()


def order(z, pieces):
    return pl.pallas_call(
        order_kernel,
        out_shape=jax.ShapeDtypeStruct((2 * N, 2 * N), F32),
        in_specs=[pl.BlockSpec(memory_space=pltpu.SMEM)] + [pl.BlockSpec(memory_space=pl.ANY)] * NZ,
        out_specs=pl.BlockSpec(memory_space=pl.ANY),
        scratch_shapes=[pltpu.SemaphoreType.DMA((NZ, 2))],
        cost_estimate=pl.CostEstimate(flops=0, bytes_accessed=2 << 20, transcendentals=0),
        name="order",
    )(z, *pieces)


def split(v):
    hi = v.astype(BF16)
    return hi, (v - hi.astype(F32)).astype(BF16)


def update_kernel(
    amap_ref, info_ref, m_ref, q0, q1, q2, q3, own_ref, other_ref, l0_ref, w0_ref, p10_ref, l1_ref, w1_ref,
    o_ref, w0t, w1t, p10t, x_s, chi, clo, p_s,
):
    t = pl.program_id(0)
    p, q, keep_own = info_ref[0], info_ref[1], info_ref[2]
    a = amap_ref[t]
    i = a * 8 + p

    def dot_hi(u, v):
        return jnp.dot(u, v, precision=lax.Precision.HIGHEST, preferred_element_type=F32)

    def solve(x):
        first = dot_hi(x[:, :N], w0t[...])
        rest = x[:, N:] - dot_hi(first, p10t[...])
        return first, dot_hi(rest, w1t[...])

    @pl.when(t == 0)
    def _():
        w0t[...] = w0_ref[...].T
        w1t[...] = w1_ref[...].T
        p10t[...] = p10_ref[...].T
        for b in range(2):
            rows = pl.ds(b * N, N)

            @pl.when(keep_own == 1)
            def _():
                x_s[...] = own_ref[rows, :]

            @pl.when(keep_own == 0)
            def _():
                x_s[...] = other_ref[rows, :]

            for k, panel in enumerate(solve(x_s[...])):
                hi, lo = split(panel.T)
                chi[pl.ds(k * N, N), pl.ds(b * N, N)] = hi
                clo[pl.ds(k * N, N), pl.ds(b * N, N)] = lo

    for d, ref in enumerate((q0, q1, q2, q3)):
        @pl.when(t // 2 == d)
        def _(ref=ref):
            x_s[...] = ref[...]

    first, second = solve(x_s[...])
    p_s[:, :N] = first
    p_s[:, N:] = second

    def put(b, value):
        for half in range(2):
            o_ref[pl.ds(2 * b + half, N, stride=4), :] = value[:, half * 128 : half * 128 + 128]

    def get(b):
        return jnp.concatenate([m_ref[pl.ds(2 * b + half, N, stride=4), :] for half in range(2)], 1)

    for b in range(2):
        j = 32 * b + q
        is_first = j == 0
        is_second = j == 1
        updates = (j > 1) & (i >= j)

        @pl.when(updates)
        def _(b=b):
            phi, plo = split(p_s[...])
            cols = pl.ds(b * N, N)
            chi_b, clo_b = chi[:, cols], clo[:, cols]

            def dot16(u, v):
                return jnp.dot(u, v, preferred_element_type=F32)

            product = dot16(plo, chi_b) + dot16(phi, clo_b) + dot16(phi, chi_b)
            put(b, get(b) - product)

        @pl.when((j > 1) & (i < j) | is_second & (i < 1))
        def _(b=b):
            put(b, get(b))

        if b == 0:
            @pl.when(is_first & (i == 0))
            def _():
                put(0, l0_ref[...])

            @pl.when(is_first & (i > 0))
            def _():
                put(0, p_s[:, :N])

            @pl.when(is_second & (i == 1))
            def _():
                put(0, l1_ref[...])

            @pl.when(is_second & (i > 1))
            def _():
                put(0, p_s[:, N:])


def update(amap, info, flat_blocks, quarters, own, other, l0, w0, p10, l1, w1):
    whole = lambda shape: pl.BlockSpec(shape, lambda t, amap, info: (0, 0))
    quarter = lambda d: pl.BlockSpec((N, 2 * N), lambda t, amap, info: (jnp.clip(t - 2 * d, 0, 1), 0))
    tiles = pl.BlockSpec((4 * N, 128), lambda t, amap, info: (amap[t], 0))
    return pl.pallas_call(
        update_kernel,
        grid_spec=pltpu.PrefetchScalarGridSpec(
            num_scalar_prefetch=2,
            grid=(8,),
            in_specs=[tiles] + [quarter(d) for d in range(4)] + [whole((2 * N, 2 * N))] * 2 + [whole((N, N))] * 5,
            out_specs=tiles,
            scratch_shapes=[pltpu.VMEM((N, N), F32)] * 3
            + [pltpu.VMEM((N, 2 * N), F32)]
            + [pltpu.VMEM((2 * N, 2 * N), BF16)] * 2
            + [pltpu.VMEM((N, 2 * N), F32)],
        ),
        out_shape=jax.ShapeDtypeStruct(flat_blocks.shape, F32),
        compiler_params=pltpu.CompilerParams(vmem_limit_bytes=48 << 20, dimension_semantics=("arbitrary",)),
        cost_estimate=pl.CostEstimate(flops=6 * 10**9, bytes_accessed=16 << 20, transcendentals=0),
        name="update",
    )(amap, info, flat_blocks, *quarters, own, other, l0, w0, p10, l1, w1)


def on_device(matrix):
    row_index = lax.axis_index("row")
    col_index = lax.axis_index("col")
    y, core = row_index // NC, row_index % NC
    x, z = col_index // NZ, col_index % NZ
    blocks = matrix.reshape(8, N, 2, N)
    flat_blocks = matrix.reshape(8 * N * 4, 128)
    column = blocks[:, :, 0, :]

    tile = column[0]
    second = send(tile, lambda y, c, x, z: (0, 0, 0, 0) if (y, c, x, z) == (0, 1, 0, 1) else None)
    lower = jnp.tril(tile) + jnp.triu(second.T, 1)
    extra = jnp.concatenate([jnp.diagonal(second)[None, :], jnp.zeros((7, N), F32)], 0)
    item = jnp.where(core == 0, jnp.concatenate([lower, extra], 0), jnp.concatenate([tile, jnp.zeros((8, N), F32)], 0))

    arrived = [
        send(column[d::4], lambda y, c, x, z, d=d: (y, c, d, z) if x == 0 and z < 2 else None) for d in (1, 2, 3)
    ]

    def spread(item, mine, ops):
        got = [send(item, fn) for fn in ops]
        out = jnp.where(mine, item, 0.0)
        for g in got:
            out = out + g
        return out

    item = spread(
        item, (y == 0) & (x == 0) & (z == 0),
        [lambda y, c, x, z, d=d: (d, c, 0, 0) if (y, x, z) == (0, 0, 0) else None for d in (1, 2, 3)],
    )
    item = spread(
        item, (x == 0) & (z == 0),
        [lambda y, c, x, z, d=d: (y, c, 0, d) if (x, z) == (0, 0) else None for d in (2, 4, 6)],
    )
    item = spread(
        item, (x == 0) & (z % 2 == 0),
        [lambda y, c, x, z: (y, c, 0, z + 1) if x == 0 and z % 2 == 0 else None],
    )
    item = spread(
        item, x == 0,
        [lambda y, c, x, z, d=d: (y, c, d, z) if x == 0 else None for d in (1, 2, 3)],
    )
    swapped = send(item, lambda y, c, x, z: (y, 1 - c, x, z))

    quarter = jnp.where((x == 0) & (z < 2), column[0::4], 0.0) + arrived[0] + arrived[1] + arrived[2]
    parts = quarter.reshape(NZ, 64, N)
    landed = [lax.dynamic_index_in_dim(parts, z, 0, keepdims=False)]
    for d in range(1, NZ):
        part = lax.dynamic_index_in_dim(parts, (z + d) % NZ, 0, keepdims=False)
        landed.append(send(part, lambda y, c, x, z, d=d: (y, c, x, (z + d) % NZ) if z < 2 else None))
    landed = jnp.stack(landed)
    piece = jnp.stack(
        [
            lax.dynamic_index_in_dim(landed, z, 0, keepdims=False),
            lax.dynamic_index_in_dim(landed, (z + NZ - 1) % NZ, 0, keepdims=False),
        ]
    )

    pieces = [piece] + [send(piece, lambda y, c, x, z, d=d: (y, c, x, (z + d) % NZ)) for d in range(1, NZ)]
    mine = order(z.astype(jnp.int32)[None], pieces)
    quarters = [mine] + [send(mine, lambda y, c, x, z, d=d: (y, c, (x + d) % NX, z)) for d in (1, 2, 3)]

    chosen = [
        send(mine, lambda y, c, x, z, d=d: ((y + d) % NY, c, x, z) if y * NC + c == z else None) for d in (1, 2, 3)
    ]
    own = jnp.where(row_index == z, mine, 0.0) + chosen[0] + chosen[1] + chosen[2]
    other = send(own, lambda y, c, x, z: (y, 1 - c, x, z))

    packed, a10 = jnp.where(core == 0, item, swapped), jnp.where(core == 0, swapped, item)
    packed, a10, _ = lax.optimization_barrier((packed, a10, mine))
    l0, w0, p10, l1, w1 = factor(packed, a10)

    steps = jnp.arange(8, dtype=jnp.int32)
    amap = (x.astype(jnp.int32) - steps // 2 + NX) % NX + 4 * (steps % 2)
    info = jnp.stack([row_index, col_index, (core == z % 2).astype(jnp.int32)]).astype(jnp.int32)
    out = update(amap, info, flat_blocks, quarters, own, other, l0, w0, p10, l1, w1)
    return out.reshape(matrix.shape)


def solution(mesh):
    return jax.shard_map(
        on_device,
        mesh=mesh,
        in_specs=(P(None, "row", None, None, "col", None),),
        out_specs=P(None, "row", None, None, "col", None),
        check_vma=False,
    )
```

time: 768 us -> 240 us (0.31)
  waiting for transfers between devices: 552 us -> 52.9 us
  other arithmetic: 123 us -> 8.91 us
  starting transfers between devices: 0.46 us -> 93.3 us
  Pallas kernels: 0 us -> 72.9 us
  matrix products: 26.3 us -> 0 us
  local copies, waits for them, and re-layouts: 27.7 us -> 7.68 us
  between operations: 16.8 us -> 0.69 us
  loops' own time: 12.2 us -> 0 us
    psum x6 -> x0, waiting for transfers between devices: 552 us -> none  [spread(): return lax.psum(kept, axis)]
    another operation x18 -> x2, other arithmetic: 108 us -> 0.09 us  [the longest x1 0.08 us: on_device(): jnp.stack([row_index, col_index, (core == z % 2).astype(jnp.int32)])]
    ppermute x0 -> x36, starting transfers between devices: none -> 93.3 us  [send(): return lax.ppermute(value, ('row', 'col'), pairs(fn))]
    pallas_call x0 -> x3, Pallas kernels: none -> 72.9 us  [the longest x1 33 us: order(): pl.pallas_call(order_kernel, out_shape=jax.ShapeDtypeStruct((2 * N, 2 * N...]
    ppermute x0 -> x36, waiting for transfers between devices: none -> 52.9 us  [send(): return lax.ppermute(value, ('row', 'col'), pairs(fn))]
    dot_general x4 -> x0, matrix products: 23.6 us -> none  [the longest x2 14 us: apply_update(): jnp.einsum('aik,bjk->aibj', rows_panel, cols_panel, precision=lax.Precisi...]
    another operation x2 -> x0, loops' own time: 12.2 us -> none  [factor_diag(): lax.linalg.triangular_solve(factor_tile, identity, left_side=True, lower=...]
    another operation x19 -> x1, local copies, waits for them, and re-layouts: 7.9 us -> 0.01 us  [on_device(): landed = jnp.stack(landed)]
  transfers between devices with their start and end apart: 6 -> 36, of which waited for: 6 -> 14; matrix products, arithmetic and copies ran while one was open for 2% -> 6% of each run, Pallas kernels for 0% -> 22%
where the time goes in v1:
time: 240 us; the launch traced here: 236 us
  starting transfers between devices  93.3 us (39%)
  Pallas kernels  72.9 us (30%)
  waiting for transfers between devices  52.9 us (22%)
  other arithmetic  8.91 us (4%)
  local copies, waits for them, and re-layouts  7.68 us (3%)
    ppermute x36, starting transfers between devices, send(): return lax.ppermute(value, ('row', 'col'), pairs(fn))  93.3 us
    ppermute x36, waiting for transfers between devices, send(): return lax.ppermute(value, ('row', 'col'), pairs(fn))  52.9 us
    pallas_call x1, Pallas kernels, order(): pl.pallas_call(order_kernel, out_shape=jax.ShapeDtypeStruct((2 * N, 2 * N...  33 us
    pallas_call x1, Pallas kernels, update(): pl.pallas_call(update_kernel, grid_spec=pltpu.PrefetchScalarGridSpec(num_...  20 us
    pallas_call x1, Pallas kernels, factor(): pl.pallas_call(factor_kernel, out_shape=[jax.ShapeDtypeStruct((N, N), F32...  20 us
  transfers between devices with their start and end apart: 36, of which 14 were waited for; matrix products, arithmetic and copies ran while one was open for 6% of the time, Pallas kernels for 22%

profile of v1, /device:TPU:1, one launch (start us, length us, event | category | flops | bytes accessed | tf_op | source)
XLA Modules:
  0.0 236.4 jit_solution(7112391541216543529)
XLA Ops:
  0.0 2.7 %copy.12 = f32[8,1,256,2,1,256]{5,2,3,0,4,1:T(8,128)S(1)} copy(f32[8,1,256,2,1,256]{5,4,3,2,1,0:T(1,128)} %param.1) | data formatting | bytes 8388608 | tf_op args[0]
  4.8 4.7 %collective-permute-start = (f32[2,256,256]{2,1,0:T(8,128)}, f32[2,256,256]{2,1,0:T(8,128)}, u32[]{:S(2)}, u32[]{:S(2)}) collective-permute-start(f32[2,256,256]{2,1,0:T(8,128)} %get-tuple-element.19), channel_id=1, source_target_pairs={{0,8},{1,9},{32,40},{33,41},{64,72},{65,73},{96,104},{97,105},{128... | collective-permute-start | bytes 1572872 | tf_op jit(solution)/shard_map/ppermute | solution.py:32
  9.6 2.7 %collective-permute-start.2 = (f32[2,256,256]{2,1,0:T(8,128)}, f32[2,256,256]{2,1,0:T(8,128)}, u32[]{:S(2)}, u32[]{:S(2)}) collective-permute-start(f32[2,256,256]{2,1,0:T(8,128)} %get-tuple-element.20), channel_id=1, source_target_pairs={{0,24},{1,25},{32,56},{33,57},{64,88},{65,89},{96,120},{97,121},{1... | collective-permute-start | bytes 1572872 | tf_op jit(solution)/shard_map/ppermute | solution.py:32
  12.3 2.1 collective-permute-start.1
  14.8 2.3 gather_fusion
  17.5 4.7 %collective-permute-start.27 = (f32[264,256]{1,0:T(8,128)S(1)}, f32[264,256]{1,0:T(8,128)S(1)}, u32[]{:S(2)}, u32[]{:S(2)}) collective-permute-start(f32[264,256]{1,0:T(8,128)S(1)} %pad_select_fusion), channel_id=1, source_target_pairs={{0,192},{32,224}} | collective-permute-start | bytes 811016 | tf_op jit(solution)/shard_map/ppermute | solution.py:32
  22.1 1.3 collective-permute-start.26
  23.5 1.3 collective-permute-start.25
  24.8 5.8 %collective-permute-done.1 = f32[2,256,256]{2,1,0:T(8,128)} collective-permute-done((f32[2,256,256]{2,1,0:T(8,128)}, f32[2,256,256]{2,1,0:T(8,128)}, u32[]{:S(2)}, u32[]{:S(2)}) %collective-permute-start.1) | collective-permute-done | bytes 524320 | tf_op jit(solution)/shard_map/ppermute | solution.py:32
  30.6 1.5 add_add_fusion.1
  32.2 1.9 collective-permute-start.9
  34.1 1.3 collective-permute-start.8
  35.4 1.3 collective-permute-start.7
  36.7 1.3 collective-permute-start.6
  38.0 5.5 %collective-permute-start.3 = (f32[64,256]{1,0:T(8,128)S(1)}, f32[64,256]{1,0:T(8,128)S(1)}, u32[]{:S(2)}, u32[]{:S(2)}) collective-permute-start(f32[64,256]{1,0:T(8,128)S(1)} %get-tuple-element.32), channel_id=1, source_target_pairs={{0,1},{1,2},{8,9},{9,10},{16,17},{17,18},{24,25},{25,26},{32,33},{... | collective-permute-start | bytes 196616 | tf_op jit(solution)/shard_map/ppermute | solution.py:32
  43.6 1.2 collective-permute-done.3
  44.8 4.2 %collective-permute-start.4 = (f32[64,256]{1,0:T(8,128)S(1)}, f32[64,256]{1,0:T(8,128)S(1)}, u32[]{:S(2)}, u32[]{:S(2)}) collective-permute-start(f32[64,256]{1,0:T(8,128)S(1)} %get-tuple-element.31), channel_id=1, source_target_pairs={{0,2},{1,3},{8,10},{9,11},{16,18},{17,19},{24,26},{25,27},{32,34},... | collective-permute-start | bytes 196616 | tf_op jit(solution)/shard_map/ppermute | solution.py:32
  49.0 1.3 collective-permute-done.4
  50.3 3.7 %collective-permute-start.5 = (f32[64,256]{1,0:T(8,128)S(1)}, f32[64,256]{1,0:T(8,128)S(1)}, u32[]{:S(2)}, u32[]{:S(2)}) collective-permute-start(f32[64,256]{1,0:T(8,128)S(1)} %get-tuple-element.30), channel_id=1, source_target_pairs={{0,3},{1,4},{8,11},{9,12},{16,19},{17,20},{24,27},{25,28},{32,35},... | collective-permute-start | bytes 196616 | tf_op jit(solution)/shard_map/ppermute | solution.py:32
  54.1 1.3 collective-permute-done.5
  55.4 1.3 collective-permute-start.30
  57.0 5.3 %collective-permute-start.14 = (f32[2,64,256]{2,1,0:T(8,128)S(1)}, f32[2,64,256]{2,1,0:T(8,128)S(1)}, u32[]{:S(2)}, u32[]{:S(2)}) collective-permute-start(f32[2,64,256]{2,1,0:T(8,128)S(1)} %pad_maximum_fusion.refs_0_), channel_id=1, source_target_pairs={{0,5},{1,6},{2,7},{3,0},{4,1},{5,2},{6,3},{7,4},{8,13},{9,14},{10,... | collective-permute-start | bytes 393224 | tf_op jit(solution)/shard_map/ppermute | solution.py:32
  62.6 1.3 collective-permute-done.16.refs_7_
  63.8 2.2 collective-permute-start.12
  66.0 4.8 %collective-permute-done.15.refs_6_ = f32[2,64,256]{2,1,0:T(8,128)S(1)} collective-permute-done((f32[2,64,256]{2,1,0:T(8,128)S(1)}, f32[2,64,256]{2,1,0:T(8,128)S(1)}, u32[]{:S(2)}, u32[]{:S(2)}) %collective-permute-start.15) | collective-permute-done | bytes 131104 | tf_op jit(solution)/shard_map/ppermute | solution.py:32
  70.8 1.3 collective-permute-start.11
  72.2 10.4 %collective-permute-done.14.refs_5_ = f32[2,64,256]{2,1,0:T(8,128)S(1)} collective-permute-done((f32[2,64,256]{2,1,0:T(8,128)S(1)}, f32[2,64,256]{2,1,0:T(8,128)S(1)}, u32[]{:S(2)}, u32[]{:S(2)}) %collective-permute-start.14) | collective-permute-done | bytes 131104 | tf_op jit(solution)/shard_map/ppermute | solution.py:32
  82.7 5.0 %collective-permute-done.10.refs_1_ = f32[2,64,256]{2,1,0:T(8,128)S(1)} collective-permute-done((f32[2,64,256]{2,1,0:T(8,128)S(1)}, f32[2,64,256]{2,1,0:T(8,128)S(1)}, u32[]{:S(2)}, u32[]{:S(2)}) %collective-permute-start.10) | collective-permute-done | bytes 131104 | tf_op jit(solution)/shard_map/ppermute | solution.py:32
  88.3 33.0 %order.1.q0 = f32[512,512]{1,0:T(8,128)} custom-call(s32[1]{0:T(128)} %bitcast.4.z_ref, f32[2,64,256]{2,1,0:T(8,128)} %copy-done.1, f32[2,64,256]{2,1,0:T(8,128)} %copy-done.8, f32[2,64,256]{2,1,0:T(8,128)} %copy-done.7, f32[2,64,256]{2,1,0:T(8,128)} %copy-done.6, f32[2,64,256]{2,1,0:T(8,128)} %copy-done.5, f32[2,64,256]{2,1,0:T(8,128)} %copy-done.4, ...), custom_call_target="tpu_custom_call" | custom-call | bytes 2097152 | tf_op jit(solution)/shard_map/order/pallas_call | solution.py:194
  121.3 1.8 collective-permute-start.22
  123.1 1.6 collective-permute-start.21
  124.7 1.6 collective-permute-start.20
  126.4 4.9 %collective-permute-start.29 = (f32[264,256]{1,0:T(8,128)S(1)}, f32[264,256]{1,0:T(8,128)S(1)}, u32[]{:S(2)}, u32[]{:S(2)}) collective-permute-start(f32[264,256]{1,0:T(8,128)S(1)} %add_add_fusion.4), channel_id=1, source_target_pairs={{0,4},{32,36},{64,68},{96,100},{128,132},{160,164},{192,196},{224,... | collective-permute-start | bytes 811016 | tf_op jit(solution)/shard_map/ppermute | solution.py:32
  131.3 1.3 collective-permute-start.28
  132.6 2.0 collective-permute-done.29
  134.7 2.9 %collective-permute-done.28 = f32[264,256]{1,0:T(8,128)S(1)} collective-permute-done((f32[264,256]{1,0:T(8,128)S(1)}, f32[264,256]{1,0:T(8,128)S(1)}, u32[]{:S(2)}, u32[]{:S(2)}) %collective-permute-start.28) | collective-permute-done | bytes 270368 | tf_op jit(solution)/shard_map/ppermute | solution.py:32
  138.4 2.0 collective-permute-start.31
  140.4 5.9 %collective-permute-done.31 = f32[264,256]{1,0:T(8,128)} collective-permute-done((f32[264,256]{1,0:T(8,128)}, f32[264,256]{1,0:T(8,128)}, u32[]{:S(2)}, u32[]{:S(2)}) %collective-permute-start.31) | collective-permute-done | bytes 270368 | tf_op jit(solution)/shard_map/ppermute | solution.py:32
  147.3 1.3 collective-permute-start.34
  148.6 4.2 %collective-permute-start.33 = (f32[264,256]{1,0:T(8,128)S(1)}, f32[264,256]{1,0:T(8,128)S(1)}, u32[]{:S(2)}, u32[]{:S(2)}) collective-permute-start(f32[264,256]{1,0:T(8,128)S(1)} %select_add_fusion), channel_id=1, source_target_pairs={{0,16},{1,17},{2,18},{3,19},{4,20},{5,21},{6,22},{7,23},{32,48},{3... | collective-permute-start | bytes 811016 | tf_op jit(solution)/shard_map/ppermute | solution.py:32
  152.8 1.3 collective-permute-start.32
  154.2 3.3 %add_add_fusion.own_ref = f32[512,512]{1,0:T(8,128)} fusion(f32[512,512]{1,0:T(8,128)} %collective-permute-done.22, f32[512,512]{1,0:T(8,128)} %collective-permute-done.21, f32[512,512]{1,0:T(8,128)} %collective-permute-done.20, f32[512,512]{1,0:T(8,128)} %order.1.q0, pred[]{:T(512)S(6)} %eq.46), kind=kLoop, calls=%fused_computation.3 | loop fusion | flops 1048576 | bytes 5242881 | tf_op jit(solution)/shard_map/add | solution.py:392
  157.5 5.0 %collective-permute-done.34 = f32[264,256]{1,0:T(8,128)S(1)} collective-permute-done((f32[264,256]{1,0:T(8,128)S(1)}, f32[264,256]{1,0:T(8,128)S(1)}, u32[]{:S(2)}, u32[]{:S(2)}) %collective-permute-start.34) | collective-permute-done | bytes 270368 | tf_op jit(solution)/shard_map/ppermute | solution.py:32
  162.5 3.8 %collective-permute-done.33 = f32[264,256]{1,0:T(8,128)S(1)} collective-permute-done((f32[264,256]{1,0:T(8,128)S(1)}, f32[264,256]{1,0:T(8,128)S(1)}, u32[]{:S(2)}, u32[]{:S(2)}) %collective-permute-start.33) | collective-permute-done | bytes 270368 | tf_op jit(solution)/shard_map/ppermute | solution.py:32
  166.3 26.0 %collective-permute-start.23 = (f32[512,512]{1,0:T(8,128)}, f32[512,512]{1,0:T(8,128)}, u32[]{:S(2)}, u32[]{:S(2)}) collective-permute-start(f32[512,512]{1,0:T(8,128)} %add_add_fusion.own_ref), channel_id=1, source_target_pairs={{0,32},{1,33},{2,34},{3,35},{4,36},{5,37},{6,38},{7,39},{8,40},{9,... | collective-permute-start | bytes 3145736 | tf_op jit(solution)/shard_map/ppermute | solution.py:32
  193.2 2.1 collective-permute-done.35
  196.4 20.0 %factor.1 = (f32[256,256]{1,0:T(8,128)S(1)}, f32[256,256]{1,0:T(8,128)S(1)}, f32[256,256]{1,0:T(8,128)S(1)}, f32[256,256]{1,0:T(8,128)S(1)}, f32[256,256]{1,0:T(8,128)S(1)}) custom-call(f32[264,256]{1,0:T(8,128)S(1)} %get-tuple-element.12.packed_ref, f32[264,256]{1,0:T(8,128)S(1)} %get-tuple-element.13.a10_ref), custom_call_target="tpu_custom_call" | custom-call | flops 1000000000 | bytes 62914560 | tf_op jit(solution)/shard_map/factor/pallas_call | solution.py:161
  216.4 20.0 %update.1 = f32[8192,128]{1,0:T(8,128)} custom-call(s32[8]{0:T(128)S(1)} %fusion.1.amap_ref, s32[3]{0:T(128)S(1)} %pad_add_fusion.info_ref, f32[8192,128]{1,0:T(8,128)} %bitcast.51, f32[512,512]{1,0:T(8,128)S(1)} %copy-done, f32[512,512]{1,0:T(8,128)} %collective-permute-done.17.q1, f32[512,512]{1,0:T(8,128)S(1)} %collective-permute-done.18.q2, ...), custom_call_target="tpu_custom_call" | custom-call | flops 6000000000 | bytes 16777216 | tf_op jit(solution)/shard_map/update/pallas_call | solution.py:308
  (78 shorter events, 7.9 us)
Async XLA Ops:
  2.7 12.0 %collective-permute-start.24 = (f32[256,256]{1,0:T(8,128)S(1)}, f32[256,256]{1,0:T(8,128)S(1)}, u32[]{:S(2)}, u32[]{:S(2)}) collective-permute-start(f32[256,256]{1,0:T(8,128)S(1)} %slice_bitcast_fusion.1), channel_id=1, source_target_pairs={{33,0}} | collective-permute-start | bytes 786440 | tf_op jit(solution)/shard_map/ppermute | solution.py:32
  4.8 18.6 %collective-permute-start = (f32[2,256,256]{2,1,0:T(8,128)}, f32[2,256,256]{2,1,0:T(8,128)}, u32[]{:S(2)}, u32[]{:S(2)}) collective-permute-start(f32[2,256,256]{2,1,0:T(8,128)} %get-tuple-element.19), channel_id=1, source_target_pairs={{0,8},{1,9},{32,40},{33,41},{64,72},{65,73},{96,104},{97,105},{128... | collective-permute-start | bytes 1572872 | tf_op jit(solution)/shard_map/ppermute | solution.py:32
  9.6 15.2 %collective-permute-start.2 = (f32[2,256,256]{2,1,0:T(8,128)}, f32[2,256,256]{2,1,0:T(8,128)}, u32[]{:S(2)}, u32[]{:S(2)}) collective-permute-start(f32[2,256,256]{2,1,0:T(8,128)} %get-tuple-element.20), channel_id=1, source_target_pairs={{0,24},{1,25},{32,56},{33,57},{64,88},{65,89},{96,120},{97,121},{1... | collective-permute-start | bytes 1572872 | tf_op jit(solution)/shard_map/ppermute | solution.py:32
  12.3 18.3 %collective-permute-start.1 = (f32[2,256,256]{2,1,0:T(8,128)}, f32[2,256,256]{2,1,0:T(8,128)}, u32[]{:S(2)}, u32[]{:S(2)}) collective-permute-start(f32[2,256,256]{2,1,0:T(8,128)} %get-tuple-element.21), channel_id=1, source_target_pairs={{0,16},{1,17},{32,48},{33,49},{64,80},{65,81},{96,112},{97,113},{1... | collective-permute-start | bytes 1572872 | tf_op jit(solution)/shard_map/ppermute | solution.py:32
  17.5 17.9 %collective-permute-start.27 = (f32[264,256]{1,0:T(8,128)S(1)}, f32[264,256]{1,0:T(8,128)S(1)}, u32[]{:S(2)}, u32[]{:S(2)}) collective-permute-start(f32[264,256]{1,0:T(8,128)S(1)} %pad_select_fusion), channel_id=1, source_target_pairs={{0,192},{32,224}} | collective-permute-start | bytes 811016 | tf_op jit(solution)/shard_map/ppermute | solution.py:32
  22.1 14.6 %collective-permute-start.26 = (f32[264,256]{1,0:T(8,128)S(1)}, f32[264,256]{1,0:T(8,128)S(1)}, u32[]{:S(2)}, u32[]{:S(2)}) collective-permute-start(f32[264,256]{1,0:T(8,128)S(1)} %pad_select_fusion), channel_id=1, source_target_pairs={{0,128},{32,160}} | collective-permute-start | bytes 811016 | tf_op jit(solution)/shard_map/ppermute | solution.py:32
  23.5 14.5 %collective-permute-start.25 = (f32[264,256]{1,0:T(8,128)S(1)}, f32[264,256]{1,0:T(8,128)S(1)}, u32[]{:S(2)}, u32[]{:S(2)}) collective-permute-start(f32[264,256]{1,0:T(8,128)S(1)} %pad_select_fusion), channel_id=1, source_target_pairs={{0,64},{32,96}} | collective-permute-start | bytes 811016 | tf_op jit(solution)/shard_map/ppermute | solution.py:32
  32.2 24.6 %collective-permute-start.9 = (f32[64,256]{1,0:T(8,128)S(1)}, f32[64,256]{1,0:T(8,128)S(1)}, u32[]{:S(2)}, u32[]{:S(2)}) collective-permute-start(f32[64,256]{1,0:T(8,128)S(1)} %get-tuple-element.26), channel_id=1, source_target_pairs={{0,7},{1,0},{8,15},{9,8},{16,23},{17,16},{24,31},{25,24},{32,39},{... | collective-permute-start | bytes 196616 | tf_op jit(solution)/shard_map/ppermute | solution.py:32
  34.1 22.6 %collective-permute-start.8 = (f32[64,256]{1,0:T(8,128)S(1)}, f32[64,256]{1,0:T(8,128)S(1)}, u32[]{:S(2)}, u32[]{:S(2)}) collective-permute-start(f32[64,256]{1,0:T(8,128)S(1)} %get-tuple-element.27), channel_id=1, source_target_pairs={{0,6},{1,7},{8,14},{9,15},{16,22},{17,23},{24,30},{25,31},{32,38},... | collective-permute-start | bytes 196616 | tf_op jit(solution)/shard_map/ppermute | solution.py:32
  35.4 21.3 %collective-permute-start.7 = (f32[64,256]{1,0:T(8,128)S(1)}, f32[64,256]{1,0:T(8,128)S(1)}, u32[]{:S(2)}, u32[]{:S(2)}) collective-permute-start(f32[64,256]{1,0:T(8,128)S(1)} %get-tuple-element.28), channel_id=1, source_target_pairs={{0,5},{1,6},{8,13},{9,14},{16,21},{17,22},{24,29},{25,30},{32,37},... | collective-permute-start | bytes 196616 | tf_op jit(solution)/shard_map/ppermute | solution.py:32
  36.7 20.0 %collective-permute-start.6 = (f32[64,256]{1,0:T(8,128)S(1)}, f32[64,256]{1,0:T(8,128)S(1)}, u32[]{:S(2)}, u32[]{:S(2)}) collective-permute-start(f32[64,256]{1,0:T(8,128)S(1)} %get-tuple-element.29), channel_id=1, source_target_pairs={{0,4},{1,5},{8,12},{9,13},{16,20},{17,21},{24,28},{25,29},{32,36},... | collective-permute-start | bytes 196616 | tf_op jit(solution)/shard_map/ppermute | solution.py:32
  38.0 6.8 %collective-permute-start.3 = (f32[64,256]{1,0:T(8,128)S(1)}, f32[64,256]{1,0:T(8,128)S(1)}, u32[]{:S(2)}, u32[]{:S(2)}) collective-permute-start(f32[64,256]{1,0:T(8,128)S(1)} %get-tuple-element.32), channel_id=1, source_target_pairs={{0,1},{1,2},{8,9},{9,10},{16,17},{17,18},{24,25},{25,26},{32,33},{... | collective-permute-start | bytes 196616 | tf_op jit(solution)/shard_map/ppermute | solution.py:32
  44.8 5.5 %collective-permute-start.4 = (f32[64,256]{1,0:T(8,128)S(1)}, f32[64,256]{1,0:T(8,128)S(1)}, u32[]{:S(2)}, u32[]{:S(2)}) collective-permute-start(f32[64,256]{1,0:T(8,128)S(1)} %get-tuple-element.31), channel_id=1, source_target_pairs={{0,2},{1,3},{8,10},{9,11},{16,18},{17,19},{24,26},{25,27},{32,34},... | collective-permute-start | bytes 196616 | tf_op jit(solution)/shard_map/ppermute | solution.py:32
  50.3 5.1 %collective-permute-start.5 = (f32[64,256]{1,0:T(8,128)S(1)}, f32[64,256]{1,0:T(8,128)S(1)}, u32[]{:S(2)}, u32[]{:S(2)}) collective-permute-start(f32[64,256]{1,0:T(8,128)S(1)} %get-tuple-element.30), channel_id=1, source_target_pairs={{0,3},{1,4},{8,11},{9,12},{16,19},{17,20},{24,27},{25,28},{32,35},... | collective-permute-start | bytes 196616 | tf_op jit(solution)/shard_map/ppermute | solution.py:32
  55.4 75.9 %collective-permute-start.30 = (f32[264,256]{1,0:T(8,128)S(1)}, f32[264,256]{1,0:T(8,128)S(1)}, u32[]{:S(2)}, u32[]{:S(2)}) collective-permute-start(f32[264,256]{1,0:T(8,128)S(1)} %add_add_fusion.4), channel_id=1, source_target_pairs={{0,6},{32,38},{64,70},{96,102},{128,134},{160,166},{192,198},{224,... | collective-permute-start | bytes 811016 | tf_op jit(solution)/shard_map/ppermute | solution.py:32
  56.8 30.8 %copy-start.1 = (f32[2,64,256]{2,1,0:T(8,128)}, f32[2,64,256]{2,1,0:T(8,128)S(1)}, u32[]{:S(2)}) copy-start(f32[2,64,256]{2,1,0:T(8,128)S(1)} %pad_maximum_fusion.refs_0_) | copy-start | bytes 393220
  56.8 7.0 %collective-permute-start.16 = (f32[2,64,256]{2,1,0:T(8,128)S(1)}, f32[2,64,256]{2,1,0:T(8,128)S(1)}, u32[]{:S(2)}, u32[]{:S(2)}) collective-permute-start(f32[2,64,256]{2,1,0:T(8,128)S(1)} %pad_maximum_fusion.refs_0_), channel_id=1, source_target_pairs={{0,7},{1,0},{2,1},{3,2},{4,3},{5,4},{6,5},{7,6},{8,15},{9,8},{10,9... | collective-permute-start | bytes 393224 | tf_op jit(solution)/shard_map/ppermute | solution.py:32
  56.9 13.9 %collective-permute-start.15 = (f32[2,64,256]{2,1,0:T(8,128)S(1)}, f32[2,64,256]{2,1,0:T(8,128)S(1)}, u32[]{:S(2)}, u32[]{:S(2)}) collective-permute-start(f32[2,64,256]{2,1,0:T(8,128)S(1)} %pad_maximum_fusion.refs_0_), channel_id=1, source_target_pairs={{0,6},{1,7},{2,0},{3,1},{4,2},{5,3},{6,4},{7,5},{8,14},{9,15},{10,... | collective-permute-start | bytes 393224 | tf_op jit(solution)/shard_map/ppermute | solution.py:32
  57.0 25.6 %collective-permute-start.14 = (f32[2,64,256]{2,1,0:T(8,128)S(1)}, f32[2,64,256]{2,1,0:T(8,128)S(1)}, u32[]{:S(2)}, u32[]{:S(2)}) collective-permute-start(f32[2,64,256]{2,1,0:T(8,128)S(1)} %pad_maximum_fusion.refs_0_), channel_id=1, source_target_pairs={{0,5},{1,6},{2,7},{3,0},{4,1},{5,2},{6,3},{7,4},{8,13},{9,14},{10,... | collective-permute-start | bytes 393224 | tf_op jit(solution)/shard_map/ppermute | solution.py:32
  62.3 20.3 %collective-permute-start.13 = (f32[2,64,256]{2,1,0:T(8,128)S(1)}, f32[2,64,256]{2,1,0:T(8,128)S(1)}, u32[]{:S(2)}, u32[]{:S(2)}) collective-permute-start(f32[2,64,256]{2,1,0:T(8,128)S(1)} %pad_maximum_fusion.refs_0_), channel_id=1, source_target_pairs={{0,4},{1,5},{2,6},{3,7},{4,0},{5,1},{6,2},{7,3},{8,12},{9,13},{10,... | collective-permute-start | bytes 393224 | tf_op jit(solution)/shard_map/ppermute | solution.py:32
  63.8 23.8 %copy-start.2 = (f32[2,64,256]{2,1,0:T(8,128)}, f32[2,64,256]{2,1,0:T(8,128)S(1)}, u32[]{:S(2)}) copy-start(f32[2,64,256]{2,1,0:T(8,128)S(1)} %collective-permute-done.16.refs_7_) | copy-start | bytes 393220
  63.8 18.8 %collective-permute-start.12 = (f32[2,64,256]{2,1,0:T(8,128)S(1)}, f32[2,64,256]{2,1,0:T(8,128)S(1)}, u32[]{:S(2)}, u32[]{:S(2)}) collective-permute-start(f32[2,64,256]{2,1,0:T(8,128)S(1)} %pad_maximum_fusion.refs_0_), channel_id=1, source_target_pairs={{0,3},{1,4},{2,5},{3,6},{4,7},{5,0},{6,1},{7,2},{8,11},{9,12},{10,... | collective-permute-start | bytes 393224 | tf_op jit(solution)/shard_map/ppermute | solution.py:32
  70.8 16.9 %copy-start.3 = (f32[2,64,256]{2,1,0:T(8,128)}, f32[2,64,256]{2,1,0:T(8,128)S(1)}, u32[]{:S(2)}) copy-start(f32[2,64,256]{2,1,0:T(8,128)S(1)} %collective-permute-done.15.refs_6_) | copy-start | bytes 393220
  70.8 11.8 %collective-permute-start.11 = (f32[2,64,256]{2,1,0:T(8,128)S(1)}, f32[2,64,256]{2,1,0:T(8,128)S(1)}, u32[]{:S(2)}, u32[]{:S(2)}) collective-permute-start(f32[2,64,256]{2,1,0:T(8,128)S(1)} %pad_maximum_fusion.refs_0_), channel_id=1, source_target_pairs={{0,2},{1,3},{2,4},{3,5},{4,6},{5,7},{6,0},{7,1},{8,10},{9,11},{10,... | collective-permute-start | bytes 393224 | tf_op jit(solution)/shard_map/ppermute | solution.py:32
  82.6 5.1 %copy-start.4 = (f32[2,64,256]{2,1,0:T(8,128)}, f32[2,64,256]{2,1,0:T(8,128)S(1)}, u32[]{:S(2)}) copy-start(f32[2,64,256]{2,1,0:T(8,128)S(1)} %collective-permute-done.14.refs_5_) | copy-start | bytes 393220
  82.6 5.1 %collective-permute-start.10 = (f32[2,64,256]{2,1,0:T(8,128)S(1)}, f32[2,64,256]{2,1,0:T(8,128)S(1)}, u32[]{:S(2)}, u32[]{:S(2)}) collective-permute-start(f32[2,64,256]{2,1,0:T(8,128)S(1)} %pad_maximum_fusion.refs_0_), channel_id=1, source_target_pairs={{0,1},{1,2},{2,3},{3,4},{4,5},{5,6},{6,7},{7,0},{8,9},{9,10},{10,1... | collective-permute-start | bytes 393224 | tf_op jit(solution)/shard_map/ppermute | solution.py:32
  82.6 5.1 %copy-start.5 = (f32[2,64,256]{2,1,0:T(8,128)}, f32[2,64,256]{2,1,0:T(8,128)S(1)}, u32[]{:S(2)}) copy-start(f32[2,64,256]{2,1,0:T(8,128)S(1)} %collective-permute-done.13.refs_4_) | copy-start | bytes 393220
  82.6 5.1 %copy-start.6 = (f32[2,64,256]{2,1,0:T(8,128)}, f32[2,64,256]{2,1,0:T(8,128)S(1)}, u32[]{:S(2)}) copy-start(f32[2,64,256]{2,1,0:T(8,128)S(1)} %collective-permute-done.12.refs_3_) | copy-start | bytes 393220
  82.6 5.1 %copy-start.7 = (f32[2,64,256]{2,1,0:T(8,128)}, f32[2,64,256]{2,1,0:T(8,128)S(1)}, u32[]{:S(2)}) copy-start(f32[2,64,256]{2,1,0:T(8,128)S(1)} %collective-permute-done.11.refs_2_) | copy-start | bytes 393220
  87.7 0.7 copy-start.8
  121.3 41.2 %copy-start = (f32[512,512]{1,0:T(8,128)S(1)}, f32[512,512]{1,0:T(8,128)}, u32[]{:S(2)}) copy-start(f32[512,512]{1,0:T(8,128)} %order.1.q0) | copy-start | bytes 3145732
  121.3 26.0 %collective-permute-start.22 = (f32[512,512]{1,0:T(8,128)}, f32[512,512]{1,0:T(8,128)}, u32[]{:S(2)}, u32[]{:S(2)}) collective-permute-start(f32[512,512]{1,0:T(8,128)} %order.1.q0), channel_id=1, source_target_pairs={{0,192},{8,200},{16,208},{24,216},{33,225},{41,233},{49,241},{57,2... | collective-permute-start | bytes 3145736 | tf_op jit(solution)/shard_map/ppermute | solution.py:32
  123.1 25.5 %collective-permute-start.21 = (f32[512,512]{1,0:T(8,128)}, f32[512,512]{1,0:T(8,128)}, u32[]{:S(2)}, u32[]{:S(2)}) collective-permute-start(f32[512,512]{1,0:T(8,128)} %order.1.q0), channel_id=1, source_target_pairs={{0,128},{8,136},{16,144},{24,152},{33,161},{41,169},{49,177},{57,1... | collective-permute-start | bytes 3145736 | tf_op jit(solution)/shard_map/ppermute | solution.py:32
  124.7 28.1 %collective-permute-start.20 = (f32[512,512]{1,0:T(8,128)}, f32[512,512]{1,0:T(8,128)}, u32[]{:S(2)}, u32[]{:S(2)}) collective-permute-start(f32[512,512]{1,0:T(8,128)} %order.1.q0), channel_id=1, source_target_pairs={{0,64},{8,72},{16,80},{24,88},{33,97},{41,105},{49,113},{57,121},{... | collective-permute-start | bytes 3145736 | tf_op jit(solution)/shard_map/ppermute | solution.py:32
  126.4 8.3 %collective-permute-start.29 = (f32[264,256]{1,0:T(8,128)S(1)}, f32[264,256]{1,0:T(8,128)S(1)}, u32[]{:S(2)}, u32[]{:S(2)}) collective-permute-start(f32[264,256]{1,0:T(8,128)S(1)} %add_add_fusion.4), channel_id=1, source_target_pairs={{0,4},{32,36},{64,68},{96,100},{128,132},{160,164},{192,196},{224,... | collective-permute-start | bytes 811016 | tf_op jit(solution)/shard_map/ppermute | solution.py:32
  131.3 6.3 %collective-permute-start.28 = (f32[264,256]{1,0:T(8,128)S(1)}, f32[264,256]{1,0:T(8,128)S(1)}, u32[]{:S(2)}, u32[]{:S(2)}) collective-permute-start(f32[264,256]{1,0:T(8,128)S(1)} %add_add_fusion.4), channel_id=1, source_target_pairs={{0,2},{32,34},{64,66},{96,98},{128,130},{160,162},{192,194},{224,2... | collective-permute-start | bytes 811016 | tf_op jit(solution)/shard_map/ppermute | solution.py:32
  138.4 7.9 %collective-permute-start.31 = (f32[264,256]{1,0:T(8,128)}, f32[264,256]{1,0:T(8,128)}, u32[]{:S(2)}, u32[]{:S(2)}) collective-permute-start(f32[264,256]{1,0:T(8,128)} %add_add_fusion.3), channel_id=1, source_target_pairs={{0,1},{2,3},{4,5},{6,7},{32,33},{34,35},{36,37},{38,39},{64,65},{6... | collective-permute-start | bytes 811016 | tf_op jit(solution)/shard_map/ppermute | solution.py:32
  140.4 76.0 %collective-permute-start.19 = (f32[512,512]{1,0:T(8,128)}, f32[512,512]{1,0:T(8,128)S(1)}, u32[]{:S(2)}, u32[]{:S(2)}) collective-permute-start(f32[512,512]{1,0:T(8,128)} %order.1.q0), channel_id=1, source_target_pairs={{0,24},{1,25},{2,26},{3,27},{4,28},{5,29},{6,30},{7,31},{8,0},{9,1... | collective-permute-start | bytes 3145736 | tf_op jit(solution)/shard_map/ppermute | solution.py:32
  146.2 70.1 %collective-permute-start.18 = (f32[512,512]{1,0:T(8,128)}, f32[512,512]{1,0:T(8,128)S(1)}, u32[]{:S(2)}, u32[]{:S(2)}) collective-permute-start(f32[512,512]{1,0:T(8,128)} %order.1.q0), channel_id=1, source_target_pairs={{0,16},{1,17},{2,18},{3,19},{4,20},{5,21},{6,22},{7,23},{8,24},{9,... | collective-permute-start | bytes 3145736 | tf_op jit(solution)/shard_map/ppermute | solution.py:32
  147.3 15.2 %collective-permute-start.34 = (f32[264,256]{1,0:T(8,128)S(1)}, f32[264,256]{1,0:T(8,128)S(1)}, u32[]{:S(2)}, u32[]{:S(2)}) collective-permute-start(f32[264,256]{1,0:T(8,128)S(1)} %select_add_fusion), channel_id=1, source_target_pairs={{0,24},{1,25},{2,26},{3,27},{4,28},{5,29},{6,30},{7,31},{32,56},{3... | collective-permute-start | bytes 811016 | tf_op jit(solution)/shard_map/ppermute | solution.py:32
  148.6 17.7 %collective-permute-start.33 = (f32[264,256]{1,0:T(8,128)S(1)}, f32[264,256]{1,0:T(8,128)S(1)}, u32[]{:S(2)}, u32[]{:S(2)}) collective-permute-start(f32[264,256]{1,0:T(8,128)S(1)} %select_add_fusion), channel_id=1, source_target_pairs={{0,16},{1,17},{2,18},{3,19},{4,20},{5,21},{6,22},{7,23},{32,48},{3... | collective-permute-start | bytes 811016 | tf_op jit(solution)/shard_map/ppermute | solution.py:32
  152.8 39.5 %collective-permute-start.32 = (f32[264,256]{1,0:T(8,128)S(1)}, f32[264,256]{1,0:T(8,128)S(1)}, u32[]{:S(2)}, u32[]{:S(2)}) collective-permute-start(f32[264,256]{1,0:T(8,128)S(1)} %select_add_fusion), channel_id=1, source_target_pairs={{0,8},{1,9},{2,10},{3,11},{4,12},{5,13},{6,14},{7,15},{32,40},{33,... | collective-permute-start | bytes 811016 | tf_op jit(solution)/shard_map/ppermute | solution.py:32
  162.5 53.8 %collective-permute-start.17 = (f32[512,512]{1,0:T(8,128)S(1)}, f32[512,512]{1,0:T(8,128)}, u32[]{:S(2)}, u32[]{:S(2)}) collective-permute-start(f32[512,512]{1,0:T(8,128)S(1)} %copy-done), channel_id=1, source_target_pairs={{0,8},{1,9},{2,10},{3,11},{4,12},{5,13},{6,14},{7,15},{8,16},{9,17... | collective-permute-start | bytes 3145736 | tf_op jit(solution)/shard_map/ppermute | solution.py:32
  166.3 50.0 %collective-permute-start.23 = (f32[512,512]{1,0:T(8,128)}, f32[512,512]{1,0:T(8,128)}, u32[]{:S(2)}, u32[]{:S(2)}) collective-permute-start(f32[512,512]{1,0:T(8,128)} %add_add_fusion.own_ref), channel_id=1, source_target_pairs={{0,32},{1,33},{2,34},{3,35},{4,36},{5,37},{6,38},{7,39},{8,40},{9,... | collective-permute-start | bytes 3145736 | tf_op jit(solution)/shard_map/ppermute | solution.py:32
  193.1 2.2 collective-permute-start.35

commit v2 on v1

v2 whole, which is shorter than its diff:
```python
import jax
import jax.numpy as jnp
from jax import lax
from jax.experimental import pallas as pl
from jax.experimental.pallas import tpu as pltpu
from jax.sharding import PartitionSpec as P

F32 = jnp.float32
BF16 = jnp.bfloat16
N = 256
SLAB = 64
NY, NC, NX, NZ = 4, 2, 4, 8


def flat(y, c, x, z):
    return ((y * NC + c) * NX + x) * NZ + z


def pairs(fn):
    found = []
    for y in range(NY):
        for c in range(NC):
            for x in range(NX):
                for z in range(NZ):
                    to = fn(y, c, x, z)
                    if to is not None:
                        found.append((flat(y, c, x, z), flat(*to)))
    return found


def send(value, fn):
    return lax.ppermute(value, ("row", "col"), pairs(fn))


def sweep_slab(slab):
    left = [g[:, :128] for g in slab]
    right = [g[:, 128:] for g in slab]
    lane = lax.broadcasted_iota(jnp.int32, (8, 128), 1)
    sub = lax.broadcasted_iota(jnp.int32, (8, 128), 0)

    def splat(v):
        return jnp.broadcast_to(v, (8, 128))

    def assemble(rows):
        out = rows[0]
        for i in range(1, 8):
            out = jnp.where(sub == i, rows[i], out)
        return out

    z_left, z_right, u_left = [], [], []
    for s in range(len(slab)):
        a0, a1 = left[s], right[s]
        o = 8 * s
        cols = [splat(a0[:, o + j : o + j + 1]) for j in range(8)]
        d = [[splat(cols[j][i : i + 1, :]) for j in range(i + 1)] for i in range(8)]
        r0 = [splat(a0[i : i + 1, :]) for i in range(8)]
        r1 = [splat(a1[i : i + 1, :]) for i in range(8)]
        in_block = (lane >= o) & (lane < o + 8)
        r = []
        l = [[None] * 8 for _ in range(8)]
        zl, zr, ul = [], [], []
        for k in range(8):
            rk = lax.rsqrt(d[k][k])
            r.append(rk)
            for i in range(k + 1, 8):
                l[i][k] = d[i][k] * rk
            for j in range(k + 1, 8):
                for i in range(j, 8):
                    d[i][j] = d[i][j] - l[i][k] * l[j][k]
            x0 = jnp.where(in_block, jnp.where(lane == o + k, 1.0, 0.0).astype(F32), r0[k])
            x1 = r1[k]
            x2 = r0[k]
            for m in range(k):
                x0 = x0 - l[k][m] * zl[m]
                x1 = x1 - l[k][m] * zr[m]
                x2 = x2 - l[k][m] * ul[m]
            zl.append(x0 * rk)
            zr.append(x1 * rk)
            ul.append(x2 * rk)
        z_left.append(assemble(zl))
        z_right.append(assemble(zr))
        u_left.append(assemble(ul))
        for t in range(s + 1, len(slab)):
            coef = []
            for k in range(8):
                c = splat(left[t][:, o + k : o + k + 1])
                for m in range(k):
                    c = c - l[k][m] * coef[m]
                coef.append(c * r[k])
            x0 = jnp.where(in_block, 0.0, left[t])
            x1 = right[t]
            for k in range(8):
                x0 = x0 - coef[k] * zl[k]
                x1 = x1 - coef[k] * zr[k]
            left[t] = x0
            right[t] = x1
    return z_left, z_right, u_left


def factor_tile(m_ref, u_ref):
    row = lax.broadcasted_iota(jnp.int32, (N, N), 0)
    lan = lax.broadcasted_iota(jnp.int32, (N, N), 1)
    row_s = lax.broadcasted_iota(jnp.int32, (SLAB, N), 0)
    lan_s = lax.broadcasted_iota(jnp.int32, (SLAB, N), 1)

    @pl.loop(0, N // SLAB)
    def _(b):
        o = b * SLAB
        rows = pl.ds(pl.multiple_of(o, SLAB), SLAB)
        slab = pltpu.roll(m_ref[rows, :], N - o, 1)
        zl, zr, ul = sweep_slab([slab[8 * g : 8 * g + 8, :] for g in range(SLAB // 8)])
        zr = jnp.concatenate(zr, 0)
        z = jnp.concatenate([jnp.concatenate(zl, 0), zr], 1)
        u = jnp.concatenate([jnp.concatenate(ul, 0), zr], 1)
        z = jnp.where((lan_s < SLAB) & (lan_s > row_s), 0.0, z)
        z = pltpu.roll(z, o, 1)
        u = pltpu.roll(u, o, 1)
        u_ref[rows, :] = u

        @pl.when(b < N // SLAB - 1)
        def _():
            coef = jnp.where(lan_s >= o + SLAB, u, 0.0)
            update = lax.dot_general(
                coef, z, (((0,), (0,)), ((), ())), precision=lax.Precision.HIGHEST, preferred_element_type=F32
            )
            m = m_ref[...]
            m = jnp.where((row >= o + SLAB) & (lan >= o) & (lan < o + SLAB), 0.0, m)
            m_ref[...] = m - update

        m_ref[rows, :] = z


def dot_nt(a, b):
    return lax.dot_general(a, b, (((1,), (1,)), ((), ())), precision=lax.Precision.HIGHEST, preferred_element_type=F32)


def read_out(l_ref, w_ref, m_ref, u_ref):
    row = lax.broadcasted_iota(jnp.int32, (N, N), 0)
    lan = lax.broadcasted_iota(jnp.int32, (N, N), 1)
    l_ref[...] = jnp.where(row >= lan, u_ref[...].T, 0.0)
    w_ref[...] = jnp.where(row >= lan, m_ref[...], 0.0)


def factor_kernel(core_ref, own_ref, other_ref, l0_ref, w0_ref, p10_ref, l1_ref, w1_ref, m_ref, u_ref):
    row = lax.broadcasted_iota(jnp.int32, (N, N), 0)
    lan = lax.broadcasted_iota(jnp.int32, (N, N), 1)

    def half(core, lo, hi):
        return jnp.where(core_ref[0] == core, own_ref[:, lo:hi, :], other_ref[:, lo:hi, :])

    def mirrored(core):
        t = half(core, 0, 8).reshape(N, N)
        return jnp.where(row >= lan, t, t.T)

    m_ref[...] = mirrored(0)
    factor_tile(m_ref, u_ref)
    read_out(l0_ref, w0_ref, m_ref, u_ref)
    a10 = jnp.concatenate([half(0, 8, 12), half(1, 8, 12)], 1).reshape(N, N)
    p10 = dot_nt(a10, w0_ref[...])
    p10_ref[...] = p10
    m_ref[...] = mirrored(1) - dot_nt(p10, p10)
    factor_tile(m_ref, u_ref)
    read_out(l1_ref, w1_ref, m_ref, u_ref)


def factor(core, own, other):
    vmem = pl.BlockSpec(memory_space=pltpu.VMEM)
    return pl.pallas_call(
        factor_kernel,
        out_shape=[jax.ShapeDtypeStruct((N, N), F32)] * 5,
        in_specs=[pl.BlockSpec(memory_space=pltpu.SMEM), vmem, vmem],
        out_specs=[vmem] * 5,
        scratch_shapes=[pltpu.VMEM((N, N), F32)] * 2,
        compiler_params=pltpu.CompilerParams(vmem_limit_bytes=24 << 20),
        cost_estimate=pl.CostEstimate(flops=10**9, bytes_accessed=60 << 20, transcendentals=0),
        name="factor",
    )(core, own, other)


def column_kernel(m_ref, o_ref):
    for half in range(2):
        o_ref[0, 0, :, half * 128 : half * 128 + 128] = m_ref[pl.ds(half, N, stride=4), :]


def first_column(flat_blocks):
    return pl.pallas_call(
        column_kernel,
        grid=(8,),
        out_shape=jax.ShapeDtypeStruct((4, 2, N, N), F32),
        in_specs=[pl.BlockSpec((4 * N, 128), lambda a: (a, 0))],
        out_specs=pl.BlockSpec((1, 1, N, N), lambda a: (a % 4, a // 4, 0, 0)),
        compiler_params=pltpu.CompilerParams(vmem_limit_bytes=16 << 20, dimension_semantics=("arbitrary",)),
        cost_estimate=pl.CostEstimate(flops=0, bytes_accessed=6 << 20, transcendentals=0),
        name="first_column",
    )(flat_blocks)


def split(v):
    hi = v.astype(BF16)
    return hi, (v - hi.astype(F32)).astype(BF16)


def dot_nn(a, b):
    return jnp.dot(a, b, precision=lax.Precision.HIGHEST, preferred_element_type=F32)


def rows_kernel(info_ref, w0_ref, p10_ref, w1_ref, a0, a1, a2, a3, b0, b1, b2, b3, o_ref):
    t = pl.program_id(0)
    odd = info_ref[3]
    for d, (mine, others) in enumerate(((a0, b0), (a1, b1), (a2, b2), (a3, b3))):
        @pl.when(t == d)
        def _(mine=mine, others=others):
            even = odd == 0
            x0 = jnp.where(even, mine[...], others[...])
            x1 = jnp.where(even, others[...], mine[...])
            first = dot_nt(x0, w0_ref[...])
            o_ref[0, :, :N] = first
            o_ref[0, :, N:] = dot_nt(x1 - dot_nt(first, p10_ref[...]), w1_ref[...])


def solve_rows(info, w0, p10, w1, own_quarters, other_quarters):
    whole = lambda *shape: pl.BlockSpec(shape, lambda t: (0,) * len(shape))
    return pl.pallas_call(
        rows_kernel,
        grid=(4,),
        in_specs=[pl.BlockSpec(memory_space=pltpu.SMEM)] + [whole(N, N)] * 3 + [whole(2 * N, N)] * 8,
        out_specs=pl.BlockSpec((1, 2 * N, 2 * N), lambda t: (t, 0, 0)),
        out_shape=jax.ShapeDtypeStruct((4, 2 * N, 2 * N), F32),
        compiler_params=pltpu.CompilerParams(vmem_limit_bytes=60 << 20, dimension_semantics=("arbitrary",)),
        cost_estimate=pl.CostEstimate(flops=5 * 10**9, bytes_accessed=9 << 20, transcendentals=0),
        name="solve_rows",
    )(info, w0, p10, w1, *own_quarters, *other_quarters)


def update_kernel(
    info_ref, m_ref, p_ref, own_ref, other_ref, l0_ref, w0_ref, p10_ref, l1_ref, w1_ref, o_ref, x_s, chi, clo
):
    t = pl.program_id(0)
    p, q, keep_own, x = info_ref[0], info_ref[1], info_ref[2], info_ref[4]
    i = 8 * lax.rem(x - t + 4, 4) + p

    @pl.when(t == 0)
    def _():
        for value, kept in ((own_ref, 1), (other_ref, 0)):
            @pl.when(keep_own == kept)
            def _(value=value):
                x_s[...] = value[...]

        first = dot_nt(w0_ref[...], x_s[0])
        second = dot_nn(w1_ref[...], x_s[1].T - dot_nn(p10_ref[...], first))
        for k, panel in enumerate((first, second)):
            hi, lo = split(panel)
            chi[k * N : k * N + N, :] = hi
            clo[k * N : k * N + N, :] = lo

    def put(h, b, value):
        for half in range(2):
            o_ref[h, pl.ds(2 * b + half, N, stride=4), :] = value[:, half * 128 : half * 128 + 128]

    def get(h, b):
        return jnp.concatenate([m_ref[h, pl.ds(2 * b + half, N, stride=4), :] for half in range(2)], 1)

    def change(h, b):
        hi, lo = split(p_ref[0, h * N : h * N + N, :])
        cols = slice(b * N, b * N + N)

        def dot16(u, v):
            return jnp.dot(u, v, preferred_element_type=F32)

        product = dot16(lo, chi[:, cols]) + dot16(hi, clo[:, cols]) + dot16(hi, chi[:, cols])
        put(h, b, get(h, b) - product)

    @pl.when(q > 1)
    def _():
        change(1, 0)

    @pl.when((q > 1) & (i >= q))
    def _():
        change(0, 0)

    @pl.when((q > 1) & (i < q) | (q == 1) & (i < 1))
    def _():
        put(0, 0, get(0, 0))

    @pl.when(i >= q)
    def _():
        change(1, 1)

    @pl.when(i < q)
    def _():
        put(1, 1, get(1, 1))

    put(0, 1, get(0, 1))

    for k, l_ref in enumerate((l0_ref, l1_ref)):
        cols = slice(k * N, k * N + N)

        @pl.when(q == k)
        def _(cols=cols):
            put(1, 0, p_ref[0, N:, cols])

        @pl.when((q == k) & (i > k))
        def _(cols=cols):
            put(0, 0, p_ref[0, :N, cols])

        @pl.when((q == k) & (i == k))
        def _(l_ref=l_ref):
            put(0, 0, l_ref[...])


def update(info, flat_blocks, rows, own, other, l0, w0, p10, l1, w1):
    whole = lambda *shape: pl.BlockSpec(shape, lambda t, info: (0,) * len(shape))
    tiles = pl.BlockSpec((2, 4 * N, 128), lambda t, info: (0, lax.rem(info[4] - t + 4, 4), 0))
    return pl.pallas_call(
        update_kernel,
        grid_spec=pltpu.PrefetchScalarGridSpec(
            num_scalar_prefetch=1,
            grid=(4,),
            in_specs=[tiles, pl.BlockSpec((1, 2 * N, 2 * N), lambda t, info: (t, 0, 0))]
            + [whole(2, 2 * N, N)] * 2
            + [whole(N, N)] * 5,
            out_specs=tiles,
            scratch_shapes=[pltpu.VMEM((2, 2 * N, N), F32)] + [pltpu.VMEM((2 * N, 2 * N), BF16)] * 2,
        ),
        out_shape=jax.ShapeDtypeStruct(flat_blocks.shape, F32),
        compiler_params=pltpu.CompilerParams(vmem_limit_bytes=40 << 20, dimension_semantics=("arbitrary",)),
        cost_estimate=pl.CostEstimate(flops=5 * 10**9, bytes_accessed=16 << 20, transcendentals=0),
        name="update",
    )(info, flat_blocks, rows, own, other, l0, w0, p10, l1, w1)


def after(value, *others):
    return lax.optimization_barrier((value, *others))[0]


def pick(index, options):
    out = options[0]
    for k in range(1, len(options)):
        out = jnp.where(index == k, options[k], out)
    return out


def on_device(matrix):
    row_index = lax.axis_index("row")
    col_index = lax.axis_index("col")
    y, core = row_index // NC, row_index % NC
    x, z = col_index // NZ, col_index % NZ
    flat_blocks = matrix.reshape(8 * N * 4, 128)
    column = first_column(flat_blocks)

    arrived = [
        send(column[d], lambda y, c, x, z, d=d: (y, c, (x + d) % NX, z) if z < 2 else None) for d in (1, 2, 3)
    ]

    own_rows = lax.all_to_all(column[0, 0].reshape(32, 8, N), "col", 0, 0, tiled=True)[:2]

    quarter = after(pick(x, [column[0], *arrived]), own_rows)

    parts = quarter.reshape(4, 128, N)
    sent = [
        send(
            lax.dynamic_index_in_dim(parts, (z // 2 + d) % 4, 0, keepdims=False),
            lambda y, c, x, z, d=d: (y, c, x, (z + 2 * d) % NZ) if z < 2 else None,
        )
        for d in (1, 2, 3)
    ]
    piece = pick(z // 2, [parts[0], *sent])
    tile_rows = lax.all_to_all(jnp.broadcast_to(own_rows[None], (8, 2, 8, N)), "row", 0, 0, tiled=True)
    lead, middle, last = tile_rows[0, 0], tile_rows[1, 0], tile_rows[1, 1]
    core_rows = jnp.where(
        core == 0, jnp.concatenate([lead, middle[:4]], 0), jnp.concatenate([last, middle[4:]], 0)
    )
    pieces = [piece] + [send(piece, lambda y, c, x, z, d=d: (y, c, x, (z + 2 * d) % NZ)) for d in (1, 2, 3)]
    ordered = jnp.stack([pieces[0], pieces[3], pieces[2], pieces[1]] * 2)
    mine = lax.dynamic_slice_in_dim(ordered, (4 - z // 2) % 4, 4, 0).reshape(2 * N, N)
    piece, core_rows = lax.optimization_barrier((piece, core_rows))
    core_rows = lax.all_to_all(jnp.broadcast_to(core_rows[None], (32, 12, N)), "col", 0, 0, tiled=True)
    other_rows = send(core_rows, lambda y, c, x, z: (y, 1 - c, x, z))
    mine = after(mine, other_rows)

    own_quarters = [mine] + [send(mine, lambda y, c, x, z, d=d: (y, c, (x + d) % NX, z)) for d in (1, 2, 3)]
    others = send(mine, lambda y, c, x, z: (y, c, x, z ^ 1))
    turn = (y - z // 2 + NY) % NY
    two = send(mine, lambda y, c, x, z: ((y + 2) % NY, c, x, z))
    half = jnp.where(turn >= 2, two, mine)
    others, half, core_rows, *_ = lax.optimization_barrier((others, half, core_rows, *own_quarters))

    other_quarters = [others] + [send(others, lambda y, c, x, z, d=d: (y, c, (x + d) % NX, z)) for d in (1, 2, 3)]
    one = send(half, lambda y, c, x, z: ((y + 1) % NY, c, x, z))
    l0, w0, p10, l1, w1 = factor(core.astype(jnp.int32)[None], core_rows, other_rows)
    half = after(jnp.where(turn % 2 == 1, one, half), l1, *other_quarters)
    next_half = send(half, lambda y, c, x, z: (y, c, x, z ^ 1))
    info = jnp.stack([row_index, col_index, core == z % 2, z % 2, x]).astype(jnp.int32)
    rows = solve_rows(info, w0, p10, w1, own_quarters, other_quarters)
    next_half, rows = lax.optimization_barrier((next_half, rows))
    panel = jnp.stack([jnp.where(z % 2 == 0, half, next_half), jnp.where(z % 2 == 0, next_half, half)])
    other_panel = send(panel, lambda y, c, x, z: (y, 1 - c, x, z))

    out = update(info, flat_blocks.reshape(2, 4 * N * 4, 128), rows, panel, other_panel, l0, w0, p10, l1, w1)
    return out.reshape(matrix.shape)


def solution(mesh):
    return jax.shard_map(
        on_device,
        mesh=mesh,
        in_specs=(P(None, "row", None, None, "col", None),),
        out_specs=P(None, "row", None, None, "col", None),
        check_vma=False,
    )
```

time: 240 us -> 179 us (0.75); the launches traced: 236 us -> 179 us
  starting transfers between devices: 93.3 us -> 57.7 us
  Pallas kernels: 72.9 us -> 39.2 us
  waiting for transfers between devices: 52.9 us -> 64.1 us
  local copies, waits for them, and re-layouts: 7.68 us -> 16.2 us
  other arithmetic: 8.91 us -> 1.12 us
    ppermute x36 -> x21, starting transfers between devices: 93.3 us -> 38.6 us  [send(): return lax.ppermute(value, ('row', 'col'), pairs(fn))]
    all_to_all x0 -> x3, waiting for transfers between devices: none -> 27.3 us  [the longest x1 16.8 us: on_device(): lax.all_to_all(column[0, 0].reshape(32, 8, N), 'col', 0, 0, tiled=True)[:2]]
    pallas_call x1 -> x2, Pallas kernels: 33 us -> 13 us  [the longest x1 12.7 us: solve_rows(): pl.pallas_call(rows_kernel, grid=(4,), in_specs=[pl.BlockSpec(memory_spac...]
    all_to_all x0 -> x3, starting transfers between devices: none -> 19.1 us  [the longest x1 8.77 us: on_device(): lax.all_to_all(jnp.broadcast_to(core_rows[None], (32, 12, N)), 'col', 0,...]
    ppermute x36 -> x21, waiting for transfers between devices: 52.9 us -> 36.8 us  [send(): return lax.ppermute(value, ('row', 'col'), pairs(fn))]
    pallas_call x1, Pallas kernels: 20 us -> 6.21 us  [update(): pl.pallas_call(update_kernel, grid_spec=pltpu.PrefetchScalarGridSpec(num_...]
    add x8 -> x0, other arithmetic: 7.67 us -> none  [the longest x1 3.34 us: on_device(): jnp.where(row_index == z, mine, 0.0) + chosen[0] + chosen[1] + chosen[2]]
    unnamed x25 -> x30, local copies, waits for them, and re-layouts: 3.35 us -> 10.5 us
  transfers between devices with their start and end apart: 36 -> 24, of which waited for: 14 -> 12; matrix products, arithmetic and copies ran while one was open for 6% -> 5% of each run, Pallas kernels for 22% -> 18%
where the time goes in v2:
time: 179 us
  waiting for transfers between devices  64.1 us (36%)
  starting transfers between devices  57.7 us (32%)
  Pallas kernels  39.2 us (22%)
  local copies, waits for them, and re-layouts  16.2 us (9%)
    ppermute x21, starting transfers between devices, send(): return lax.ppermute(value, ('row', 'col'), pairs(fn))  38.6 us
    ppermute x21, waiting for transfers between devices, send(): return lax.ppermute(value, ('row', 'col'), pairs(fn))  36.8 us
    pallas_call x1, Pallas kernels, factor(): pl.pallas_call(factor_kernel, out_shape=[jax.ShapeDtypeStruct((N, N), F32...  20 us
    all_to_all x1, waiting for transfers between devices, on_device(): lax.all_to_all(column[0, 0].reshape(32, 8, N), 'col', 0, 0, tiled=True)[:2]  16.8 us
    pallas_call x1, Pallas kernels, solve_rows(): pl.pallas_call(rows_kernel, grid=(4,), in_specs=[pl.BlockSpec(memory_spac...  12.7 us
    unnamed x30, local copies, waits for them, and re-layouts  10.5 us
    all_to_all x1, waiting for transfers between devices, on_device(): lax.all_to_all(jnp.broadcast_to(core_rows[None], (32, 12, N)), 'col', 0,...  9.36 us
    all_to_all x1, starting transfers between devices, on_device(): lax.all_to_all(jnp.broadcast_to(core_rows[None], (32, 12, N)), 'col', 0,...  8.77 us
  transfers between devices with their start and end apart: 24, of which 12 were waited for; matrix products, arithmetic and copies ran while one was open for 5% of the time, Pallas kernels for 18%

profile of v2, /device:TPU:1, one launch (start us, length us, event | category | flops | bytes accessed | tf_op | source)
XLA Modules:
  0.0 178.7 jit_solution(17822896851210494302)
XLA Ops:
  0.0 2.2 %copy-done = f32[8,1,256,2,1,256]{5,4,3,2,1,0:T(1,128)S(1)} copy-done((f32[8,1,256,2,1,256]{5,4,3,2,1,0:T(1,128)S(1)}, f32[8,1,256,2,1,256]{5,4,3,2,1,0:T(1,128)}, u32[]{:S(2)}) %copy-start) | copy-done | bytes 4194328
  2.5 1.1 slice_bitcast_fusion.1
  3.6 3.9 %collective-permute-start.2 = (f32[2,256,256]{2,1,0:T(8,128)}, f32[2,256,256]{2,1,0:T(8,128)S(1)}, u32[]{:S(2)}, u32[]{:S(2)}) collective-permute-start(f32[2,256,256]{2,1,0:T(8,128)} %get-tuple-element.35), channel_id=1, source_target_pairs={{0,8},{1,9},{8,16},{9,17},{16,24},{17,25},{24,0},{25,1},{32,40},{3... | collective-permute-start | bytes 1572872 | tf_op jit(solution)/shard_map/ppermute | solution.py:32
  7.5 4.4 %collective-permute-start.1 = (f32[2,256,256]{2,1,0:T(8,128)}, f32[2,256,256]{2,1,0:T(8,128)}, u32[]{:S(2)}, u32[]{:S(2)}) collective-permute-start(f32[2,256,256]{2,1,0:T(8,128)} %get-tuple-element.36), channel_id=1, source_target_pairs={{0,16},{1,17},{8,24},{9,25},{16,0},{17,1},{24,8},{25,9},{32,48},{3... | collective-permute-start | bytes 1572872 | tf_op jit(solution)/shard_map/ppermute | solution.py:32
  11.9 3.1 %collective-permute-start = (f32[2,256,256]{2,1,0:T(8,128)S(1)}, f32[2,256,256]{2,1,0:T(8,128)}, u32[]{:S(2)}, u32[]{:S(2)}) collective-permute-start(f32[2,256,256]{2,1,0:T(8,128)S(1)} %get-tuple-element.37), channel_id=1, source_target_pairs={{0,24},{1,25},{8,0},{9,1},{16,8},{17,9},{24,16},{25,17},{32,56},{3... | collective-permute-start | bytes 1572872 | tf_op jit(solution)/shard_map/ppermute | solution.py:32
  15.0 0.7 slice_bitcast_fusion.4
  15.7 4.1 %all-to-all-start = ((f32[32,8,256]{2,1,0:T(8,128)}), f32[32,8,256]{2,1,0:T(8,128)S(1)}, u32[]{:S(2)}, u32[]{:S(2)}) async-start(f32[32,8,256]{2,1,0:T(8,128)} %slice_bitcast_fusion.4), calls=%async_computation | async-start | bytes 524288 | tf_op jit(solution)/shard_map/all_to_all | solution.py:355
  20.0 16.8 %all-to-all-done = f32[32,8,256]{2,1,0:T(8,128)S(1)} async-done(((f32[32,8,256]{2,1,0:T(8,128)}), f32[32,8,256]{2,1,0:T(8,128)S(1)}, u32[]{:S(2)}, u32[]{:S(2)}) %all-to-all-start) | async-done | bytes 262176 | tf_op jit(solution)/shard_map/all_to_all | solution.py:355
  37.5 6.2 %all-to-all-start.1 = ((f32[8,2,8,256]{3,2,1,0:T(8,128)}), f32[8,2,8,256]{3,2,1,0:T(8,128)S(1)}, u32[]{:S(2)}, u32[]{:S(2)}) async-start(f32[8,2,8,256]{3,2,1,0:T(8,128)} %broadcast_in_dim.6), calls=%async_computation.1 | async-start | bytes 262144 | tf_op jit(solution)/shard_map/all_to_all | solution.py:368
  43.9 1.3 collective-permute-start.5
  45.2 1.3 collective-permute-start.4
  46.5 1.3 collective-permute-start.3
  47.8 1.1 all-to-all-done.1
  49.0 2.2 %collective-permute-done.4 = f32[128,256]{1,0:T(8,128)S(1)} collective-permute-done((f32[128,256]{1,0:T(8,128)S(1)}, f32[128,256]{1,0:T(8,128)S(1)}, u32[]{:S(2)}, u32[]{:S(2)}) %collective-permute-start.4) | collective-permute-done | bytes 131104 | tf_op jit(solution)/shard_map/ppermute | solution.py:32
  51.2 5.4 %collective-permute-done.3 = f32[128,256]{1,0:T(8,128)S(1)} collective-permute-done((f32[128,256]{1,0:T(8,128)S(1)}, f32[128,256]{1,0:T(8,128)S(1)}, u32[]{:S(2)}, u32[]{:S(2)}) %collective-permute-start.3) | collective-permute-done | bytes 131104 | tf_op jit(solution)/shard_map/ppermute | solution.py:32
  56.6 0.7 bitcast_dynamic-update-slice_fusion.6
  57.2 4.3 %collective-permute-start.6 = (f32[128,256]{1,0:T(8,128)S(1)}, f32[128,256]{1,0:T(8,128)S(1)}, u32[]{:S(2)}, u32[]{:S(2)}) collective-permute-start(f32[128,256]{1,0:T(8,128)S(1)} %get-tuple-element.34), channel_id=1, source_target_pairs={{0,6},{1,7},{2,0},{3,1},{4,2},{5,3},{6,4},{7,5},{8,14},{9,15},{10,... | collective-permute-start | bytes 393224 | tf_op jit(solution)/shard_map/ppermute | solution.py:32
  61.7 2.1 %collective-permute-start.7 = (f32[128,256]{1,0:T(8,128)S(1)}, f32[128,256]{1,0:T(8,128)S(1)}, u32[]{:S(2)}, u32[]{:S(2)}) collective-permute-start(f32[128,256]{1,0:T(8,128)S(1)} %get-tuple-element.34), channel_id=1, source_target_pairs={{0,4},{1,5},{2,6},{3,7},{4,0},{5,1},{6,2},{7,3},{8,12},{9,13},{10,... | collective-permute-start | bytes 393224 | tf_op jit(solution)/shard_map/ppermute | solution.py:32
  63.7 0.8 broadcast_in_dim.7
  64.6 8.8 %all-to-all-start.2 = ((f32[32,12,256]{2,1,0:T(8,128)}), f32[32,12,256]{2,1,0:T(8,128)S(1)}, u32[]{:S(2)}, u32[]{:S(2)}) async-start(f32[32,12,256]{2,1,0:T(8,128)} %broadcast_in_dim.7), calls=%async_computation.2 | async-start | bytes 1048576 | tf_op jit(solution)/shard_map/all_to_all | solution.py:377
  73.4 0.7 bitcast_dynamic-update-slice_fusion.4
  74.6 0.7 bitcast_dynamic-update-slice_fusion.2
  75.3 0.7 bitcast_dynamic-update-slice_fusion
  76.6 0.7 bitcast_dynamic-update-slice_fusion.5
  77.3 9.4 %all-to-all-done.2.own_ref = f32[32,12,256]{2,1,0:T(8,128)S(1)} async-done(((f32[32,12,256]{2,1,0:T(8,128)}), f32[32,12,256]{2,1,0:T(8,128)S(1)}, u32[]{:S(2)}, u32[]{:S(2)}) %all-to-all-start.2) | async-done | bytes 393248 | tf_op jit(solution)/shard_map/all_to_all | solution.py:377
  86.6 5.1 %collective-permute-start.9 = (f32[32,12,256]{2,1,0:T(8,128)S(1)}, f32[32,12,256]{2,1,0:T(8,128)S(1)}, u32[]{:S(2)}, u32[]{:S(2)}) collective-permute-start(f32[32,12,256]{2,1,0:T(8,128)S(1)} %all-to-all-done.2.own_ref), channel_id=1, source_target_pairs={{0,32},{1,33},{2,34},{3,35},{4,36},{5,37},{6,38},{7,39},{8,40},{9,... | collective-permute-start | bytes 1179656 | tf_op jit(solution)/shard_map/ppermute | solution.py:32
  92.4 0.7 bitcast_dynamic-update-slice_fusion.1
  93.1 1.1 constant_dynamic-slice_fusion
  94.2 2.9 %collective-permute-start.11 = (f32[512,256]{1,0:T(8,128)S(1)}, f32[512,256]{1,0:T(8,128)S(1)}, u32[]{:S(2)}, u32[]{:S(2)}) collective-permute-start(f32[512,256]{1,0:T(8,128)S(1)} %bitcast.68), channel_id=1, source_target_pairs={{0,128},{1,129},{2,130},{3,131},{4,132},{5,133},{6,134},{7,135},{8... | collective-permute-start | bytes 1572872 | tf_op jit(solution)/shard_map/ppermute | solution.py:32
  97.7 0.9 collective-permute-start.13
  98.8 2.2 %collective-permute-start.10 = (f32[512,256]{1,0:T(8,128)S(1)}, f32[512,256]{1,0:T(8,128)}, u32[]{:S(2)}, u32[]{:S(2)}) collective-permute-start(f32[512,256]{1,0:T(8,128)S(1)} %bitcast.72), channel_id=1, source_target_pairs={{0,1},{1,0},{2,3},{3,2},{4,5},{5,4},{6,7},{7,6},{8,9},{9,8},{10,11... | collective-permute-start | bytes 1572872 | tf_op jit(solution)/shard_map/ppermute | solution.py:32
  100.9 8.5 %collective-permute-done.11 = f32[512,256]{1,0:T(8,128)S(1)} collective-permute-done((f32[512,256]{1,0:T(8,128)S(1)}, f32[512,256]{1,0:T(8,128)S(1)}, u32[]{:S(2)}, u32[]{:S(2)}) %collective-permute-start.11) | collective-permute-done | bytes 524320 | tf_op jit(solution)/shard_map/ppermute | solution.py:32
  109.5 0.9 collective-permute-done.14.a3
  110.4 1.9 %collective-permute-done.13.a2 = f32[512,256]{1,0:T(8,128)} collective-permute-done((f32[512,256]{1,0:T(8,128)S(1)}, f32[512,256]{1,0:T(8,128)}, u32[]{:S(2)}, u32[]{:S(2)}) %collective-permute-start.13) | collective-permute-done | bytes 524320 | tf_op jit(solution)/shard_map/ppermute | solution.py:32
  112.2 12.1 %collective-permute-done.12.a1 = f32[512,256]{1,0:T(8,128)} collective-permute-done((f32[512,256]{1,0:T(8,128)S(1)}, f32[512,256]{1,0:T(8,128)}, u32[]{:S(2)}, u32[]{:S(2)}) %collective-permute-start.12) | collective-permute-done | bytes 524320 | tf_op jit(solution)/shard_map/ppermute | solution.py:32
  124.6 0.9 collective-permute-start.17
  125.5 0.9 collective-permute-start.16
  126.4 20.0 %factor.1 = (f32[256,256]{1,0:T(8,128)S(1)}, f32[256,256]{1,0:T(8,128)S(1)}, f32[256,256]{1,0:T(8,128)S(1)}, f32[256,256]{1,0:T(8,128)S(1)}, f32[256,256]{1,0:T(8,128)S(1)}) custom-call(s32[1]{0:T(128)} %bitcast.26.core_ref, f32[32,12,256]{2,1,0:T(8,128)S(1)} %all-to-all-done.2.own_ref, f32[32,12,256]{2,1,0:T(8,128)S(1)} %collective-permute-done.9.other_ref), custom_call_target="tpu_custom_call" | custom-call | flops 1000000000 | bytes 62914560 | tf_op jit(solution)/shard_map/factor/pallas_call | solution.py:168
  146.4 0.7 copy-done.4
  147.1 0.7 copy-done.6
  147.8 0.7 copy-done.8
  148.6 3.0 %collective-permute-done.16.b1 = f32[512,256]{1,0:T(8,128)} collective-permute-done((f32[512,256]{1,0:T(8,128)}, f32[512,256]{1,0:T(8,128)}, u32[]{:S(2)}, u32[]{:S(2)}) %collective-permute-start.16) | collective-permute-done | bytes 524320 | tf_op jit(solution)/shard_map/ppermute | solution.py:32
  151.5 2.1 %collective-permute-start.19 = (f32[512,256]{1,0:T(8,128)S(1)}, f32[512,256]{1,0:T(8,128)S(1)}, u32[]{:S(2)}, u32[]{:S(2)}) collective-permute-start(f32[512,256]{1,0:T(8,128)S(1)} %broadcast_select_fusion.1), channel_id=1, source_target_pairs={{0,1},{1,0},{2,3},{3,2},{4,5},{5,4},{6,7},{7,6},{8,9},{9,8},{10,11... | collective-permute-start | bytes 1572872 | tf_op jit(solution)/shard_map/ppermute | solution.py:32
  154.2 12.7 %solve_rows.1.p_ref = f32[4,512,512]{2,1,0:T(8,128)} custom-call(s32[5]{0:T(128)} %stack.55.info_ref, f32[256,256]{1,0:T(8,128)} %copy-done.4, f32[256,256]{1,0:T(8,128)} %copy-done.6, f32[256,256]{1,0:T(8,128)} %copy-done.8, f32[512,256]{1,0:T(8,128)} %bitcast.74, f32[512,256]{1,0:T(8,128)} %collective-permute-done.12.a1, ...), custom_call_target="tpu_custom_call" | custom-call | flops 5000000000 | bytes 9437184 | tf_op jit(solution)/shard_map/solve_rows/pallas_call | solution.py:223
  167.1 0.9 collective-permute-start.20
  168.0 2.3 %collective-permute-done.20.other_ref = f32[2,512,256]{2,1,0:T(8,128)S(1)} collective-permute-done((f32[2,512,256]{2,1,0:T(8,128)S(1)}, f32[2,512,256]{2,1,0:T(8,128)S(1)}, u32[]{:S(2)}, u32[]{:S(2)}) %collective-permute-start.20) | collective-permute-done | bytes 1048608 | tf_op jit(solution)/shard_map/ppermute | solution.py:32
  170.3 2.2 %copy-done.3 = f32[4,512,512]{2,1,0:T(8,128)S(1)} copy-done((f32[4,512,512]{2,1,0:T(8,128)S(1)}, f32[4,512,512]{2,1,0:T(8,128)}, u32[]{:S(2)}) %copy-start.3) | copy-done | bytes 4194328
  172.5 6.2 %update.1 = f32[2,4096,128]{2,1,0:T(8,128)} custom-call(s32[5]{0:T(128)S(1)} %copy-done.2, f32[2,4096,128]{2,1,0:T(8,128)S(1)} %bitcast.67, f32[4,512,512]{2,1,0:T(8,128)S(1)} %copy-done.3, f32[2,512,256]{2,1,0:T(8,128)S(1)} %pad_maximum_fusion.own_ref, f32[2,512,256]{2,1,0:T(8,128)S(1)} %collective-permute-done.20.other_ref, ...), custom_call_target="tpu_custom_call" | custom-call | flops 5000000000 | bytes 16777216 | tf_op jit(solution)/shard_map/update/pallas_call | solution.py:314
  (52 shorter events, 5.2 us)
Async XLA Ops:
  0.0 2.2 %copy-start = (f32[8,1,256,2,1,256]{5,4,3,2,1,0:T(1,128)S(1)}, f32[8,1,256,2,1,256]{5,4,3,2,1,0:T(1,128)}, u32[]{:S(2)}) copy-start(f32[8,1,256,2,1,256]{5,4,3,2,1,0:T(1,128)} %param.1) | copy-start | bytes 12582916
  3.6 40.1 %collective-permute-start.2 = (f32[2,256,256]{2,1,0:T(8,128)}, f32[2,256,256]{2,1,0:T(8,128)S(1)}, u32[]{:S(2)}, u32[]{:S(2)}) collective-permute-start(f32[2,256,256]{2,1,0:T(8,128)} %get-tuple-element.35), channel_id=1, source_target_pairs={{0,8},{1,9},{8,16},{9,17},{16,24},{17,25},{24,0},{25,1},{32,40},{3... | collective-permute-start | bytes 1572872 | tf_op jit(solution)/shard_map/ppermute | solution.py:32
  7.5 36.2 %collective-permute-start.1 = (f32[2,256,256]{2,1,0:T(8,128)}, f32[2,256,256]{2,1,0:T(8,128)}, u32[]{:S(2)}, u32[]{:S(2)}) collective-permute-start(f32[2,256,256]{2,1,0:T(8,128)} %get-tuple-element.36), channel_id=1, source_target_pairs={{0,16},{1,17},{8,24},{9,25},{16,0},{17,1},{24,8},{25,9},{32,48},{3... | collective-permute-start | bytes 1572872 | tf_op jit(solution)/shard_map/ppermute | solution.py:32
  11.9 31.8 %collective-permute-start = (f32[2,256,256]{2,1,0:T(8,128)S(1)}, f32[2,256,256]{2,1,0:T(8,128)}, u32[]{:S(2)}, u32[]{:S(2)}) collective-permute-start(f32[2,256,256]{2,1,0:T(8,128)S(1)} %get-tuple-element.37), channel_id=1, source_target_pairs={{0,24},{1,25},{8,0},{9,1},{16,8},{17,9},{24,16},{25,17},{32,56},{3... | collective-permute-start | bytes 1572872 | tf_op jit(solution)/shard_map/ppermute | solution.py:32
  15.7 21.1 %all-to-all-start = ((f32[32,8,256]{2,1,0:T(8,128)}), f32[32,8,256]{2,1,0:T(8,128)S(1)}, u32[]{:S(2)}, u32[]{:S(2)}) async-start(f32[32,8,256]{2,1,0:T(8,128)} %slice_bitcast_fusion.4), calls=%async_computation | async-start | bytes 524288 | tf_op jit(solution)/shard_map/all_to_all | solution.py:355
  37.5 11.5 %all-to-all-start.1 = ((f32[8,2,8,256]{3,2,1,0:T(8,128)}), f32[8,2,8,256]{3,2,1,0:T(8,128)S(1)}, u32[]{:S(2)}, u32[]{:S(2)}) async-start(f32[8,2,8,256]{3,2,1,0:T(8,128)} %broadcast_in_dim.6), calls=%async_computation.1 | async-start | bytes 262144 | tf_op jit(solution)/shard_map/all_to_all | solution.py:368
  43.9 5.1 %collective-permute-start.5 = (f32[128,256]{1,0:T(8,128)S(1)}, f32[128,256]{1,0:T(8,128)S(1)}, u32[]{:S(2)}, u32[]{:S(2)}) collective-permute-start(f32[128,256]{1,0:T(8,128)S(1)} %get-tuple-element.40), channel_id=1, source_target_pairs={{0,2},{1,3},{8,10},{9,11},{16,18},{17,19},{24,26},{25,27},{32,34},... | collective-permute-start | bytes 393224 | tf_op jit(solution)/shard_map/ppermute | solution.py:32
  45.2 5.9 %collective-permute-start.4 = (f32[128,256]{1,0:T(8,128)S(1)}, f32[128,256]{1,0:T(8,128)S(1)}, u32[]{:S(2)}, u32[]{:S(2)}) collective-permute-start(f32[128,256]{1,0:T(8,128)S(1)} %get-tuple-element.41), channel_id=1, source_target_pairs={{0,4},{1,5},{8,12},{9,13},{16,20},{17,21},{24,28},{25,29},{32,36},... | collective-permute-start | bytes 393224 | tf_op jit(solution)/shard_map/ppermute | solution.py:32
  46.5 10.0 %collective-permute-start.3 = (f32[128,256]{1,0:T(8,128)S(1)}, f32[128,256]{1,0:T(8,128)S(1)}, u32[]{:S(2)}, u32[]{:S(2)}) collective-permute-start(f32[128,256]{1,0:T(8,128)S(1)} %get-tuple-element.42), channel_id=1, source_target_pairs={{0,6},{1,7},{8,14},{9,15},{16,22},{17,23},{24,30},{25,31},{32,38},... | collective-permute-start | bytes 393224 | tf_op jit(solution)/shard_map/ppermute | solution.py:32
  57.2 16.1 %collective-permute-start.6 = (f32[128,256]{1,0:T(8,128)S(1)}, f32[128,256]{1,0:T(8,128)S(1)}, u32[]{:S(2)}, u32[]{:S(2)}) collective-permute-start(f32[128,256]{1,0:T(8,128)S(1)} %get-tuple-element.34), channel_id=1, source_target_pairs={{0,6},{1,7},{2,0},{3,1},{4,2},{5,3},{6,4},{7,5},{8,14},{9,15},{10,... | collective-permute-start | bytes 393224 | tf_op jit(solution)/shard_map/ppermute | solution.py:32
  61.6 13.7 %collective-permute-start.8 = (f32[128,256]{1,0:T(8,128)S(1)}, f32[128,256]{1,0:T(8,128)S(1)}, u32[]{:S(2)}, u32[]{:S(2)}) collective-permute-start(f32[128,256]{1,0:T(8,128)S(1)} %get-tuple-element.34), channel_id=1, source_target_pairs={{0,2},{1,3},{2,4},{3,5},{4,6},{5,7},{6,0},{7,1},{8,10},{9,11},{10,... | collective-permute-start | bytes 393224 | tf_op jit(solution)/shard_map/ppermute | solution.py:32
  61.7 12.9 %collective-permute-start.7 = (f32[128,256]{1,0:T(8,128)S(1)}, f32[128,256]{1,0:T(8,128)S(1)}, u32[]{:S(2)}, u32[]{:S(2)}) collective-permute-start(f32[128,256]{1,0:T(8,128)S(1)} %get-tuple-element.34), channel_id=1, source_target_pairs={{0,4},{1,5},{2,6},{3,7},{4,0},{5,1},{6,2},{7,3},{8,12},{9,13},{10,... | collective-permute-start | bytes 393224 | tf_op jit(solution)/shard_map/ppermute | solution.py:32
  64.6 22.1 %all-to-all-start.2 = ((f32[32,12,256]{2,1,0:T(8,128)}), f32[32,12,256]{2,1,0:T(8,128)S(1)}, u32[]{:S(2)}, u32[]{:S(2)}) async-start(f32[32,12,256]{2,1,0:T(8,128)} %broadcast_in_dim.7), calls=%async_computation.2 | async-start | bytes 1048576 | tf_op jit(solution)/shard_map/all_to_all | solution.py:377
  86.6 7.5 %collective-permute-start.9 = (f32[32,12,256]{2,1,0:T(8,128)S(1)}, f32[32,12,256]{2,1,0:T(8,128)S(1)}, u32[]{:S(2)}, u32[]{:S(2)}) collective-permute-start(f32[32,12,256]{2,1,0:T(8,128)S(1)} %all-to-all-done.2.own_ref), channel_id=1, source_target_pairs={{0,32},{1,33},{2,34},{3,35},{4,36},{5,37},{6,38},{7,39},{8,40},{9,... | collective-permute-start | bytes 1179656 | tf_op jit(solution)/shard_map/ppermute | solution.py:32
  94.1 52.2 %copy-start.10 = (f32[4,128,256]{2,1,0:T(8,128)}, f32[4,128,256]{2,1,0:T(8,128)S(1)}, u32[]{:S(2)}) copy-start(f32[4,128,256]{2,1,0:T(8,128)S(1)} %constant_dynamic-slice_fusion) | copy-start | bytes 1572868
  94.2 15.3 %collective-permute-start.11 = (f32[512,256]{1,0:T(8,128)S(1)}, f32[512,256]{1,0:T(8,128)S(1)}, u32[]{:S(2)}, u32[]{:S(2)}) collective-permute-start(f32[512,256]{1,0:T(8,128)S(1)} %bitcast.68), channel_id=1, source_target_pairs={{0,128},{1,129},{2,130},{3,131},{4,132},{5,133},{6,134},{7,135},{8... | collective-permute-start | bytes 1572872 | tf_op jit(solution)/shard_map/ppermute | solution.py:32
  97.0 13.3 %collective-permute-start.14 = (f32[512,256]{1,0:T(8,128)S(1)}, f32[512,256]{1,0:T(8,128)S(1)}, u32[]{:S(2)}, u32[]{:S(2)}) collective-permute-start(f32[512,256]{1,0:T(8,128)S(1)} %bitcast.69), channel_id=1, source_target_pairs={{0,24},{1,25},{2,26},{3,27},{4,28},{5,29},{6,30},{7,31},{8,0},{9,1... | collective-permute-start | bytes 1572872 | tf_op jit(solution)/shard_map/ppermute | solution.py:32
  97.7 14.6 %collective-permute-start.13 = (f32[512,256]{1,0:T(8,128)S(1)}, f32[512,256]{1,0:T(8,128)}, u32[]{:S(2)}, u32[]{:S(2)}) collective-permute-start(f32[512,256]{1,0:T(8,128)S(1)} %bitcast.70), channel_id=1, source_target_pairs={{0,16},{1,17},{2,18},{3,19},{4,20},{5,21},{6,22},{7,23},{8,24},{9,... | collective-permute-start | bytes 1572872 | tf_op jit(solution)/shard_map/ppermute | solution.py:32
  98.5 25.8 %collective-permute-start.12 = (f32[512,256]{1,0:T(8,128)S(1)}, f32[512,256]{1,0:T(8,128)}, u32[]{:S(2)}, u32[]{:S(2)}) collective-permute-start(f32[512,256]{1,0:T(8,128)S(1)} %bitcast.71), channel_id=1, source_target_pairs={{0,8},{1,9},{2,10},{3,11},{4,12},{5,13},{6,14},{7,15},{8,16},{9,17... | collective-permute-start | bytes 1572872 | tf_op jit(solution)/shard_map/ppermute | solution.py:32
  98.8 25.6 %collective-permute-start.10 = (f32[512,256]{1,0:T(8,128)S(1)}, f32[512,256]{1,0:T(8,128)}, u32[]{:S(2)}, u32[]{:S(2)}) collective-permute-start(f32[512,256]{1,0:T(8,128)S(1)} %bitcast.72), channel_id=1, source_target_pairs={{0,1},{1,0},{2,3},{3,2},{4,5},{5,4},{6,7},{7,6},{8,9},{9,8},{10,11... | collective-permute-start | bytes 1572872 | tf_op jit(solution)/shard_map/ppermute | solution.py:32
  110.4 14.0 %copy-start.11 = (f32[512,256]{1,0:T(8,128)}, f32[512,256]{1,0:T(8,128)S(1)}, u32[]{:S(2)}) copy-start(f32[512,256]{1,0:T(8,128)S(1)} %collective-permute-done.14.a3) | copy-start | bytes 1572868
  124.4 24.1 %collective-permute-start.15 = (f32[512,256]{1,0:T(8,128)S(1)}, f32[512,256]{1,0:T(8,128)S(1)}, u32[]{:S(2)}, u32[]{:S(2)}) collective-permute-start(f32[512,256]{1,0:T(8,128)S(1)} %broadcast_select_fusion), channel_id=1, source_target_pairs={{0,64},{1,65},{2,66},{3,67},{4,68},{5,69},{6,70},{7,71},{8,72},{9,... | collective-permute-start | bytes 1572872 | tf_op jit(solution)/shard_map/ppermute | solution.py:32
  124.6 23.9 %collective-permute-start.18 = (f32[512,256]{1,0:T(8,128)}, f32[512,256]{1,0:T(8,128)}, u32[]{:S(2)}, u32[]{:S(2)}) collective-permute-start(f32[512,256]{1,0:T(8,128)} %collective-permute-done.10.b0), channel_id=1, source_target_pairs={{0,24},{1,25},{2,26},{3,27},{4,28},{5,29},{6,30},{7,31},{8,0},{9,1... | collective-permute-start | bytes 1572872 | tf_op jit(solution)/shard_map/ppermute | solution.py:32
  124.6 23.9 %collective-permute-start.17 = (f32[512,256]{1,0:T(8,128)}, f32[512,256]{1,0:T(8,128)}, u32[]{:S(2)}, u32[]{:S(2)}) collective-permute-start(f32[512,256]{1,0:T(8,128)} %collective-permute-done.10.b0), channel_id=1, source_target_pairs={{0,16},{1,17},{2,18},{3,19},{4,20},{5,21},{6,22},{7,23},{8,24},{9,... | collective-permute-start | bytes 1572872 | tf_op jit(solution)/shard_map/ppermute | solution.py:32
  125.5 26.0 %collective-permute-start.16 = (f32[512,256]{1,0:T(8,128)}, f32[512,256]{1,0:T(8,128)}, u32[]{:S(2)}, u32[]{:S(2)}) collective-permute-start(f32[512,256]{1,0:T(8,128)} %collective-permute-done.10.b0), channel_id=1, source_target_pairs={{0,8},{1,9},{2,10},{3,11},{4,12},{5,13},{6,14},{7,15},{8,16},{9,17... | collective-permute-start | bytes 1572872 | tf_op jit(solution)/shard_map/ppermute | solution.py:32
  146.4 0.7 copy-start.4
  147.1 0.7 copy-start.6
  147.8 0.7 copy-start.8
  151.5 15.4 %collective-permute-start.19 = (f32[512,256]{1,0:T(8,128)S(1)}, f32[512,256]{1,0:T(8,128)S(1)}, u32[]{:S(2)}, u32[]{:S(2)}) collective-permute-start(f32[512,256]{1,0:T(8,128)S(1)} %broadcast_select_fusion.1), channel_id=1, source_target_pairs={{0,1},{1,0},{2,3},{3,2},{4,5},{5,4},{6,7},{7,6},{8,9},{9,8},{10,11... | collective-permute-start | bytes 1572872 | tf_op jit(solution)/shard_map/ppermute | solution.py:32
  154.2 16.0 %copy-start.5 = (f32[256,256]{1,0:T(8,128)S(1)}, f32[256,256]{1,0:T(8,128)}, u32[]{:S(2)}) copy-start(f32[256,256]{1,0:T(8,128)} %copy-done.4) | copy-start | bytes 786436
  154.2 16.0 %copy-start.7 = (f32[256,256]{1,0:T(8,128)S(1)}, f32[256,256]{1,0:T(8,128)}, u32[]{:S(2)}) copy-start(f32[256,256]{1,0:T(8,128)} %copy-done.6) | copy-start | bytes 786436
  154.2 16.0 %copy-start.9 = (f32[256,256]{1,0:T(8,128)S(1)}, f32[256,256]{1,0:T(8,128)}, u32[]{:S(2)}) copy-start(f32[256,256]{1,0:T(8,128)} %copy-done.8) | copy-start | bytes 786436
  166.9 3.3 %copy-start.1 = (f32[8,1,256,2,1,256]{5,4,3,2,1,0:T(1,128)S(1)}, f32[8,1,256,2,1,256]{5,4,3,2,1,0:T(1,128)}, u32[]{:S(2)}) copy-start(f32[8,1,256,2,1,256]{5,4,3,2,1,0:T(1,128)} %param.1) | copy-start | bytes 12582916
  166.9 3.3 %copy-start.2 = (s32[5]{0:T(128)S(1)}, s32[5]{0:T(128)}, u32[]{:S(2)}) copy-start(s32[5]{0:T(128)} %stack.55.info_ref) | copy-start | bytes 64
  167.1 3.1 %collective-permute-start.20 = (f32[2,512,256]{2,1,0:T(8,128)S(1)}, f32[2,512,256]{2,1,0:T(8,128)S(1)}, u32[]{:S(2)}, u32[]{:S(2)}) collective-permute-start(f32[2,512,256]{2,1,0:T(8,128)S(1)} %pad_maximum_fusion.own_ref), channel_id=1, source_target_pairs={{0,32},{1,33},{2,34},{3,35},{4,36},{5,37},{6,38},{7,39},{8,40},{9,... | collective-permute-start | bytes 3145736 | tf_op jit(solution)/shard_map/ppermute | solution.py:32
  170.3 2.2 %copy-start.3 = (f32[4,512,512]{2,1,0:T(8,128)S(1)}, f32[4,512,512]{2,1,0:T(8,128)}, u32[]{:S(2)}) copy-start(f32[4,512,512]{2,1,0:T(8,128)} %solve_rows.1.p_ref) | copy-start | bytes 12582916

commit v3 on v2

--- a/solution.py
+++ b/solution.py
@@ -141,26 +141,38 @@
     w_ref[...] = jnp.where(row >= lan, m_ref[...], 0.0)
 
 
-def factor_kernel(core_ref, own_ref, other_ref, l0_ref, w0_ref, p10_ref, l1_ref, w1_ref, m_ref, u_ref):
+def factor_kernel(core_ref, own_ref, other_ref, l0_out, w0_out, p10_out, l1_out, w1_out, m_ref, u_ref, tiles, sem):
+    l0_ref, w0_ref, p10_ref, l1_ref, w1_ref = (tiles.at[k] for k in range(5))
+    outs = (l0_out, w0_out, p10_out, l1_out, w1_out)
+    copies = [pltpu.make_async_copy(tiles.at[k], out, sem.at[k]) for k, out in enumerate(outs)]
     row = lax.broadcasted_iota(jnp.int32, (N, N), 0)
     lan = lax.broadcasted_iota(jnp.int32, (N, N), 1)
 
-    def half(core, lo, hi):
-        return jnp.where(core_ref[0] == core, own_ref[:, lo:hi, :], other_ref[:, lo:hi, :])
+    def part(core, k, lo=0, hi=8):
+        return jnp.where(core_ref[0] == core, own_ref[:, k, lo:hi, :], other_ref[:, k, lo:hi, :])
 
     def mirrored(core):
-        t = half(core, 0, 8).reshape(N, N)
+        t = jnp.concatenate([part(core, k).reshape(N, 128) for k in range(2)], 1)
         return jnp.where(row >= lan, t, t.T)
+
+    def between():
+        sides = [jnp.concatenate([part(core, 2, lo, lo + 4) for core in range(2)], 1) for lo in (0, 4)]
+        return jnp.concatenate([side.reshape(N, 128) for side in sides], 1)
 
     m_ref[...] = mirrored(0)
     factor_tile(m_ref, u_ref)
     read_out(l0_ref, w0_ref, m_ref, u_ref)
-    a10 = jnp.concatenate([half(0, 8, 12), half(1, 8, 12)], 1).reshape(N, N)
-    p10 = dot_nt(a10, w0_ref[...])
+    p10 = dot_nt(between(), w0_ref[...])
     p10_ref[...] = p10
+    for copy in copies[:3]:
+        copy.start()
     m_ref[...] = mirrored(1) - dot_nt(p10, p10)
     factor_tile(m_ref, u_ref)
     read_out(l1_ref, w1_ref, m_ref, u_ref)
+    for copy in copies[3:]:
+        copy.start()
+    for copy in copies:
+        copy.wait()
 
 
 def factor(core, own, other):
@@ -169,9 +181,9 @@
         factor_kernel,
         out_shape=[jax.ShapeDtypeStruct((N, N), F32)] * 5,
         in_specs=[pl.BlockSpec(memory_space=pltpu.SMEM), vmem, vmem],
-        out_specs=[vmem] * 5,
-        scratch_shapes=[pltpu.VMEM((N, N), F32)] * 2,
-        compiler_params=pltpu.CompilerParams(vmem_limit_bytes=24 << 20),
+        out_specs=[pl.BlockSpec(memory_space=pltpu.HBM)] * 5,
+        scratch_shapes=[pltpu.VMEM((N, N), F32)] * 2 + [pltpu.VMEM((5, N, N), F32), pltpu.SemaphoreType.DMA((5,))],
+        compiler_params=pltpu.CompilerParams(vmem_limit_bytes=60 << 20),
         cost_estimate=pl.CostEstimate(flops=10**9, bytes_accessed=60 << 20, transcendentals=0),
         name="factor",
     )(core, own, other)
@@ -195,41 +207,123 @@
     )(flat_blocks)
 
 
+def order_kernel(slot_ref, *refs):
+    pieces, o_ref = refs[:-1], refs[-1]
+    for d, piece in enumerate(pieces):
+        slot = lax.rem(slot_ref[0] + len(pieces) - d, len(pieces))
+        o_ref[pl.ds(pl.multiple_of(slot * 128, 128), 128), :] = piece[...]
+
+
+def order(slot, pieces):
+    return pl.pallas_call(
+        order_kernel,
+        out_shape=jax.ShapeDtypeStruct((2 * N, N), F32),
+        in_specs=[pl.BlockSpec(memory_space=pltpu.SMEM)] + [pl.BlockSpec(memory_space=pltpu.VMEM)] * 4,
+        out_specs=pl.BlockSpec(memory_space=pltpu.VMEM),
+        compiler_params=pltpu.CompilerParams(vmem_limit_bytes=8 << 20),
+        cost_estimate=pl.CostEstimate(flops=0, bytes_accessed=1 << 20, transcendentals=0),
+        name="order",
+    )(slot, *pieces)
+
+
 def split(v):
     hi = v.astype(BF16)
     return hi, (v - hi.astype(F32)).astype(BF16)
 
 
+def split3(v):
+    hi = v.astype(BF16)
+    rest = v - hi.astype(F32)
+    mid = rest.astype(BF16)
+    return hi, mid, (rest - mid.astype(F32)).astype(BF16)
+
+
+def six_left(v):
+    hi, mid, lo = split3(v)
+    return jnp.concatenate([lo, hi, mid, mid, hi, hi], 1)
+
+
+def six_right(v):
+    hi, mid, lo = split3(v)
+    return jnp.concatenate([hi, lo, mid, hi, mid, hi], 0)
+
+
+def dot16(a, b):
+    return jnp.dot(a, b, preferred_element_type=F32)
+
+
 def dot_nn(a, b):
     return jnp.dot(a, b, precision=lax.Precision.HIGHEST, preferred_element_type=F32)
 
 
-def rows_kernel(info_ref, w0_ref, p10_ref, w1_ref, a0, a1, a2, a3, b0, b1, b2, b3, o_ref):
+def own_kernel(info_ref, w0_ref, p10_ref, w1_ref, a0, a1, a2, a3, o_ref, turned_ref, w_s):
     t = pl.program_id(0)
-    odd = info_ref[3]
-    for d, (mine, others) in enumerate(((a0, b0), (a1, b1), (a2, b2), (a3, b3))):
+
+    @pl.when(t == 0)
+    def _():
+        turned_ref[...] = dot_nn(w1_ref[...], p10_ref[...])
+        w_s[...] = six_right(jnp.where(info_ref[3] == 0, w0_ref[...], w1_ref[...]).T)
+
+    for d, mine in enumerate((a0, a1, a2, a3)):
         @pl.when(t == d)
-        def _(mine=mine, others=others):
-            even = odd == 0
-            x0 = jnp.where(even, mine[...], others[...])
-            x1 = jnp.where(even, others[...], mine[...])
-            first = dot_nt(x0, w0_ref[...])
+        def _(mine=mine):
+            o_ref[0] = dot16(six_left(mine[...]), w_s[...])
+
+
+def solve_own(info, w0, p10, w1, own_quarters):
+    whole = lambda *shape: pl.BlockSpec(shape, lambda t: (0,) * len(shape))
+    return pl.pallas_call(
+        own_kernel,
+        grid=(4,),
+        in_specs=[pl.BlockSpec(memory_space=pltpu.SMEM)] + [whole(N, N)] * 3 + [whole(2 * N, N)] * 4,
+        out_specs=[pl.BlockSpec((1, 2 * N, N), lambda t: (t, 0, 0)), whole(N, N)],
+        out_shape=[jax.ShapeDtypeStruct((4, 2 * N, N), F32), jax.ShapeDtypeStruct((N, N), F32)],
+        scratch_shapes=[pltpu.VMEM((6 * N, N), BF16)],
+        compiler_params=pltpu.CompilerParams(vmem_limit_bytes=60 << 20, dimension_semantics=("arbitrary",)),
+        cost_estimate=pl.CostEstimate(flops=2 * 10**9, bytes_accessed=60 << 20, transcendentals=0),
+        name="solve_own",
+    )(info, w0, p10, w1, *own_quarters)
+
+
+def rows_kernel(info_ref, w0_ref, w1_ref, turned_ref, part_ref, others_ref, lower_ref, u1, u2, u3, o_ref, w_s, t_s):
+    t = pl.program_id(0)
+    even = info_ref[3] == 0
+
+    @pl.when(t == 0)
+    def _():
+        w_s[...] = six_right(jnp.where(even, w1_ref[...], w0_ref[...]).T)
+        t_s[...] = six_right(turned_ref[...].T)
+
+    for d, upper in enumerate((None, u1, u2, u3)):
+        @pl.when(t == d)
+        def _(d=d, upper=upper):
+            if d == 0:
+                others = others_ref[...]
+            else:
+                others = jnp.concatenate([lower_ref[d * N - N : d * N, :], upper[...]], 0)
+            part = part_ref[0]
+            rest = dot16(six_left(others), w_s[...])
+            first = jnp.where(even, part, rest)
             o_ref[0, :, :N] = first
-            o_ref[0, :, N:] = dot_nt(x1 - dot_nt(first, p10_ref[...]), w1_ref[...])
-
-
-def solve_rows(info, w0, p10, w1, own_quarters, other_quarters):
+            o_ref[0, :, N:] = jnp.where(even, rest, part) - dot16(six_left(first), t_s[...])
+
+
+def solve_rows(info, w0, w1, turned, part, others, lower, upper):
     whole = lambda *shape: pl.BlockSpec(shape, lambda t: (0,) * len(shape))
     return pl.pallas_call(
         rows_kernel,
         grid=(4,),
-        in_specs=[pl.BlockSpec(memory_space=pltpu.SMEM)] + [whole(N, N)] * 3 + [whole(2 * N, N)] * 8,
+        in_specs=[pl.BlockSpec(memory_space=pltpu.SMEM)]
+        + [whole(N, N)] * 3
+        + [pl.BlockSpec((1, 2 * N, N), lambda t: (t, 0, 0)), whole(2 * N, N), whole(3 * N, N)]
+        + [whole(N, N)] * 3,
         out_specs=pl.BlockSpec((1, 2 * N, 2 * N), lambda t: (t, 0, 0)),
         out_shape=jax.ShapeDtypeStruct((4, 2 * N, 2 * N), F32),
+        scratch_shapes=[pltpu.VMEM((6 * N, N), BF16)] * 2,
         compiler_params=pltpu.CompilerParams(vmem_limit_bytes=60 << 20, dimension_semantics=("arbitrary",)),
         cost_estimate=pl.CostEstimate(flops=5 * 10**9, bytes_accessed=9 << 20, transcendentals=0),
         name="solve_rows",
-    )(info, w0, p10, w1, *own_quarters, *other_quarters)
+    )(info, w0, w1, turned, part, others, lower, *upper)
 
 
 def update_kernel(
@@ -263,9 +357,6 @@
     def change(h, b):
         hi, lo = split(p_ref[0, h * N : h * N + N, :])
         cols = slice(b * N, b * N + N)
-
-        def dot16(u, v):
-            return jnp.dot(u, v, preferred_element_type=F32)
 
         product = dot16(lo, chi[:, cols]) + dot16(hi, clo[:, cols]) + dot16(hi, chi[:, cols])
         put(h, b, get(h, b) - product)
@@ -349,7 +440,7 @@
     column = first_column(flat_blocks)
 
     arrived = [
-        send(column[d], lambda y, c, x, z, d=d: (y, c, (x + d) % NX, z) if z < 2 else None) for d in (1, 2, 3)
+        send(column[d], lambda y, c, x, z, d=d: (y, c, d, z) if x == 0 and z < 2 else None) for d in (1, 2, 3)
     ]
 
     own_rows = lax.all_to_all(column[0, 0].reshape(32, 8, N), "col", 0, 0, tiled=True)[:2]
@@ -367,31 +458,32 @@
     piece = pick(z // 2, [parts[0], *sent])
     tile_rows = lax.all_to_all(jnp.broadcast_to(own_rows[None], (8, 2, 8, N)), "row", 0, 0, tiled=True)
     lead, middle, last = tile_rows[0, 0], tile_rows[1, 0], tile_rows[1, 1]
-    core_rows = jnp.where(
-        core == 0, jnp.concatenate([lead, middle[:4]], 0), jnp.concatenate([last, middle[4:]], 0)
-    )
+    whole, part = jnp.where(core == 0, lead, last), jnp.where(core == 0, middle[:4], middle[4:])
+    core_rows = jnp.stack([whole[:, :128], whole[:, 128:], jnp.concatenate([part[:, :128], part[:, 128:]], 0)])
+    piece, core_rows = lax.optimization_barrier((piece, core_rows))
     pieces = [piece] + [send(piece, lambda y, c, x, z, d=d: (y, c, x, (z + 2 * d) % NZ)) for d in (1, 2, 3)]
-    ordered = jnp.stack([pieces[0], pieces[3], pieces[2], pieces[1]] * 2)
-    mine = lax.dynamic_slice_in_dim(ordered, (4 - z // 2) % 4, 4, 0).reshape(2 * N, N)
-    piece, core_rows = lax.optimization_barrier((piece, core_rows))
-    core_rows = lax.all_to_all(jnp.broadcast_to(core_rows[None], (32, 12, N)), "col", 0, 0, tiled=True)
+    mine = order((z // 2).astype(jnp.int32)[None], pieces)
+    core_rows = lax.all_to_all(jnp.broadcast_to(core_rows[None], (32, 3, 8, 128)), "col", 0, 0, tiled=True)
+    mine, core_rows = lax.optimization_barrier((mine, core_rows))
     other_rows = send(core_rows, lambda y, c, x, z: (y, 1 - c, x, z))
-    mine = after(mine, other_rows)
 
     own_quarters = [mine] + [send(mine, lambda y, c, x, z, d=d: (y, c, (x + d) % NX, z)) for d in (1, 2, 3)]
     others = send(mine, lambda y, c, x, z: (y, c, x, z ^ 1))
     turn = (y - z // 2 + NY) % NY
     two = send(mine, lambda y, c, x, z: ((y + 2) % NY, c, x, z))
     half = jnp.where(turn >= 2, two, mine)
-    others, half, core_rows, *_ = lax.optimization_barrier((others, half, core_rows, *own_quarters))
-
-    other_quarters = [others] + [send(others, lambda y, c, x, z, d=d: (y, c, (x + d) % NX, z)) for d in (1, 2, 3)]
+    l0, w0, p10, l1, w1 = factor(core.astype(jnp.int32)[None], core_rows, other_rows)
+    others, half, *_ = lax.optimization_barrier((others, half, l1, *own_quarters))
+
+    upper = [send(others[N:], lambda y, c, x, z, d=d: (y, c, (x + d) % NX, z)) for d in (1, 2, 3)]
+    lower = send(jnp.concatenate([q[:N] for q in own_quarters[1:]], 0), lambda y, c, x, z: (y, c, x, z ^ 1))
     one = send(half, lambda y, c, x, z: ((y + 1) % NY, c, x, z))
-    l0, w0, p10, l1, w1 = factor(core.astype(jnp.int32)[None], core_rows, other_rows)
-    half = after(jnp.where(turn % 2 == 1, one, half), l1, *other_quarters)
+    info = jnp.stack([row_index, col_index, core == z % 2, z % 2, x]).astype(jnp.int32)
+    first_part, turned = solve_own(info, w0, p10, w1, own_quarters)
+    one, half, *_ = lax.optimization_barrier((one, half, first_part, lower, *upper))
+    half = jnp.where(turn % 2 == 1, one, half)
     next_half = send(half, lambda y, c, x, z: (y, c, x, z ^ 1))
-    info = jnp.stack([row_index, col_index, core == z % 2, z % 2, x]).astype(jnp.int32)
-    rows = solve_rows(info, w0, p10, w1, own_quarters, other_quarters)
+    rows = solve_rows(info, w0, w1, turned, first_part, others, lower, upper)
     next_half, rows = lax.optimization_barrier((next_half, rows))
     panel = jnp.stack([jnp.where(z % 2 == 0, half, next_half), jnp.where(z % 2 == 0, next_half, half)])
     other_panel = send(panel, lambda y, c, x, z: (y, 1 - c, x, z))

time: 179 us -> 168 us (0.939)
  waiting for transfers between devices: 64.1 us -> 46.8 us
  local copies, waits for them, and re-layouts: 16.2 us -> 10.3 us
  starting transfers between devices: 57.7 us -> 63.6 us
  Pallas kernels: 39.2 us -> 44.5 us
    all_to_all x1, waiting for transfers between devices: 9.36 us -> 0.01 us  [on_device(): lax.all_to_all(jnp.broadcast_to(core_rows[None], (32, 3, 8, 128)), 'col',...]
    pallas_call x0 -> x2, Pallas kernels: none -> 5.69 us  [the longest x1 5.65 us: solve_own(): pl.pallas_call(own_kernel, grid=(4,), in_specs=[pl.BlockSpec(memory_space...]
    unnamed x30 -> x34, local copies, waits for them, and re-layouts: 10.5 us -> 5.39 us
    all_to_all x1, waiting for transfers between devices: 16.8 us -> 12.5 us  [on_device(): lax.all_to_all(column[0, 0].reshape(32, 8, N), 'col', 0, 0, tiled=True)[:2]]
    ppermute x21 -> x22, waiting for transfers between devices: 36.8 us -> 34.3 us  [send(): return lax.ppermute(value, ('row', 'col'), pairs(fn))]
    pallas_call x1, Pallas kernels: 12.7 us -> 10.3 us  [solve_rows(): pl.pallas_call(rows_kernel, grid=(4,), in_specs=[pl.BlockSpec(memory_spac...]
    ppermute x21 -> x22, starting transfers between devices: 38.6 us -> 40.9 us  [send(): return lax.ppermute(value, ('row', 'col'), pairs(fn))]
    all_to_all x1, starting transfers between devices: 4.13 us -> 6.42 us  [on_device(): lax.all_to_all(column[0, 0].reshape(32, 8, N), 'col', 0, 0, tiled=True)[:2]]
  transfers between devices with their start and end apart: 24 -> 25, of which waited for: 12 -> 11; matrix products, arithmetic and copies ran while one was open for 5% -> 2% of each run, Pallas kernels for 18% -> 23%
where the time goes in v3:
time: 168 us; the launch traced here: 166 us
  starting transfers between devices  63.6 us (38%)
  waiting for transfers between devices  46.8 us (28%)
  Pallas kernels  44.5 us (26%)
  local copies, waits for them, and re-layouts  10.3 us (6%)
    ppermute x22, starting transfers between devices, send(): return lax.ppermute(value, ('row', 'col'), pairs(fn))  40.9 us
    ppermute x22, waiting for transfers between devices, send(): return lax.ppermute(value, ('row', 'col'), pairs(fn))  34.3 us
    pallas_call x1, Pallas kernels, factor(): pl.pallas_call(factor_kernel, out_shape=[jax.ShapeDtypeStruct((N, N), F32...  21.9 us
    all_to_all x1, waiting for transfers between devices, on_device(): lax.all_to_all(column[0, 0].reshape(32, 8, N), 'col', 0, 0, tiled=True)[:2]  12.5 us
    pallas_call x1, Pallas kernels, solve_rows(): pl.pallas_call(rows_kernel, grid=(4,), in_specs=[pl.BlockSpec(memory_spac...  10.3 us
    all_to_all x1, starting transfers between devices, on_device(): lax.all_to_all(jnp.broadcast_to(core_rows[None], (32, 3, 8, 128)), 'col',...  10.3 us
    all_to_all x1, starting transfers between devices, on_device(): lax.all_to_all(column[0, 0].reshape(32, 8, N), 'col', 0, 0, tiled=True)[:2]  6.42 us
    pallas_call x1, Pallas kernels, update(): pl.pallas_call(update_kernel, grid_spec=pltpu.PrefetchScalarGridSpec(num_...  6.22 us
  transfers between devices with their start and end apart: 25, of which 11 were waited for; matrix products, arithmetic and copies ran while one was open for 2% of the time, Pallas kernels for 23%

profile of v3, /device:TPU:1, one launch (start us, length us, event | category | flops | bytes accessed | tf_op | source)
XLA Modules:
  0.0 166.3 jit_solution(13121647522048883290)
XLA Ops:
  0.0 2.2 %copy-done = f32[8,1,256,2,1,256]{5,4,3,2,1,0:T(1,128)S(1)} copy-done((f32[8,1,256,2,1,256]{5,4,3,2,1,0:T(1,128)S(1)}, f32[8,1,256,2,1,256]{5,4,3,2,1,0:T(1,128)}, u32[]{:S(2)}) %copy-start) | copy-done | bytes 4194328
  2.2 0.3 first_column.1
  2.5 1.1 slice_bitcast_fusion.1
  3.6 4.0 %collective-permute-start.2 = (f32[2,256,256]{2,1,0:T(8,128)}, f32[2,256,256]{2,1,0:T(8,128)S(1)}, u32[]{:S(2)}, u32[]{:S(2)}) collective-permute-start(f32[2,256,256]{2,1,0:T(8,128)} %get-tuple-element.41), channel_id=1, source_target_pairs={{0,8},{1,9},{32,40},{33,41},{64,72},{65,73},{96,104},{97,105},{128... | collective-permute-start | bytes 1572872 | tf_op jit(solution)/shard_map/ppermute | solution.py:32
  7.6 3.0 %collective-permute-start.1 = (f32[2,256,256]{2,1,0:T(8,128)}, f32[2,256,256]{2,1,0:T(8,128)}, u32[]{:S(2)}, u32[]{:S(2)}) collective-permute-start(f32[2,256,256]{2,1,0:T(8,128)} %get-tuple-element.42), channel_id=1, source_target_pairs={{0,16},{1,17},{32,48},{33,49},{64,80},{65,81},{96,112},{97,113},{1... | collective-permute-start | bytes 1572872 | tf_op jit(solution)/shard_map/ppermute | solution.py:32
  10.6 2.1 %collective-permute-start = (f32[2,256,256]{2,1,0:T(8,128)S(1)}, f32[2,256,256]{2,1,0:T(8,128)}, u32[]{:S(2)}, u32[]{:S(2)}) collective-permute-start(f32[2,256,256]{2,1,0:T(8,128)S(1)} %get-tuple-element.43), channel_id=1, source_target_pairs={{0,24},{1,25},{32,56},{33,57},{64,88},{65,89},{96,120},{97,121},{1... | collective-permute-start | bytes 1572872 | tf_op jit(solution)/shard_map/ppermute | solution.py:32
  12.7 0.7 slice_bitcast_fusion.4
  13.4 6.4 %all-to-all-start = ((f32[32,8,256]{2,1,0:T(8,128)}), f32[32,8,256]{2,1,0:T(8,128)S(1)}, u32[]{:S(2)}, u32[]{:S(2)}) async-start(f32[32,8,256]{2,1,0:T(8,128)} %slice_bitcast_fusion.4), calls=%async_computation | async-start | bytes 524288 | tf_op jit(solution)/shard_map/all_to_all | solution.py:446
  20.0 12.5 %all-to-all-done = f32[32,8,256]{2,1,0:T(8,128)S(1)} async-done(((f32[32,8,256]{2,1,0:T(8,128)}), f32[32,8,256]{2,1,0:T(8,128)S(1)}, u32[]{:S(2)}, u32[]{:S(2)}) %all-to-all-start) | async-done | bytes 262176 | tf_op jit(solution)/shard_map/all_to_all | solution.py:446
  32.5 0.7 broadcast_in_dim.9
  33.1 6.0 %all-to-all-start.1 = ((f32[8,2,8,256]{3,2,1,0:T(8,128)}), f32[8,2,8,256]{3,2,1,0:T(8,128)S(1)}, u32[]{:S(2)}, u32[]{:S(2)}) async-start(f32[8,2,8,256]{3,2,1,0:T(8,128)} %broadcast_in_dim.9), calls=%async_computation.1 | async-start | bytes 262144 | tf_op jit(solution)/shard_map/all_to_all | solution.py:459
  39.4 2.7 %collective-permute-start.5 = (f32[128,256]{1,0:T(8,128)S(1)}, f32[128,256]{1,0:T(8,128)S(1)}, u32[]{:S(2)}, u32[]{:S(2)}) collective-permute-start(f32[128,256]{1,0:T(8,128)S(1)} %get-tuple-element.46), channel_id=1, source_target_pairs={{0,2},{1,3},{8,10},{9,11},{16,18},{17,19},{24,26},{25,27},{32,34},... | collective-permute-start | bytes 393224 | tf_op jit(solution)/shard_map/ppermute | solution.py:32
  42.1 1.3 collective-permute-start.4
  43.4 1.3 collective-permute-start.3
  45.0 2.8 %collective-permute-done.4 = f32[128,256]{1,0:T(8,128)S(1)} collective-permute-done((f32[128,256]{1,0:T(8,128)S(1)}, f32[128,256]{1,0:T(8,128)S(1)}, u32[]{:S(2)}, u32[]{:S(2)}) %collective-permute-start.4) | collective-permute-done | bytes 131104 | tf_op jit(solution)/shard_map/ppermute | solution.py:32
  47.8 4.5 %collective-permute-done.3 = f32[128,256]{1,0:T(8,128)S(1)} collective-permute-done((f32[128,256]{1,0:T(8,128)S(1)}, f32[128,256]{1,0:T(8,128)S(1)}, u32[]{:S(2)}, u32[]{:S(2)}) %collective-permute-start.3) | collective-permute-done | bytes 131104 | tf_op jit(solution)/shard_map/ppermute | solution.py:32
  52.3 0.8 broadcast_in_dim.20
  53.1 10.3 %all-to-all-start.2 = ((f32[32,3,8,128]{3,2,1,0:T(8,128)}), f32[32,3,8,128]{3,2,1,0:T(8,128)S(1)}, u32[]{:S(2)}, u32[]{:S(2)}) async-start(f32[32,3,8,128]{3,2,1,0:T(8,128)} %broadcast_in_dim.20), calls=%async_computation.2 | async-start | bytes 786432 | tf_op jit(solution)/shard_map/all_to_all | solution.py:466
  63.4 3.4 %collective-permute-start.8 = (f32[128,256]{1,0:T(8,128)S(1)}, f32[128,256]{1,0:T(8,128)S(1)}, u32[]{:S(2)}, u32[]{:S(2)}) collective-permute-start(f32[128,256]{1,0:T(8,128)S(1)} %fusion.5.refs_0_), channel_id=1, source_target_pairs={{0,6},{1,7},{2,0},{3,1},{4,2},{5,3},{6,4},{7,5},{8,14},{9,15},{10,... | collective-permute-start | bytes 393224 | tf_op jit(solution)/shard_map/ppermute | solution.py:32
  66.8 2.1 %collective-permute-start.7 = (f32[128,256]{1,0:T(8,128)S(1)}, f32[128,256]{1,0:T(8,128)S(1)}, u32[]{:S(2)}, u32[]{:S(2)}) collective-permute-start(f32[128,256]{1,0:T(8,128)S(1)} %fusion.5.refs_0_), channel_id=1, source_target_pairs={{0,4},{1,5},{2,6},{3,7},{4,0},{5,1},{6,2},{7,3},{8,12},{9,13},{10,... | collective-permute-start | bytes 393224 | tf_op jit(solution)/shard_map/ppermute | solution.py:32
  68.9 2.1 %collective-permute-start.6 = (f32[128,256]{1,0:T(8,128)S(1)}, f32[128,256]{1,0:T(8,128)S(1)}, u32[]{:S(2)}, u32[]{:S(2)}) collective-permute-start(f32[128,256]{1,0:T(8,128)S(1)} %fusion.5.refs_0_), channel_id=1, source_target_pairs={{0,2},{1,3},{2,4},{3,5},{4,6},{5,7},{6,0},{7,1},{8,10},{9,11},{10,... | collective-permute-start | bytes 393224 | tf_op jit(solution)/shard_map/ppermute | solution.py:32
  71.0 8.5 %collective-permute-done.8.refs_3_ = f32[128,256]{1,0:T(8,128)S(1)} collective-permute-done((f32[128,256]{1,0:T(8,128)S(1)}, f32[128,256]{1,0:T(8,128)S(1)}, u32[]{:S(2)}, u32[]{:S(2)}) %collective-permute-start.8) | collective-permute-done | bytes 131104 | tf_op jit(solution)/shard_map/ppermute | solution.py:32
  79.5 2.4 %collective-permute-done.7.refs_2_ = f32[128,256]{1,0:T(8,128)S(1)} collective-permute-done((f32[128,256]{1,0:T(8,128)S(1)}, f32[128,256]{1,0:T(8,128)S(1)}, u32[]{:S(2)}, u32[]{:S(2)}) %collective-permute-start.7) | collective-permute-done | bytes 131104 | tf_op jit(solution)/shard_map/ppermute | solution.py:32
  81.9 4.7 %collective-permute-done.6.refs_1_ = f32[128,256]{1,0:T(8,128)S(1)} collective-permute-done((f32[128,256]{1,0:T(8,128)S(1)}, f32[128,256]{1,0:T(8,128)S(1)}, u32[]{:S(2)}, u32[]{:S(2)}) %collective-permute-start.6) | collective-permute-done | bytes 131104 | tf_op jit(solution)/shard_map/ppermute | solution.py:32
  86.7 2.3 %collective-permute-start.14 = (f32[512,256]{1,0:T(8,128)S(1)}, f32[512,256]{1,0:T(8,128)S(1)}, u32[]{:S(2)}, u32[]{:S(2)}) collective-permute-start(f32[512,256]{1,0:T(8,128)S(1)} %order.1.a0), channel_id=1, source_target_pairs={{0,24},{1,25},{2,26},{3,27},{4,28},{5,29},{6,30},{7,31},{8,0},{9,1... | collective-permute-start | bytes 1572872 | tf_op jit(solution)/shard_map/ppermute | solution.py:32
  89.0 0.5 collective-permute-start.13
  89.5 0.6 collective-permute-start.12
  90.1 2.6 %collective-permute-start.11 = (f32[32,3,8,128]{3,2,1,0:T(8,128)S(1)}, f32[32,3,8,128]{3,2,1,0:T(8,128)S(1)}, u32[]{:S(2)}, u32[]{:S(2)}) collective-permute-start(f32[32,3,8,128]{3,2,1,0:T(8,128)S(1)} %all-to-all-done.2.own_ref), channel_id=1, source_target_pairs={{0,32},{1,33},{2,34},{3,35},{4,36},{5,37},{6,38},{7,39},{8,40},{9,... | collective-permute-start | bytes 1179656 | tf_op jit(solution)/shard_map/ppermute | solution.py:32
  92.7 2.9 %collective-permute-start.10 = (f32[512,256]{1,0:T(8,128)S(1)}, f32[512,256]{1,0:T(8,128)S(1)}, u32[]{:S(2)}, u32[]{:S(2)}) collective-permute-start(f32[512,256]{1,0:T(8,128)S(1)} %order.1.a0), channel_id=1, source_target_pairs={{0,128},{1,129},{2,130},{3,131},{4,132},{5,133},{6,134},{7,135},{8... | collective-permute-start | bytes 1572872 | tf_op jit(solution)/shard_map/ppermute | solution.py:32
  95.6 2.1 %collective-permute-start.9 = (f32[512,256]{1,0:T(8,128)S(1)}, f32[512,256]{1,0:T(8,128)S(1)}, u32[]{:S(2)}, u32[]{:S(2)}) collective-permute-start(f32[512,256]{1,0:T(8,128)S(1)} %order.1.a0), channel_id=1, source_target_pairs={{0,1},{1,0},{2,3},{3,2},{4,5},{5,4},{6,7},{7,6},{8,9},{9,8},{10,11... | collective-permute-start | bytes 1572872 | tf_op jit(solution)/shard_map/ppermute | solution.py:32
  97.6 21.9 %factor.1 = (f32[256,256]{1,0:T(8,128)}, f32[256,256]{1,0:T(8,128)}, f32[256,256]{1,0:T(8,128)}, f32[256,256]{1,0:T(8,128)}, f32[256,256]{1,0:T(8,128)}) custom-call(s32[1]{0:T(128)} %bitcast.23.core_ref, f32[32,3,8,128]{3,2,1,0:T(8,128)} %copy-done.10, f32[32,3,8,128]{3,2,1,0:T(8,128)} %copy-done.14), custom_call_target="tpu_custom_call" | custom-call | flops 1000000000 | bytes 62914560 | tf_op jit(solution)/shard_map/factor/pallas_call | solution.py:180
  119.7 0.7 copy-done.12
  120.6 1.0 slice.98
  121.7 0.8 collective-permute-start.16
  122.6 0.4 collective-permute-start.15
  123.0 2.2 %collective-permute-start.19 = (f32[256,256]{1,0:T(8,128)S(1)}, f32[256,256]{1,0:T(8,128)S(1)}, u32[]{:S(2)}, u32[]{:S(2)}) collective-permute-start(f32[256,256]{1,0:T(8,128)S(1)} %slice.82), channel_id=1, source_target_pairs={{0,24},{1,25},{2,26},{3,27},{4,28},{5,29},{6,30},{7,31},{8,0},{9,1... | collective-permute-start | bytes 786440 | tf_op jit(solution)/shard_map/ppermute | solution.py:32
  125.2 1.2 collective-permute-start.18
  126.4 0.7 stack.48.info_ref
  127.1 5.7 %solve_own.1 = (f32[4,512,256]{2,1,0:T(8,128)}, f32[256,256]{1,0:T(8,128)}) custom-call(s32[5]{0:T(128)} %stack.48.info_ref, f32[256,256]{1,0:T(8,128)} %get-tuple-element.30.w0_ref, f32[256,256]{1,0:T(8,128)} %get-tuple-element.31.p10_ref, f32[256,256]{1,0:T(8,128)} %get-tuple-element.32.w1_ref, f32[512,256]{1,0:T(8,128)} %copy-done.2, ...), custom_call_target="tpu_custom_call" | custom-call | flops 2000000000 | bytes 62914560 | tf_op jit(solution)/shard_map/solve_own/pallas_call | solution.py:275
  132.7 0.6 collective-permute-done.18.u2
  133.4 7.2 %collective-permute-done.17.u1 = f32[256,256]{1,0:T(8,128)} collective-permute-done((f32[256,256]{1,0:T(8,128)S(1)}, f32[256,256]{1,0:T(8,128)}, u32[]{:S(2)}, u32[]{:S(2)}) %collective-permute-start.17) | collective-permute-done | bytes 262176 | tf_op jit(solution)/shard_map/ppermute | solution.py:32
  140.7 1.2 collective-permute-start.20
  141.9 10.3 %solve_rows.1.p_ref = f32[4,512,512]{2,1,0:T(8,128)} custom-call(s32[5]{0:T(128)} %stack.48.info_ref, f32[256,256]{1,0:T(8,128)} %get-tuple-element.30.w0_ref, f32[256,256]{1,0:T(8,128)} %get-tuple-element.32.w1_ref, f32[256,256]{1,0:T(8,128)} %get-tuple-element.37.turned_ref, f32[4,512,256]{2,1,0:T(8,128)} %get-tuple-element.33.part_ref, ...), custom_call_target="tpu_custom_call" | custom-call | flops 5000000000 | bytes 9437184 | tf_op jit(solution)/shard_map/solve_rows/pallas_call | solution.py:313
  152.3 1.0 collective-permute-done.20
  153.4 2.2 %collective-permute-start.21 = (f32[2,512,256]{2,1,0:T(8,128)S(1)}, f32[2,512,256]{2,1,0:T(8,128)S(1)}, u32[]{:S(2)}, u32[]{:S(2)}) collective-permute-start(f32[2,512,256]{2,1,0:T(8,128)S(1)} %pad_maximum_fusion.own_ref), channel_id=1, source_target_pairs={{0,32},{1,33},{2,34},{3,35},{4,36},{5,37},{6,38},{7,39},{8,40},{9,... | collective-permute-start | bytes 3145736 | tf_op jit(solution)/shard_map/ppermute | solution.py:32
  155.6 2.3 %collective-permute-done.21.other_ref = f32[2,512,256]{2,1,0:T(8,128)S(1)} collective-permute-done((f32[2,512,256]{2,1,0:T(8,128)S(1)}, f32[2,512,256]{2,1,0:T(8,128)S(1)}, u32[]{:S(2)}, u32[]{:S(2)}) %collective-permute-start.21) | collective-permute-done | bytes 1048608 | tf_op jit(solution)/shard_map/ppermute | solution.py:32
  157.9 2.2 %copy-done.4 = f32[4,512,512]{2,1,0:T(8,128)S(1)} copy-done((f32[4,512,512]{2,1,0:T(8,128)S(1)}, f32[4,512,512]{2,1,0:T(8,128)}, u32[]{:S(2)}) %copy-start.4) | copy-done | bytes 4194328
  160.1 6.2 %update.1 = f32[2,4096,128]{2,1,0:T(8,128)} custom-call(s32[5]{0:T(128)S(1)} %copy-done.3, f32[2,4096,128]{2,1,0:T(8,128)S(1)} %bitcast.56, f32[4,512,512]{2,1,0:T(8,128)S(1)} %copy-done.4, f32[2,512,256]{2,1,0:T(8,128)S(1)} %pad_maximum_fusion.own_ref, f32[2,512,256]{2,1,0:T(8,128)S(1)} %collective-permute-done.21.other_ref, f32[256,256]{1,0:T(8,128)S(1)} %copy-done.5, ...), custom_call_target="tpu_custom_call" | custom-call | flops 5000000000 | bytes 16777216 | tf_op jit(solution)/shard_map/update/pallas_call | solution.py:405
  (66 shorter events, 1.3 us)
Async XLA Ops:
  0.0 2.2 %copy-start = (f32[8,1,256,2,1,256]{5,4,3,2,1,0:T(1,128)S(1)}, f32[8,1,256,2,1,256]{5,4,3,2,1,0:T(1,128)}, u32[]{:S(2)}) copy-start(f32[8,1,256,2,1,256]{5,4,3,2,1,0:T(1,128)} %param.1) | copy-start | bytes 12582916
  3.6 35.5 %collective-permute-start.2 = (f32[2,256,256]{2,1,0:T(8,128)}, f32[2,256,256]{2,1,0:T(8,128)S(1)}, u32[]{:S(2)}, u32[]{:S(2)}) collective-permute-start(f32[2,256,256]{2,1,0:T(8,128)} %get-tuple-element.41), channel_id=1, source_target_pairs={{0,8},{1,9},{32,40},{33,41},{64,72},{65,73},{96,104},{97,105},{128... | collective-permute-start | bytes 1572872 | tf_op jit(solution)/shard_map/ppermute | solution.py:32
  7.6 31.6 %collective-permute-start.1 = (f32[2,256,256]{2,1,0:T(8,128)}, f32[2,256,256]{2,1,0:T(8,128)}, u32[]{:S(2)}, u32[]{:S(2)}) collective-permute-start(f32[2,256,256]{2,1,0:T(8,128)} %get-tuple-element.42), channel_id=1, source_target_pairs={{0,16},{1,17},{32,48},{33,49},{64,80},{65,81},{96,112},{97,113},{1... | collective-permute-start | bytes 1572872 | tf_op jit(solution)/shard_map/ppermute | solution.py:32
  10.6 28.5 %collective-permute-start = (f32[2,256,256]{2,1,0:T(8,128)S(1)}, f32[2,256,256]{2,1,0:T(8,128)}, u32[]{:S(2)}, u32[]{:S(2)}) collective-permute-start(f32[2,256,256]{2,1,0:T(8,128)S(1)} %get-tuple-element.43), channel_id=1, source_target_pairs={{0,24},{1,25},{32,56},{33,57},{64,88},{65,89},{96,120},{97,121},{1... | collective-permute-start | bytes 1572872 | tf_op jit(solution)/shard_map/ppermute | solution.py:32
  13.4 19.0 %all-to-all-start = ((f32[32,8,256]{2,1,0:T(8,128)}), f32[32,8,256]{2,1,0:T(8,128)S(1)}, u32[]{:S(2)}, u32[]{:S(2)}) async-start(f32[32,8,256]{2,1,0:T(8,128)} %slice_bitcast_fusion.4), calls=%async_computation | async-start | bytes 524288 | tf_op jit(solution)/shard_map/all_to_all | solution.py:446
  33.1 11.6 %all-to-all-start.1 = ((f32[8,2,8,256]{3,2,1,0:T(8,128)}), f32[8,2,8,256]{3,2,1,0:T(8,128)S(1)}, u32[]{:S(2)}, u32[]{:S(2)}) async-start(f32[8,2,8,256]{3,2,1,0:T(8,128)} %broadcast_in_dim.9), calls=%async_computation.1 | async-start | bytes 262144 | tf_op jit(solution)/shard_map/all_to_all | solution.py:459
  39.4 5.6 %collective-permute-start.5 = (f32[128,256]{1,0:T(8,128)S(1)}, f32[128,256]{1,0:T(8,128)S(1)}, u32[]{:S(2)}, u32[]{:S(2)}) collective-permute-start(f32[128,256]{1,0:T(8,128)S(1)} %get-tuple-element.46), channel_id=1, source_target_pairs={{0,2},{1,3},{8,10},{9,11},{16,18},{17,19},{24,26},{25,27},{32,34},... | collective-permute-start | bytes 393224 | tf_op jit(solution)/shard_map/ppermute | solution.py:32
  42.1 5.7 %collective-permute-start.4 = (f32[128,256]{1,0:T(8,128)S(1)}, f32[128,256]{1,0:T(8,128)S(1)}, u32[]{:S(2)}, u32[]{:S(2)}) collective-permute-start(f32[128,256]{1,0:T(8,128)S(1)} %get-tuple-element.47), channel_id=1, source_target_pairs={{0,4},{1,5},{8,12},{9,13},{16,20},{17,21},{24,28},{25,29},{32,36},... | collective-permute-start | bytes 393224 | tf_op jit(solution)/shard_map/ppermute | solution.py:32
  43.4 8.9 %collective-permute-start.3 = (f32[128,256]{1,0:T(8,128)S(1)}, f32[128,256]{1,0:T(8,128)S(1)}, u32[]{:S(2)}, u32[]{:S(2)}) collective-permute-start(f32[128,256]{1,0:T(8,128)S(1)} %get-tuple-element.48), channel_id=1, source_target_pairs={{0,6},{1,7},{8,14},{9,15},{16,22},{17,23},{24,30},{25,31},{32,38},... | collective-permute-start | bytes 393224 | tf_op jit(solution)/shard_map/ppermute | solution.py:32
  53.1 33.5 %all-to-all-start.2 = ((f32[32,3,8,128]{3,2,1,0:T(8,128)}), f32[32,3,8,128]{3,2,1,0:T(8,128)S(1)}, u32[]{:S(2)}, u32[]{:S(2)}) async-start(f32[32,3,8,128]{3,2,1,0:T(8,128)} %broadcast_in_dim.20), calls=%async_computation.2 | async-start | bytes 786432 | tf_op jit(solution)/shard_map/all_to_all | solution.py:466
  63.4 16.1 %collective-permute-start.8 = (f32[128,256]{1,0:T(8,128)S(1)}, f32[128,256]{1,0:T(8,128)S(1)}, u32[]{:S(2)}, u32[]{:S(2)}) collective-permute-start(f32[128,256]{1,0:T(8,128)S(1)} %fusion.5.refs_0_), channel_id=1, source_target_pairs={{0,6},{1,7},{2,0},{3,1},{4,2},{5,3},{6,4},{7,5},{8,14},{9,15},{10,... | collective-permute-start | bytes 393224 | tf_op jit(solution)/shard_map/ppermute | solution.py:32
  66.8 15.1 %collective-permute-start.7 = (f32[128,256]{1,0:T(8,128)S(1)}, f32[128,256]{1,0:T(8,128)S(1)}, u32[]{:S(2)}, u32[]{:S(2)}) collective-permute-start(f32[128,256]{1,0:T(8,128)S(1)} %fusion.5.refs_0_), channel_id=1, source_target_pairs={{0,4},{1,5},{2,6},{3,7},{4,0},{5,1},{6,2},{7,3},{8,12},{9,13},{10,... | collective-permute-start | bytes 393224 | tf_op jit(solution)/shard_map/ppermute | solution.py:32
  68.9 17.7 %collective-permute-start.6 = (f32[128,256]{1,0:T(8,128)S(1)}, f32[128,256]{1,0:T(8,128)S(1)}, u32[]{:S(2)}, u32[]{:S(2)}) collective-permute-start(f32[128,256]{1,0:T(8,128)S(1)} %fusion.5.refs_0_), channel_id=1, source_target_pairs={{0,2},{1,3},{2,4},{3,5},{4,6},{5,7},{6,0},{7,1},{8,10},{9,11},{10,... | collective-permute-start | bytes 393224 | tf_op jit(solution)/shard_map/ppermute | solution.py:32
  86.6 35.9 %copy-start.2 = (f32[512,256]{1,0:T(8,128)}, f32[512,256]{1,0:T(8,128)S(1)}, u32[]{:S(2)}) copy-start(f32[512,256]{1,0:T(8,128)S(1)} %order.1.a0) | copy-start | bytes 1572868
  86.7 11.0 %copy-start.10 = (f32[32,3,8,128]{3,2,1,0:T(8,128)}, f32[32,3,8,128]{3,2,1,0:T(8,128)S(1)}, u32[]{:S(2)}) copy-start(f32[32,3,8,128]{3,2,1,0:T(8,128)S(1)} %all-to-all-done.2.own_ref) | copy-start | bytes 1179652
  86.7 32.9 %collective-permute-start.14 = (f32[512,256]{1,0:T(8,128)S(1)}, f32[512,256]{1,0:T(8,128)S(1)}, u32[]{:S(2)}, u32[]{:S(2)}) collective-permute-start(f32[512,256]{1,0:T(8,128)S(1)} %order.1.a0), channel_id=1, source_target_pairs={{0,24},{1,25},{2,26},{3,27},{4,28},{5,29},{6,30},{7,31},{8,0},{9,1... | collective-permute-start | bytes 1572872 | tf_op jit(solution)/shard_map/ppermute | solution.py:32
  89.0 30.7 %collective-permute-start.13 = (f32[512,256]{1,0:T(8,128)S(1)}, f32[512,256]{1,0:T(8,128)S(1)}, u32[]{:S(2)}, u32[]{:S(2)}) collective-permute-start(f32[512,256]{1,0:T(8,128)S(1)} %order.1.a0), channel_id=1, source_target_pairs={{0,16},{1,17},{2,18},{3,19},{4,20},{5,21},{6,22},{7,23},{8,24},{9,... | collective-permute-start | bytes 1572872 | tf_op jit(solution)/shard_map/ppermute | solution.py:32
  89.5 30.2 %collective-permute-start.12 = (f32[512,256]{1,0:T(8,128)S(1)}, f32[512,256]{1,0:T(8,128)}, u32[]{:S(2)}, u32[]{:S(2)}) collective-permute-start(f32[512,256]{1,0:T(8,128)S(1)} %order.1.a0), channel_id=1, source_target_pairs={{0,8},{1,9},{2,10},{3,11},{4,12},{5,13},{6,14},{7,15},{8,16},{9,17... | collective-permute-start | bytes 1572872 | tf_op jit(solution)/shard_map/ppermute | solution.py:32
  90.1 5.5 %collective-permute-start.11 = (f32[32,3,8,128]{3,2,1,0:T(8,128)S(1)}, f32[32,3,8,128]{3,2,1,0:T(8,128)S(1)}, u32[]{:S(2)}, u32[]{:S(2)}) collective-permute-start(f32[32,3,8,128]{3,2,1,0:T(8,128)S(1)} %all-to-all-done.2.own_ref), channel_id=1, source_target_pairs={{0,32},{1,33},{2,34},{3,35},{4,36},{5,37},{6,38},{7,39},{8,40},{9,... | collective-permute-start | bytes 1179656 | tf_op jit(solution)/shard_map/ppermute | solution.py:32
  92.7 29.8 %collective-permute-start.10 = (f32[512,256]{1,0:T(8,128)S(1)}, f32[512,256]{1,0:T(8,128)S(1)}, u32[]{:S(2)}, u32[]{:S(2)}) collective-permute-start(f32[512,256]{1,0:T(8,128)S(1)} %order.1.a0), channel_id=1, source_target_pairs={{0,128},{1,129},{2,130},{3,131},{4,132},{5,133},{6,134},{7,135},{8... | collective-permute-start | bytes 1572872 | tf_op jit(solution)/shard_map/ppermute | solution.py:32
  95.5 2.1 %copy-start.14 = (f32[32,3,8,128]{3,2,1,0:T(8,128)}, f32[32,3,8,128]{3,2,1,0:T(8,128)S(1)}, u32[]{:S(2)}) copy-start(f32[32,3,8,128]{3,2,1,0:T(8,128)S(1)} %collective-permute-done.11.other_ref) | copy-start | bytes 1179652
  95.6 27.0 %collective-permute-start.9 = (f32[512,256]{1,0:T(8,128)S(1)}, f32[512,256]{1,0:T(8,128)S(1)}, u32[]{:S(2)}, u32[]{:S(2)}) collective-permute-start(f32[512,256]{1,0:T(8,128)S(1)} %order.1.a0), channel_id=1, source_target_pairs={{0,1},{1,0},{2,3},{3,2},{4,5},{5,4},{6,7},{7,6},{8,9},{9,8},{10,11... | collective-permute-start | bytes 1572872 | tf_op jit(solution)/shard_map/ppermute | solution.py:32
  119.6 0.8 copy-start.12
  119.6 1.0 copy-start.13
  121.7 18.9 %collective-permute-start.16 = (f32[768,256]{1,0:T(8,128)S(1)}, f32[768,256]{1,0:T(8,128)}, u32[]{:S(2)}, u32[]{:S(2)}) collective-permute-start(f32[768,256]{1,0:T(8,128)S(1)} %pad_maximum_fusion.1), channel_id=1, source_target_pairs={{0,1},{1,0},{2,3},{3,2},{4,5},{5,4},{6,7},{7,6},{8,9},{9,8},{10,11... | collective-permute-start | bytes 2359304 | tf_op jit(solution)/shard_map/ppermute | solution.py:32
  122.6 10.1 %copy-start.11 = (f32[512,256]{1,0:T(8,128)}, f32[512,256]{1,0:T(8,128)S(1)}, u32[]{:S(2)}) copy-start(f32[512,256]{1,0:T(8,128)S(1)} %collective-permute-done.9.others_ref) | copy-start | bytes 1572868
  122.6 18.0 %collective-permute-start.15 = (f32[512,256]{1,0:T(8,128)S(1)}, f32[512,256]{1,0:T(8,128)S(1)}, u32[]{:S(2)}, u32[]{:S(2)}) collective-permute-start(f32[512,256]{1,0:T(8,128)S(1)} %broadcast_select_fusion), channel_id=1, source_target_pairs={{0,64},{1,65},{2,66},{3,67},{4,68},{5,69},{6,70},{7,71},{8,72},{9,... | collective-permute-start | bytes 1572872 | tf_op jit(solution)/shard_map/ppermute | solution.py:32
  123.0 9.7 %collective-permute-start.19 = (f32[256,256]{1,0:T(8,128)S(1)}, f32[256,256]{1,0:T(8,128)S(1)}, u32[]{:S(2)}, u32[]{:S(2)}) collective-permute-start(f32[256,256]{1,0:T(8,128)S(1)} %slice.82), channel_id=1, source_target_pairs={{0,24},{1,25},{2,26},{3,27},{4,28},{5,29},{6,30},{7,31},{8,0},{9,1... | collective-permute-start | bytes 786440 | tf_op jit(solution)/shard_map/ppermute | solution.py:32
  125.2 8.2 %collective-permute-start.18 = (f32[256,256]{1,0:T(8,128)S(1)}, f32[256,256]{1,0:T(8,128)S(1)}, u32[]{:S(2)}, u32[]{:S(2)}) collective-permute-start(f32[256,256]{1,0:T(8,128)S(1)} %slice.82), channel_id=1, source_target_pairs={{0,16},{1,17},{2,18},{3,19},{4,20},{5,21},{6,22},{7,23},{8,24},{9,... | collective-permute-start | bytes 786440 | tf_op jit(solution)/shard_map/ppermute | solution.py:32
  126.4 14.2 %collective-permute-start.17 = (f32[256,256]{1,0:T(8,128)S(1)}, f32[256,256]{1,0:T(8,128)}, u32[]{:S(2)}, u32[]{:S(2)}) collective-permute-start(f32[256,256]{1,0:T(8,128)S(1)} %slice.82), channel_id=1, source_target_pairs={{0,8},{1,9},{2,10},{3,11},{4,12},{5,13},{6,14},{7,15},{8,16},{9,17... | collective-permute-start | bytes 786440 | tf_op jit(solution)/shard_map/ppermute | solution.py:32
  132.7 9.1 %copy-start.15 = (f32[256,256]{1,0:T(8,128)}, f32[256,256]{1,0:T(8,128)S(1)}, u32[]{:S(2)}) copy-start(f32[256,256]{1,0:T(8,128)S(1)} %collective-permute-done.19.u3) | copy-start | bytes 786436
  133.4 7.2 %copy-start.16 = (f32[256,256]{1,0:T(8,128)}, f32[256,256]{1,0:T(8,128)S(1)}, u32[]{:S(2)}) copy-start(f32[256,256]{1,0:T(8,128)S(1)} %collective-permute-done.18.u2) | copy-start | bytes 786436
  140.7 12.5 %collective-permute-start.20 = (f32[512,256]{1,0:T(8,128)S(1)}, f32[512,256]{1,0:T(8,128)S(1)}, u32[]{:S(2)}, u32[]{:S(2)}) collective-permute-start(f32[512,256]{1,0:T(8,128)S(1)} %broadcast_select_fusion.1), channel_id=1, source_target_pairs={{0,1},{1,0},{2,3},{3,2},{4,5},{5,4},{6,7},{7,6},{8,9},{9,8},{10,11... | collective-permute-start | bytes 1572872 | tf_op jit(solution)/shard_map/ppermute | solution.py:32
  141.9 16.0 %copy-start.5 = (f32[256,256]{1,0:T(8,128)S(1)}, f32[256,256]{1,0:T(8,128)}, u32[]{:S(2)}) copy-start(f32[256,256]{1,0:T(8,128)} %get-tuple-element.40.l0_ref) | copy-start | bytes 786436
  141.9 16.0 %copy-start.6 = (f32[256,256]{1,0:T(8,128)S(1)}, f32[256,256]{1,0:T(8,128)}, u32[]{:S(2)}) copy-start(f32[256,256]{1,0:T(8,128)} %get-tuple-element.30.w0_ref) | copy-start | bytes 786436
  141.9 16.0 %copy-start.7 = (f32[256,256]{1,0:T(8,128)S(1)}, f32[256,256]{1,0:T(8,128)}, u32[]{:S(2)}) copy-start(f32[256,256]{1,0:T(8,128)} %get-tuple-element.31.p10_ref) | copy-start | bytes 786436
  141.9 16.0 %copy-start.8 = (f32[256,256]{1,0:T(8,128)S(1)}, f32[256,256]{1,0:T(8,128)}, u32[]{:S(2)}) copy-start(f32[256,256]{1,0:T(8,128)} %get-tuple-element.28.l1_ref) | copy-start | bytes 786436
  141.9 16.0 %copy-start.9 = (f32[256,256]{1,0:T(8,128)S(1)}, f32[256,256]{1,0:T(8,128)}, u32[]{:S(2)}) copy-start(f32[256,256]{1,0:T(8,128)} %get-tuple-element.32.w1_ref) | copy-start | bytes 786436
  152.2 5.7 %copy-start.1 = (f32[8,1,256,2,1,256]{5,4,3,2,1,0:T(1,128)S(1)}, f32[8,1,256,2,1,256]{5,4,3,2,1,0:T(1,128)}, u32[]{:S(2)}) copy-start(f32[8,1,256,2,1,256]{5,4,3,2,1,0:T(1,128)} %param.1) | copy-start | bytes 12582916
  152.3 5.7 %copy-start.3 = (s32[5]{0:T(128)S(1)}, s32[5]{0:T(128)}, u32[]{:S(2)}) copy-start(s32[5]{0:T(128)} %stack.48.info_ref) | copy-start | bytes 64
  153.4 4.5 %collective-permute-start.21 = (f32[2,512,256]{2,1,0:T(8,128)S(1)}, f32[2,512,256]{2,1,0:T(8,128)S(1)}, u32[]{:S(2)}, u32[]{:S(2)}) collective-permute-start(f32[2,512,256]{2,1,0:T(8,128)S(1)} %pad_maximum_fusion.own_ref), channel_id=1, source_target_pairs={{0,32},{1,33},{2,34},{3,35},{4,36},{5,37},{6,38},{7,39},{8,40},{9,... | collective-permute-start | bytes 3145736 | tf_op jit(solution)/shard_map/ppermute | solution.py:32
  157.9 2.2 %copy-start.4 = (f32[4,512,512]{2,1,0:T(8,128)S(1)}, f32[4,512,512]{2,1,0:T(8,128)}, u32[]{:S(2)}) copy-start(f32[4,512,512]{2,1,0:T(8,128)} %solve_rows.1.p_ref) | copy-start | bytes 12582916

commit v4 on v3

--- a/solution.py
+++ b/solution.py
@@ -189,19 +189,25 @@
     )(core, own, other)
 
 
-def column_kernel(m_ref, o_ref):
-    for half in range(2):
-        o_ref[0, 0, :, half * 128 : half * 128 + 128] = m_ref[pl.ds(half, N, stride=4), :]
+def column_kernel(m_ref, *o_refs):
+    for d, o_ref in enumerate(o_refs):
+        @pl.when(pl.program_id(0) == d)
+        def _(o_ref=o_ref):
+            for half in range(2):
+                o_ref[0, :, half * 128 : half * 128 + 128] = m_ref[pl.ds(half, N, stride=4), :]
 
 
 def first_column(flat_blocks):
+    out = lambda d: pl.BlockSpec((1, N, N), lambda k, h: (jnp.where(k == d, h, jnp.where(k < d, 0, 1)), 0, 0))
     return pl.pallas_call(
         column_kernel,
-        grid=(8,),
-        out_shape=jax.ShapeDtypeStruct((4, 2, N, N), F32),
-        in_specs=[pl.BlockSpec((4 * N, 128), lambda a: (a, 0))],
-        out_specs=pl.BlockSpec((1, 1, N, N), lambda a: (a % 4, a // 4, 0, 0)),
-        compiler_params=pltpu.CompilerParams(vmem_limit_bytes=16 << 20, dimension_semantics=("arbitrary",)),
+        grid=(4, 2),
+        out_shape=[jax.ShapeDtypeStruct((2, N, N), F32)] * 4,
+        in_specs=[pl.BlockSpec((4 * N, 128), lambda k, h: (k + 4 * h, 0))],
+        out_specs=[out(d) for d in range(4)],
+        compiler_params=pltpu.CompilerParams(
+            vmem_limit_bytes=16 << 20, dimension_semantics=("arbitrary", "arbitrary")
+        ),
         cost_estimate=pl.CostEstimate(flops=0, bytes_accessed=6 << 20, transcendentals=0),
         name="first_column",
     )(flat_blocks)
@@ -443,7 +449,7 @@
         send(column[d], lambda y, c, x, z, d=d: (y, c, d, z) if x == 0 and z < 2 else None) for d in (1, 2, 3)
     ]
 
-    own_rows = lax.all_to_all(column[0, 0].reshape(32, 8, N), "col", 0, 0, tiled=True)[:2]
+    own_rows = lax.all_to_all(column[0][0].reshape(32, 8, N), "col", 0, 0, tiled=True)[:2]
 
     quarter = after(pick(x, [column[0], *arrived]), own_rows)
 
@@ -456,16 +462,17 @@
         for d in (1, 2, 3)
     ]
     piece = pick(z // 2, [parts[0], *sent])
-    tile_rows = lax.all_to_all(jnp.broadcast_to(own_rows[None], (8, 2, 8, N)), "row", 0, 0, tiled=True)
+    tile_rows = after(own_rows, quarter)
+    tile_rows = lax.all_to_all(jnp.broadcast_to(tile_rows[None], (8, 2, 8, N)), "row", 0, 0, tiled=True)
     lead, middle, last = tile_rows[0, 0], tile_rows[1, 0], tile_rows[1, 1]
     whole, part = jnp.where(core == 0, lead, last), jnp.where(core == 0, middle[:4], middle[4:])
     core_rows = jnp.stack([whole[:, :128], whole[:, 128:], jnp.concatenate([part[:, :128], part[:, 128:]], 0)])
+    core_rows = lax.all_to_all(jnp.broadcast_to(core_rows[None], (32, 3, 8, 128)), "col", 0, 0, tiled=True)
     piece, core_rows = lax.optimization_barrier((piece, core_rows))
     pieces = [piece] + [send(piece, lambda y, c, x, z, d=d: (y, c, x, (z + 2 * d) % NZ)) for d in (1, 2, 3)]
     mine = order((z // 2).astype(jnp.int32)[None], pieces)
-    core_rows = lax.all_to_all(jnp.broadcast_to(core_rows[None], (32, 3, 8, 128)), "col", 0, 0, tiled=True)
-    mine, core_rows = lax.optimization_barrier((mine, core_rows))
     other_rows = send(core_rows, lambda y, c, x, z: (y, 1 - c, x, z))
+    mine, other_rows = lax.optimization_barrier((mine, other_rows))
 
     own_quarters = [mine] + [send(mine, lambda y, c, x, z, d=d: (y, c, (x + d) % NX, z)) for d in (1, 2, 3)]
     others = send(mine, lambda y, c, x, z: (y, c, x, z ^ 1))

time: 168 us -> 167 us (level)
  waiting for transfers between devices: 46.8 us -> 50.3 us
  starting transfers between devices: 63.6 us -> 60.5 us
    all_to_all x2, waiting for transfers between devices: 12.5 us -> 20.9 us  [the longest x1 15.7 us: on_device(): lax.all_to_all(column[0][0].reshape(32, 8, N), 'col', 0, 0, tiled=True)[:2]]
    ppermute x22, waiting for transfers between devices: 34.3 us -> 29.4 us  [send(): return lax.ppermute(value, ('row', 'col'), pairs(fn))]
    all_to_all x1, starting transfers between devices: 10.3 us -> 6.73 us  [on_device(): lax.all_to_all(jnp.broadcast_to(core_rows[None], (32, 3, 8, 128)), 'col',...]
    unnamed x34 -> x32, local copies, waits for them, and re-layouts: 5.39 us -> 4.43 us
where the time goes in v4:
time: 167 us; the launch traced here: 166 us
  starting transfers between devices  60.5 us (36%)
  waiting for transfers between devices  50.3 us (30%)
  Pallas kernels  44.6 us (27%)
  local copies, waits for them, and re-layouts  9.36 us (6%)
    ppermute x22, starting transfers between devices, send(): return lax.ppermute(value, ('row', 'col'), pairs(fn))  41.7 us
    ppermute x22, waiting for transfers between devices, send(): return lax.ppermute(value, ('row', 'col'), pairs(fn))  29.4 us
    pallas_call x1, Pallas kernels, factor(): pl.pallas_call(factor_kernel, out_shape=[jax.ShapeDtypeStruct((N, N), F32...  21.9 us
    all_to_all x1, waiting for transfers between devices, on_device(): lax.all_to_all(column[0][0].reshape(32, 8, N), 'col', 0, 0, tiled=True)[:2]  15.7 us
    pallas_call x1, Pallas kernels, solve_rows(): pl.pallas_call(rows_kernel, grid=(4,), in_specs=[pl.BlockSpec(memory_spac...  10.3 us
    all_to_all x1, starting transfers between devices, on_device(): lax.all_to_all(jnp.broadcast_to(core_rows[None], (32, 3, 8, 128)), 'col',...  6.73 us
    pallas_call x1, Pallas kernels, update(): pl.pallas_call(update_kernel, grid_spec=pltpu.PrefetchScalarGridSpec(num_...  6.22 us
    all_to_all x1, starting transfers between devices, on_device(): lax.all_to_all(column[0][0].reshape(32, 8, N), 'col', 0, 0, tiled=True)[:2]  6.06 us
  transfers between devices with their start and end apart: 25, of which 11 were waited for; matrix products, arithmetic and copies ran while one was open for 2% of the time, Pallas kernels for 23%

profile of v4, /device:TPU:1, one launch (start us, length us, event | category | flops | bytes accessed | tf_op | source)
XLA Modules:
  0.0 165.9 jit_solution(11199407198145800592)
XLA Ops:
  0.0 2.2 %copy-done = f32[8,1,256,2,1,256]{5,4,3,2,1,0:T(1,128)S(1)} copy-done((f32[8,1,256,2,1,256]{5,4,3,2,1,0:T(1,128)S(1)}, f32[8,1,256,2,1,256]{5,4,3,2,1,0:T(1,128)}, u32[]{:S(2)}) %copy-start) | copy-done | bytes 4194328
  2.2 0.4 first_column.1
  2.6 5.2 %collective-permute-start = (f32[2,256,256]{2,1,0:T(8,128)S(1)}, f32[2,256,256]{2,1,0:T(8,128)S(1)}, u32[]{:S(2)}, u32[]{:S(2)}) collective-permute-start(f32[2,256,256]{2,1,0:T(8,128)S(1)} %get-tuple-element.28), channel_id=1, source_target_pairs={{0,24},{1,25},{32,56},{33,57},{64,88},{65,89},{96,120},{97,121},{1... | collective-permute-start | bytes 1572872 | tf_op jit(solution)/shard_map/ppermute | solution.py:32
  7.9 1.3 collective-permute-start.1
  9.2 2.1 %collective-permute-start.2 = (f32[2,256,256]{2,1,0:T(8,128)S(1)}, f32[2,256,256]{2,1,0:T(8,128)}, u32[]{:S(2)}, u32[]{:S(2)}) collective-permute-start(f32[2,256,256]{2,1,0:T(8,128)S(1)} %get-tuple-element.30), channel_id=1, source_target_pairs={{0,8},{1,9},{32,40},{33,41},{64,72},{65,73},{96,104},{97,105},{128... | collective-permute-start | bytes 1572872 | tf_op jit(solution)/shard_map/ppermute | solution.py:32
  11.3 0.7 slice_bitcast_fusion
  12.0 6.1 %all-to-all-start = ((f32[32,8,256]{2,1,0:T(8,128)}), f32[32,8,256]{2,1,0:T(8,128)S(1)}, u32[]{:S(2)}, u32[]{:S(2)}) async-start(f32[32,8,256]{2,1,0:T(8,128)} %slice_bitcast_fusion), calls=%async_computation | async-start | bytes 524288 | tf_op jit(solution)/shard_map/all_to_all | solution.py:452
  18.1 15.7 %all-to-all-done = f32[32,8,256]{2,1,0:T(8,128)S(1)} async-done(((f32[32,8,256]{2,1,0:T(8,128)}), f32[32,8,256]{2,1,0:T(8,128)S(1)}, u32[]{:S(2)}, u32[]{:S(2)}) %all-to-all-start) | async-done | bytes 262176 | tf_op jit(solution)/shard_map/all_to_all | solution.py:452
  33.8 0.1 select_select_fusion
  34.0 0.7 broadcast_in_dim.9
  34.6 6.0 %all-to-all-start.1 = ((f32[8,2,8,256]{3,2,1,0:T(8,128)}), f32[8,2,8,256]{3,2,1,0:T(8,128)S(1)}, u32[]{:S(2)}, u32[]{:S(2)}) async-start(f32[8,2,8,256]{3,2,1,0:T(8,128)} %broadcast_in_dim.9), calls=%async_computation.1 | async-start | bytes 262144 | tf_op jit(solution)/shard_map/all_to_all | solution.py:466
  40.6 5.3 %all-to-all-done.1 = f32[8,2,8,256]{3,2,1,0:T(8,128)S(1)} async-done(((f32[8,2,8,256]{3,2,1,0:T(8,128)}), f32[8,2,8,256]{3,2,1,0:T(8,128)S(1)}, u32[]{:S(2)}, u32[]{:S(2)}) %all-to-all-start.1) | async-done | bytes 131104 | tf_op jit(solution)/shard_map/all_to_all | solution.py:466
  45.9 0.8 broadcast_in_dim.20
  46.7 6.7 %all-to-all-start.2 = ((f32[32,3,8,128]{3,2,1,0:T(8,128)}), f32[32,3,8,128]{3,2,1,0:T(8,128)S(1)}, u32[]{:S(2)}, u32[]{:S(2)}) async-start(f32[32,3,8,128]{3,2,1,0:T(8,128)} %broadcast_in_dim.20), calls=%async_computation.2 | async-start | bytes 786432 | tf_op jit(solution)/shard_map/all_to_all | solution.py:470
  53.6 4.0 %collective-permute-start.5 = (f32[128,256]{1,0:T(8,128)S(1)}, f32[128,256]{1,0:T(8,128)S(1)}, u32[]{:S(2)}, u32[]{:S(2)}) collective-permute-start(f32[128,256]{1,0:T(8,128)S(1)} %get-tuple-element.53), channel_id=1, source_target_pairs={{0,2},{1,3},{8,10},{9,11},{16,18},{17,19},{24,26},{25,27},{32,34},... | collective-permute-start | bytes 393224 | tf_op jit(solution)/shard_map/ppermute | solution.py:32
  57.6 3.7 %collective-permute-start.4 = (f32[128,256]{1,0:T(8,128)S(1)}, f32[128,256]{1,0:T(8,128)S(1)}, u32[]{:S(2)}, u32[]{:S(2)}) collective-permute-start(f32[128,256]{1,0:T(8,128)S(1)} %get-tuple-element.54), channel_id=1, source_target_pairs={{0,4},{1,5},{8,12},{9,13},{16,20},{17,21},{24,28},{25,29},{32,36},... | collective-permute-start | bytes 393224 | tf_op jit(solution)/shard_map/ppermute | solution.py:32
  61.3 1.3 collective-permute-start.3
  62.6 0.8 collective-permute-done.5
  63.4 3.2 %collective-permute-done.4 = f32[128,256]{1,0:T(8,128)S(1)} collective-permute-done((f32[128,256]{1,0:T(8,128)S(1)}, f32[128,256]{1,0:T(8,128)S(1)}, u32[]{:S(2)}, u32[]{:S(2)}) %collective-permute-start.4) | collective-permute-done | bytes 131104 | tf_op jit(solution)/shard_map/ppermute | solution.py:32
  66.6 5.0 %collective-permute-done.3 = f32[128,256]{1,0:T(8,128)S(1)} collective-permute-done((f32[128,256]{1,0:T(8,128)S(1)}, f32[128,256]{1,0:T(8,128)S(1)}, u32[]{:S(2)}, u32[]{:S(2)}) %collective-permute-start.3) | collective-permute-done | bytes 131104 | tf_op jit(solution)/shard_map/ppermute | solution.py:32
  71.7 0.6 collective-permute-start.9
  72.3 4.4 %collective-permute-start.8 = (f32[128,256]{1,0:T(8,128)S(1)}, f32[128,256]{1,0:T(8,128)S(1)}, u32[]{:S(2)}, u32[]{:S(2)}) collective-permute-start(f32[128,256]{1,0:T(8,128)S(1)} %fusion.2.refs_0_), channel_id=1, source_target_pairs={{0,6},{1,7},{2,0},{3,1},{4,2},{5,3},{6,4},{7,5},{8,14},{9,15},{10,... | collective-permute-start | bytes 393224 | tf_op jit(solution)/shard_map/ppermute | solution.py:32
  76.7 2.1 %collective-permute-start.6 = (f32[128,256]{1,0:T(8,128)S(1)}, f32[128,256]{1,0:T(8,128)S(1)}, u32[]{:S(2)}, u32[]{:S(2)}) collective-permute-start(f32[128,256]{1,0:T(8,128)S(1)} %fusion.2.refs_0_), channel_id=1, source_target_pairs={{0,2},{1,3},{2,4},{3,5},{4,6},{5,7},{6,0},{7,1},{8,10},{9,11},{10,... | collective-permute-start | bytes 393224 | tf_op jit(solution)/shard_map/ppermute | solution.py:32
  78.7 8.6 %collective-permute-done.8.refs_3_ = f32[128,256]{1,0:T(8,128)S(1)} collective-permute-done((f32[128,256]{1,0:T(8,128)S(1)}, f32[128,256]{1,0:T(8,128)S(1)}, u32[]{:S(2)}, u32[]{:S(2)}) %collective-permute-start.8) | collective-permute-done | bytes 131104 | tf_op jit(solution)/shard_map/ppermute | solution.py:32
  87.4 1.8 %collective-permute-done.6.refs_1_ = f32[128,256]{1,0:T(8,128)S(1)} collective-permute-done((f32[128,256]{1,0:T(8,128)S(1)}, f32[128,256]{1,0:T(8,128)S(1)}, u32[]{:S(2)}, u32[]{:S(2)}) %collective-permute-start.6) | collective-permute-done | bytes 131104 | tf_op jit(solution)/shard_map/ppermute | solution.py:32
  89.2 2.2 %collective-permute-start.14 = (f32[512,256]{1,0:T(8,128)S(1)}, f32[512,256]{1,0:T(8,128)S(1)}, u32[]{:S(2)}, u32[]{:S(2)}) collective-permute-start(f32[512,256]{1,0:T(8,128)S(1)} %order.1.a0), channel_id=1, source_target_pairs={{0,24},{1,25},{2,26},{3,27},{4,28},{5,29},{6,30},{7,31},{8,0},{9,1... | collective-permute-start | bytes 1572872 | tf_op jit(solution)/shard_map/ppermute | solution.py:32
  91.5 0.5 collective-permute-start.13
  92.0 0.6 collective-permute-start.12
  92.6 0.8 collective-permute-start.11
  93.3 3.6 %collective-permute-start.10 = (f32[512,256]{1,0:T(8,128)S(1)}, f32[512,256]{1,0:T(8,128)S(1)}, u32[]{:S(2)}, u32[]{:S(2)}) collective-permute-start(f32[512,256]{1,0:T(8,128)S(1)} %order.1.a0), channel_id=1, source_target_pairs={{0,1},{1,0},{2,3},{3,2},{4,5},{5,4},{6,7},{7,6},{8,9},{9,8},{10,11... | collective-permute-start | bytes 1572872 | tf_op jit(solution)/shard_map/ppermute | solution.py:32
  97.0 21.9 %factor.1 = (f32[256,256]{1,0:T(8,128)}, f32[256,256]{1,0:T(8,128)}, f32[256,256]{1,0:T(8,128)}, f32[256,256]{1,0:T(8,128)}, f32[256,256]{1,0:T(8,128)}) custom-call(s32[1]{0:T(128)} %bitcast.19.core_ref, f32[32,3,8,128]{3,2,1,0:T(8,128)} %copy-done.10, f32[32,3,8,128]{3,2,1,0:T(8,128)} %copy-done.13), custom_call_target="tpu_custom_call" | custom-call | flops 1000000000 | bytes 62914560 | tf_op jit(solution)/shard_map/factor/pallas_call | solution.py:180
  119.0 1.1 slice.78
  120.1 1.0 slice.77
  121.1 1.7 %collective-permute-start.16 = (f32[768,256]{1,0:T(8,128)S(1)}, f32[768,256]{1,0:T(8,128)}, u32[]{:S(2)}, u32[]{:S(2)}) collective-permute-start(f32[768,256]{1,0:T(8,128)S(1)} %pad_maximum_fusion.1), channel_id=1, source_target_pairs={{0,1},{1,0},{2,3},{3,2},{4,5},{5,4},{6,7},{7,6},{8,9},{9,8},{10,11... | collective-permute-start | bytes 2359304 | tf_op jit(solution)/shard_map/ppermute | solution.py:32
  123.0 0.4 collective-permute-start.15
  123.4 1.0 collective-permute-start.19
  124.3 1.2 collective-permute-start.18
  125.6 0.6 stack.48.info_ref
  126.2 5.7 %solve_own.1 = (f32[4,512,256]{2,1,0:T(8,128)}, f32[256,256]{1,0:T(8,128)}) custom-call(s32[5]{0:T(128)} %stack.48.info_ref, f32[256,256]{1,0:T(8,128)} %get-tuple-element.40.w0_ref, f32[256,256]{1,0:T(8,128)} %get-tuple-element.41.p10_ref, f32[256,256]{1,0:T(8,128)} %get-tuple-element.42.w1_ref, f32[512,256]{1,0:T(8,128)} %copy-done.2, ...), custom_call_target="tpu_custom_call" | custom-call | flops 2000000000 | bytes 62914560 | tf_op jit(solution)/shard_map/solve_own/pallas_call | solution.py:281
  131.9 6.8 %collective-permute-done.17.u1 = f32[256,256]{1,0:T(8,128)} collective-permute-done((f32[256,256]{1,0:T(8,128)S(1)}, f32[256,256]{1,0:T(8,128)}, u32[]{:S(2)}, u32[]{:S(2)}) %collective-permute-start.17) | collective-permute-done | bytes 262176 | tf_op jit(solution)/shard_map/ppermute | solution.py:32
  138.6 0.7 collective-permute-done.16.lower_ref
  139.4 2.6 %collective-permute-start.20 = (f32[512,256]{1,0:T(8,128)S(1)}, f32[512,256]{1,0:T(8,128)S(1)}, u32[]{:S(2)}, u32[]{:S(2)}) collective-permute-start(f32[512,256]{1,0:T(8,128)S(1)} %broadcast_select_fusion.1), channel_id=1, source_target_pairs={{0,1},{1,0},{2,3},{3,2},{4,5},{5,4},{6,7},{7,6},{8,9},{9,8},{10,11... | collective-permute-start | bytes 1572872 | tf_op jit(solution)/shard_map/ppermute | solution.py:32
  142.0 10.3 %solve_rows.1.p_ref = f32[4,512,512]{2,1,0:T(8,128)} custom-call(s32[5]{0:T(128)} %stack.48.info_ref, f32[256,256]{1,0:T(8,128)} %get-tuple-element.40.w0_ref, f32[256,256]{1,0:T(8,128)} %get-tuple-element.42.w1_ref, f32[256,256]{1,0:T(8,128)} %get-tuple-element.47.turned_ref, f32[4,512,256]{2,1,0:T(8,128)} %get-tuple-element.43.part_ref, ...), custom_call_target="tpu_custom_call" | custom-call | flops 5000000000 | bytes 9437184 | tf_op jit(solution)/shard_map/solve_rows/pallas_call | solution.py:319
  152.4 0.2 collective-permute-done.20
  152.8 2.4 %collective-permute-start.21 = (f32[2,512,256]{2,1,0:T(8,128)S(1)}, f32[2,512,256]{2,1,0:T(8,128)S(1)}, u32[]{:S(2)}, u32[]{:S(2)}) collective-permute-start(f32[2,512,256]{2,1,0:T(8,128)S(1)} %pad_maximum_fusion.own_ref), channel_id=1, source_target_pairs={{0,32},{1,33},{2,34},{3,35},{4,36},{5,37},{6,38},{7,39},{8,40},{9,... | collective-permute-start | bytes 3145736 | tf_op jit(solution)/shard_map/ppermute | solution.py:32
  155.1 2.3 %collective-permute-done.21.other_ref = f32[2,512,256]{2,1,0:T(8,128)S(1)} collective-permute-done((f32[2,512,256]{2,1,0:T(8,128)S(1)}, f32[2,512,256]{2,1,0:T(8,128)S(1)}, u32[]{:S(2)}, u32[]{:S(2)}) %collective-permute-start.21) | collective-permute-done | bytes 1048608 | tf_op jit(solution)/shard_map/ppermute | solution.py:32
  157.5 2.2 %copy-done.4 = f32[4,512,512]{2,1,0:T(8,128)S(1)} copy-done((f32[4,512,512]{2,1,0:T(8,128)S(1)}, f32[4,512,512]{2,1,0:T(8,128)}, u32[]{:S(2)}) %copy-start.4) | copy-done | bytes 4194328
  159.6 6.2 %update.1 = f32[2,4096,128]{2,1,0:T(8,128)} custom-call(s32[5]{0:T(128)S(1)} %copy-done.3, f32[2,4096,128]{2,1,0:T(8,128)S(1)} %bitcast.42, f32[4,512,512]{2,1,0:T(8,128)S(1)} %copy-done.4, f32[2,512,256]{2,1,0:T(8,128)S(1)} %pad_maximum_fusion.own_ref, f32[2,512,256]{2,1,0:T(8,128)S(1)} %collective-permute-done.21.other_ref, f32[256,256]{1,0:T(8,128)S(1)} %copy-done.5, ...), custom_call_target="tpu_custom_call" | custom-call | flops 5000000000 | bytes 16777216 | tf_op jit(solution)/shard_map/update/pallas_call | solution.py:411
  (62 shorter events, 0.6 us)
Async XLA Ops:
  0.0 2.2 %copy-start = (f32[8,1,256,2,1,256]{5,4,3,2,1,0:T(1,128)S(1)}, f32[8,1,256,2,1,256]{5,4,3,2,1,0:T(1,128)}, u32[]{:S(2)}) copy-start(f32[8,1,256,2,1,256]{5,4,3,2,1,0:T(1,128)} %param.1) | copy-start | bytes 12582916
  2.6 31.2 %collective-permute-start = (f32[2,256,256]{2,1,0:T(8,128)S(1)}, f32[2,256,256]{2,1,0:T(8,128)S(1)}, u32[]{:S(2)}, u32[]{:S(2)}) collective-permute-start(f32[2,256,256]{2,1,0:T(8,128)S(1)} %get-tuple-element.28), channel_id=1, source_target_pairs={{0,24},{1,25},{32,56},{33,57},{64,88},{65,89},{96,120},{97,121},{1... | collective-permute-start | bytes 1572872 | tf_op jit(solution)/shard_map/ppermute | solution.py:32
  7.9 25.9 %collective-permute-start.1 = (f32[2,256,256]{2,1,0:T(8,128)S(1)}, f32[2,256,256]{2,1,0:T(8,128)S(1)}, u32[]{:S(2)}, u32[]{:S(2)}) collective-permute-start(f32[2,256,256]{2,1,0:T(8,128)S(1)} %get-tuple-element.29), channel_id=1, source_target_pairs={{0,16},{1,17},{32,48},{33,49},{64,80},{65,81},{96,112},{97,113},{1... | collective-permute-start | bytes 1572872 | tf_op jit(solution)/shard_map/ppermute | solution.py:32
  9.2 24.6 %collective-permute-start.2 = (f32[2,256,256]{2,1,0:T(8,128)S(1)}, f32[2,256,256]{2,1,0:T(8,128)}, u32[]{:S(2)}, u32[]{:S(2)}) collective-permute-start(f32[2,256,256]{2,1,0:T(8,128)S(1)} %get-tuple-element.30), channel_id=1, source_target_pairs={{0,8},{1,9},{32,40},{33,41},{64,72},{65,73},{96,104},{97,105},{128... | collective-permute-start | bytes 1572872 | tf_op jit(solution)/shard_map/ppermute | solution.py:32
  12.0 21.8 %all-to-all-start = ((f32[32,8,256]{2,1,0:T(8,128)}), f32[32,8,256]{2,1,0:T(8,128)S(1)}, u32[]{:S(2)}, u32[]{:S(2)}) async-start(f32[32,8,256]{2,1,0:T(8,128)} %slice_bitcast_fusion), calls=%async_computation | async-start | bytes 524288 | tf_op jit(solution)/shard_map/all_to_all | solution.py:452
  34.6 11.3 %all-to-all-start.1 = ((f32[8,2,8,256]{3,2,1,0:T(8,128)}), f32[8,2,8,256]{3,2,1,0:T(8,128)S(1)}, u32[]{:S(2)}, u32[]{:S(2)}) async-start(f32[8,2,8,256]{3,2,1,0:T(8,128)} %broadcast_in_dim.9), calls=%async_computation.1 | async-start | bytes 262144 | tf_op jit(solution)/shard_map/all_to_all | solution.py:466
  46.7 24.9 %all-to-all-start.2 = ((f32[32,3,8,128]{3,2,1,0:T(8,128)}), f32[32,3,8,128]{3,2,1,0:T(8,128)S(1)}, u32[]{:S(2)}, u32[]{:S(2)}) async-start(f32[32,3,8,128]{3,2,1,0:T(8,128)} %broadcast_in_dim.20), calls=%async_computation.2 | async-start | bytes 786432 | tf_op jit(solution)/shard_map/all_to_all | solution.py:470
  53.6 9.8 %collective-permute-start.5 = (f32[128,256]{1,0:T(8,128)S(1)}, f32[128,256]{1,0:T(8,128)S(1)}, u32[]{:S(2)}, u32[]{:S(2)}) collective-permute-start(f32[128,256]{1,0:T(8,128)S(1)} %get-tuple-element.53), channel_id=1, source_target_pairs={{0,2},{1,3},{8,10},{9,11},{16,18},{17,19},{24,26},{25,27},{32,34},... | collective-permute-start | bytes 393224 | tf_op jit(solution)/shard_map/ppermute | solution.py:32
  57.6 9.0 %collective-permute-start.4 = (f32[128,256]{1,0:T(8,128)S(1)}, f32[128,256]{1,0:T(8,128)S(1)}, u32[]{:S(2)}, u32[]{:S(2)}) collective-permute-start(f32[128,256]{1,0:T(8,128)S(1)} %get-tuple-element.54), channel_id=1, source_target_pairs={{0,4},{1,5},{8,12},{9,13},{16,20},{17,21},{24,28},{25,29},{32,36},... | collective-permute-start | bytes 393224 | tf_op jit(solution)/shard_map/ppermute | solution.py:32
  61.3 10.3 %collective-permute-start.3 = (f32[128,256]{1,0:T(8,128)S(1)}, f32[128,256]{1,0:T(8,128)S(1)}, u32[]{:S(2)}, u32[]{:S(2)}) collective-permute-start(f32[128,256]{1,0:T(8,128)S(1)} %get-tuple-element.55), channel_id=1, source_target_pairs={{0,6},{1,7},{8,14},{9,15},{16,22},{17,23},{24,30},{25,31},{32,38},... | collective-permute-start | bytes 393224 | tf_op jit(solution)/shard_map/ppermute | solution.py:32
  71.6 25.3 %copy-start.10 = (f32[32,3,8,128]{3,2,1,0:T(8,128)}, f32[32,3,8,128]{3,2,1,0:T(8,128)S(1)}, u32[]{:S(2)}) copy-start(f32[32,3,8,128]{3,2,1,0:T(8,128)S(1)} %all-to-all-done.2.own_ref) | copy-start | bytes 1179652
  71.7 17.6 %collective-permute-start.9 = (f32[32,3,8,128]{3,2,1,0:T(8,128)S(1)}, f32[32,3,8,128]{3,2,1,0:T(8,128)S(1)}, u32[]{:S(2)}, u32[]{:S(2)}) collective-permute-start(f32[32,3,8,128]{3,2,1,0:T(8,128)S(1)} %all-to-all-done.2.own_ref), channel_id=1, source_target_pairs={{0,32},{1,33},{2,34},{3,35},{4,36},{5,37},{6,38},{7,39},{8,40},{9,... | collective-permute-start | bytes 1179656 | tf_op jit(solution)/shard_map/ppermute | solution.py:32
  72.3 15.1 %collective-permute-start.8 = (f32[128,256]{1,0:T(8,128)S(1)}, f32[128,256]{1,0:T(8,128)S(1)}, u32[]{:S(2)}, u32[]{:S(2)}) collective-permute-start(f32[128,256]{1,0:T(8,128)S(1)} %fusion.2.refs_0_), channel_id=1, source_target_pairs={{0,6},{1,7},{2,0},{3,1},{4,2},{5,3},{6,4},{7,5},{8,14},{9,15},{10,... | collective-permute-start | bytes 393224 | tf_op jit(solution)/shard_map/ppermute | solution.py:32
  76.6 10.7 %collective-permute-start.7 = (f32[128,256]{1,0:T(8,128)S(1)}, f32[128,256]{1,0:T(8,128)S(1)}, u32[]{:S(2)}, u32[]{:S(2)}) collective-permute-start(f32[128,256]{1,0:T(8,128)S(1)} %fusion.2.refs_0_), channel_id=1, source_target_pairs={{0,4},{1,5},{2,6},{3,7},{4,0},{5,1},{6,2},{7,3},{8,12},{9,13},{10,... | collective-permute-start | bytes 393224 | tf_op jit(solution)/shard_map/ppermute | solution.py:32
  76.7 12.5 %collective-permute-start.6 = (f32[128,256]{1,0:T(8,128)S(1)}, f32[128,256]{1,0:T(8,128)S(1)}, u32[]{:S(2)}, u32[]{:S(2)}) collective-permute-start(f32[128,256]{1,0:T(8,128)S(1)} %fusion.2.refs_0_), channel_id=1, source_target_pairs={{0,2},{1,3},{2,4},{3,5},{4,6},{5,7},{6,0},{7,1},{8,10},{9,11},{10,... | collective-permute-start | bytes 393224 | tf_op jit(solution)/shard_map/ppermute | solution.py:32
  89.2 33.8 %copy-start.2 = (f32[512,256]{1,0:T(8,128)}, f32[512,256]{1,0:T(8,128)S(1)}, u32[]{:S(2)}) copy-start(f32[512,256]{1,0:T(8,128)S(1)} %order.1.a0) | copy-start | bytes 1572868
  89.2 7.7 %copy-start.13 = (f32[32,3,8,128]{3,2,1,0:T(8,128)}, f32[32,3,8,128]{3,2,1,0:T(8,128)S(1)}, u32[]{:S(2)}) copy-start(f32[32,3,8,128]{3,2,1,0:T(8,128)S(1)} %collective-permute-done.9.other_ref) | copy-start | bytes 1179652
  89.2 29.7 %collective-permute-start.14 = (f32[512,256]{1,0:T(8,128)S(1)}, f32[512,256]{1,0:T(8,128)S(1)}, u32[]{:S(2)}, u32[]{:S(2)}) collective-permute-start(f32[512,256]{1,0:T(8,128)S(1)} %order.1.a0), channel_id=1, source_target_pairs={{0,24},{1,25},{2,26},{3,27},{4,28},{5,29},{6,30},{7,31},{8,0},{9,1... | collective-permute-start | bytes 1572872 | tf_op jit(solution)/shard_map/ppermute | solution.py:32
  91.5 27.5 %collective-permute-start.13 = (f32[512,256]{1,0:T(8,128)S(1)}, f32[512,256]{1,0:T(8,128)}, u32[]{:S(2)}, u32[]{:S(2)}) collective-permute-start(f32[512,256]{1,0:T(8,128)S(1)} %order.1.a0), channel_id=1, source_target_pairs={{0,16},{1,17},{2,18},{3,19},{4,20},{5,21},{6,22},{7,23},{8,24},{9,... | collective-permute-start | bytes 1572872 | tf_op jit(solution)/shard_map/ppermute | solution.py:32
  92.0 28.1 %collective-permute-start.12 = (f32[512,256]{1,0:T(8,128)S(1)}, f32[512,256]{1,0:T(8,128)}, u32[]{:S(2)}, u32[]{:S(2)}) collective-permute-start(f32[512,256]{1,0:T(8,128)S(1)} %order.1.a0), channel_id=1, source_target_pairs={{0,8},{1,9},{2,10},{3,11},{4,12},{5,13},{6,14},{7,15},{8,16},{9,17... | collective-permute-start | bytes 1572872 | tf_op jit(solution)/shard_map/ppermute | solution.py:32
  92.6 30.3 %collective-permute-start.11 = (f32[512,256]{1,0:T(8,128)S(1)}, f32[512,256]{1,0:T(8,128)S(1)}, u32[]{:S(2)}, u32[]{:S(2)}) collective-permute-start(f32[512,256]{1,0:T(8,128)S(1)} %order.1.a0), channel_id=1, source_target_pairs={{0,128},{1,129},{2,130},{3,131},{4,132},{5,133},{6,134},{7,135},{8... | collective-permute-start | bytes 1572872 | tf_op jit(solution)/shard_map/ppermute | solution.py:32
  93.3 29.6 %collective-permute-start.10 = (f32[512,256]{1,0:T(8,128)S(1)}, f32[512,256]{1,0:T(8,128)S(1)}, u32[]{:S(2)}, u32[]{:S(2)}) collective-permute-start(f32[512,256]{1,0:T(8,128)S(1)} %order.1.a0), channel_id=1, source_target_pairs={{0,1},{1,0},{2,3},{3,2},{4,5},{5,4},{6,7},{7,6},{8,9},{9,8},{10,11... | collective-permute-start | bytes 1572872 | tf_op jit(solution)/shard_map/ppermute | solution.py:32
  118.9 1.2 copy-start.12
  121.1 18.2 %collective-permute-start.16 = (f32[768,256]{1,0:T(8,128)S(1)}, f32[768,256]{1,0:T(8,128)}, u32[]{:S(2)}, u32[]{:S(2)}) collective-permute-start(f32[768,256]{1,0:T(8,128)S(1)} %pad_maximum_fusion.1), channel_id=1, source_target_pairs={{0,1},{1,0},{2,3},{3,2},{4,5},{5,4},{6,7},{7,6},{8,9},{9,8},{10,11... | collective-permute-start | bytes 2359304 | tf_op jit(solution)/shard_map/ppermute | solution.py:32
  123.0 16.4 %copy-start.11 = (f32[512,256]{1,0:T(8,128)}, f32[512,256]{1,0:T(8,128)S(1)}, u32[]{:S(2)}) copy-start(f32[512,256]{1,0:T(8,128)S(1)} %collective-permute-done.10.others_ref) | copy-start | bytes 1572868
  123.0 15.7 %collective-permute-start.15 = (f32[512,256]{1,0:T(8,128)S(1)}, f32[512,256]{1,0:T(8,128)S(1)}, u32[]{:S(2)}, u32[]{:S(2)}) collective-permute-start(f32[512,256]{1,0:T(8,128)S(1)} %broadcast_select_fusion), channel_id=1, source_target_pairs={{0,64},{1,65},{2,66},{3,67},{4,68},{5,69},{6,70},{7,71},{8,72},{9,... | collective-permute-start | bytes 1572872 | tf_op jit(solution)/shard_map/ppermute | solution.py:32
  123.4 8.5 %collective-permute-start.19 = (f32[256,256]{1,0:T(8,128)S(1)}, f32[256,256]{1,0:T(8,128)S(1)}, u32[]{:S(2)}, u32[]{:S(2)}) collective-permute-start(f32[256,256]{1,0:T(8,128)S(1)} %slice.66), channel_id=1, source_target_pairs={{0,24},{1,25},{2,26},{3,27},{4,28},{5,29},{6,30},{7,31},{8,0},{9,1... | collective-permute-start | bytes 786440 | tf_op jit(solution)/shard_map/ppermute | solution.py:32
  124.3 7.5 %collective-permute-start.18 = (f32[256,256]{1,0:T(8,128)S(1)}, f32[256,256]{1,0:T(8,128)S(1)}, u32[]{:S(2)}, u32[]{:S(2)}) collective-permute-start(f32[256,256]{1,0:T(8,128)S(1)} %slice.66), channel_id=1, source_target_pairs={{0,16},{1,17},{2,18},{3,19},{4,20},{5,21},{6,22},{7,23},{8,24},{9,... | collective-permute-start | bytes 786440 | tf_op jit(solution)/shard_map/ppermute | solution.py:32
  125.6 13.1 %collective-permute-start.17 = (f32[256,256]{1,0:T(8,128)S(1)}, f32[256,256]{1,0:T(8,128)}, u32[]{:S(2)}, u32[]{:S(2)}) collective-permute-start(f32[256,256]{1,0:T(8,128)S(1)} %slice.66), channel_id=1, source_target_pairs={{0,8},{1,9},{2,10},{3,11},{4,12},{5,13},{6,14},{7,15},{8,16},{9,17... | collective-permute-start | bytes 786440 | tf_op jit(solution)/shard_map/ppermute | solution.py:32
  131.8 10.2 %copy-start.14 = (f32[256,256]{1,0:T(8,128)}, f32[256,256]{1,0:T(8,128)S(1)}, u32[]{:S(2)}) copy-start(f32[256,256]{1,0:T(8,128)S(1)} %collective-permute-done.19.u3) | copy-start | bytes 786436
  131.9 7.4 %copy-start.15 = (f32[256,256]{1,0:T(8,128)}, f32[256,256]{1,0:T(8,128)S(1)}, u32[]{:S(2)}) copy-start(f32[256,256]{1,0:T(8,128)S(1)} %collective-permute-done.18.u2) | copy-start | bytes 786436
  139.4 13.2 %collective-permute-start.20 = (f32[512,256]{1,0:T(8,128)S(1)}, f32[512,256]{1,0:T(8,128)S(1)}, u32[]{:S(2)}, u32[]{:S(2)}) collective-permute-start(f32[512,256]{1,0:T(8,128)S(1)} %broadcast_select_fusion.1), channel_id=1, source_target_pairs={{0,1},{1,0},{2,3},{3,2},{4,5},{5,4},{6,7},{7,6},{8,9},{9,8},{10,11... | collective-permute-start | bytes 1572872 | tf_op jit(solution)/shard_map/ppermute | solution.py:32
  142.0 15.4 %copy-start.5 = (f32[256,256]{1,0:T(8,128)S(1)}, f32[256,256]{1,0:T(8,128)}, u32[]{:S(2)}) copy-start(f32[256,256]{1,0:T(8,128)} %get-tuple-element.50.l0_ref) | copy-start | bytes 786436
  142.0 15.4 %copy-start.6 = (f32[256,256]{1,0:T(8,128)S(1)}, f32[256,256]{1,0:T(8,128)}, u32[]{:S(2)}) copy-start(f32[256,256]{1,0:T(8,128)} %get-tuple-element.40.w0_ref) | copy-start | bytes 786436
  142.0 15.4 %copy-start.7 = (f32[256,256]{1,0:T(8,128)S(1)}, f32[256,256]{1,0:T(8,128)}, u32[]{:S(2)}) copy-start(f32[256,256]{1,0:T(8,128)} %get-tuple-element.41.p10_ref) | copy-start | bytes 786436
  142.0 15.4 %copy-start.8 = (f32[256,256]{1,0:T(8,128)S(1)}, f32[256,256]{1,0:T(8,128)}, u32[]{:S(2)}) copy-start(f32[256,256]{1,0:T(8,128)} %get-tuple-element.38.l1_ref) | copy-start | bytes 786436
  142.0 15.4 %copy-start.9 = (f32[256,256]{1,0:T(8,128)S(1)}, f32[256,256]{1,0:T(8,128)}, u32[]{:S(2)}) copy-start(f32[256,256]{1,0:T(8,128)} %get-tuple-element.42.w1_ref) | copy-start | bytes 786436
  152.4 5.1 %copy-start.1 = (f32[8,1,256,2,1,256]{5,4,3,2,1,0:T(1,128)S(1)}, f32[8,1,256,2,1,256]{5,4,3,2,1,0:T(1,128)}, u32[]{:S(2)}) copy-start(f32[8,1,256,2,1,256]{5,4,3,2,1,0:T(1,128)} %param.1) | copy-start | bytes 12582916
  152.4 5.1 %copy-start.3 = (s32[5]{0:T(128)S(1)}, s32[5]{0:T(128)}, u32[]{:S(2)}) copy-start(s32[5]{0:T(128)} %stack.48.info_ref) | copy-start | bytes 64
  152.8 4.6 %collective-permute-start.21 = (f32[2,512,256]{2,1,0:T(8,128)S(1)}, f32[2,512,256]{2,1,0:T(8,128)S(1)}, u32[]{:S(2)}, u32[]{:S(2)}) collective-permute-start(f32[2,512,256]{2,1,0:T(8,128)S(1)} %pad_maximum_fusion.own_ref), channel_id=1, source_target_pairs={{0,32},{1,33},{2,34},{3,35},{4,36},{5,37},{6,38},{7,39},{8,40},{9,... | collective-permute-start | bytes 3145736 | tf_op jit(solution)/shard_map/ppermute | solution.py:32
  157.4 2.2 %copy-start.4 = (f32[4,512,512]{2,1,0:T(8,128)S(1)}, f32[4,512,512]{2,1,0:T(8,128)}, u32[]{:S(2)}) copy-start(f32[4,512,512]{2,1,0:T(8,128)} %solve_rows.1.p_ref) | copy-start | bytes 12582916

commit v5 on v4

--- a/solution.py
+++ b/solution.py
@@ -333,7 +333,7 @@
 
 
 def update_kernel(
-    info_ref, m_ref, p_ref, own_ref, other_ref, l0_ref, w0_ref, p10_ref, l1_ref, w1_ref, o_ref, x_s, chi, clo
+    info_ref, m_ref, p_ref, own_ref, other_ref, l0_ref, w0_ref, p10_ref, l1_ref, w1_ref, o_ref, x_s, right
 ):
     t = pl.program_id(0)
     p, q, keep_own, x = info_ref[0], info_ref[1], info_ref[2], info_ref[4]
@@ -350,8 +350,9 @@
         second = dot_nn(w1_ref[...], x_s[1].T - dot_nn(p10_ref[...], first))
         for k, panel in enumerate((first, second)):
             hi, lo = split(panel)
-            chi[k * N : k * N + N, :] = hi
-            clo[k * N : k * N + N, :] = lo
+            for group, value in enumerate((hi, lo, hi)):
+                at = 2 * N * group + N * k
+                right[at : at + N, :] = value
 
     def put(h, b, value):
         for half in range(2):
@@ -362,9 +363,8 @@
 
     def change(h, b):
         hi, lo = split(p_ref[0, h * N : h * N + N, :])
-        cols = slice(b * N, b * N + N)
-
-        product = dot16(lo, chi[:, cols]) + dot16(hi, clo[:, cols]) + dot16(hi, chi[:, cols])
+        left = jnp.concatenate([lo, hi, hi], 1)
+        product = dot16(left, right[:, b * N : b * N + N])
         put(h, b, get(h, b) - product)
 
     @pl.when(q > 1)
@@ -417,7 +417,7 @@
             + [whole(2, 2 * N, N)] * 2
             + [whole(N, N)] * 5,
             out_specs=tiles,
-            scratch_shapes=[pltpu.VMEM((2, 2 * N, N), F32)] + [pltpu.VMEM((2 * N, 2 * N), BF16)] * 2,
+            scratch_shapes=[pltpu.VMEM((2, 2 * N, N), F32)] + [pltpu.VMEM((6 * N, 2 * N), BF16)],
         ),
         out_shape=jax.ShapeDtypeStruct(flat_blocks.shape, F32),
         compiler_params=pltpu.CompilerParams(vmem_limit_bytes=40 << 20, dimension_semantics=("arbitrary",)),

time: 167 us -> 167 us (level)
  no operation moved by 1% of the time
where the time goes in v5:
time: 167 us; the launch traced here: 166 us
  starting transfers between devices  60.5 us (36%)
  waiting for transfers between devices  50.3 us (30%)
  Pallas kernels  44.6 us (27%)
  local copies, waits for them, and re-layouts  9.36 us (6%)
    ppermute x22, starting transfers between devices, send(): return lax.ppermute(value, ('row', 'col'), pairs(fn))  41.7 us
    ppermute x22, waiting for transfers between devices, send(): return lax.ppermute(value, ('row', 'col'), pairs(fn))  29.4 us
    pallas_call x1, Pallas kernels, factor(): pl.pallas_call(factor_kernel, out_shape=[jax.ShapeDtypeStruct((N, N), F32...  21.9 us
    all_to_all x1, waiting for transfers between devices, on_device(): lax.all_to_all(column[0][0].reshape(32, 8, N), 'col', 0, 0, tiled=True)[:2]  15.7 us
    pallas_call x1, Pallas kernels, solve_rows(): pl.pallas_call(rows_kernel, grid=(4,), in_specs=[pl.BlockSpec(memory_spac...  10.3 us
    all_to_all x1, starting transfers between devices, on_device(): lax.all_to_all(jnp.broadcast_to(core_rows[None], (32, 3, 8, 128)), 'col',...  6.73 us
    pallas_call x1, Pallas kernels, update(): pl.pallas_call(update_kernel, grid_spec=pltpu.PrefetchScalarGridSpec(num_...  6.25 us
    all_to_all x1, starting transfers between devices, on_device(): lax.all_to_all(column[0][0].reshape(32, 8, N), 'col', 0, 0, tiled=True)[:2]  6.06 us
  transfers between devices with their start and end apart: 25, of which 11 were waited for; matrix products, arithmetic and copies ran while one was open for 2% of the time, Pallas kernels for 23%

profile of v5, /device:TPU:1, one launch (start us, length us, event | category | flops | bytes accessed | tf_op | source)
XLA Modules:
  0.0 165.9 jit_solution(5031165418560925932)
XLA Ops:
  0.0 2.2 %copy-done = f32[8,1,256,2,1,256]{5,4,3,2,1,0:T(1,128)S(1)} copy-done((f32[8,1,256,2,1,256]{5,4,3,2,1,0:T(1,128)S(1)}, f32[8,1,256,2,1,256]{5,4,3,2,1,0:T(1,128)}, u32[]{:S(2)}) %copy-start) | copy-done | bytes 4194328
  2.2 0.4 first_column.1
  2.6 5.2 %collective-permute-start = (f32[2,256,256]{2,1,0:T(8,128)S(1)}, f32[2,256,256]{2,1,0:T(8,128)S(1)}, u32[]{:S(2)}, u32[]{:S(2)}) collective-permute-start(f32[2,256,256]{2,1,0:T(8,128)S(1)} %get-tuple-element.28), channel_id=1, source_target_pairs={{0,24},{1,25},{32,56},{33,57},{64,88},{65,89},{96,120},{97,121},{1... | collective-permute-start | bytes 1572872 | tf_op jit(solution)/shard_map/ppermute | solution.py:32
  7.9 1.3 collective-permute-start.1
  9.2 2.1 %collective-permute-start.2 = (f32[2,256,256]{2,1,0:T(8,128)S(1)}, f32[2,256,256]{2,1,0:T(8,128)}, u32[]{:S(2)}, u32[]{:S(2)}) collective-permute-start(f32[2,256,256]{2,1,0:T(8,128)S(1)} %get-tuple-element.30), channel_id=1, source_target_pairs={{0,8},{1,9},{32,40},{33,41},{64,72},{65,73},{96,104},{97,105},{128... | collective-permute-start | bytes 1572872 | tf_op jit(solution)/shard_map/ppermute | solution.py:32
  11.3 0.7 slice_bitcast_fusion
  12.0 6.1 %all-to-all-start = ((f32[32,8,256]{2,1,0:T(8,128)}), f32[32,8,256]{2,1,0:T(8,128)S(1)}, u32[]{:S(2)}, u32[]{:S(2)}) async-start(f32[32,8,256]{2,1,0:T(8,128)} %slice_bitcast_fusion), calls=%async_computation | async-start | bytes 524288 | tf_op jit(solution)/shard_map/all_to_all | solution.py:452
  18.1 15.7 %all-to-all-done = f32[32,8,256]{2,1,0:T(8,128)S(1)} async-done(((f32[32,8,256]{2,1,0:T(8,128)}), f32[32,8,256]{2,1,0:T(8,128)S(1)}, u32[]{:S(2)}, u32[]{:S(2)}) %all-to-all-start) | async-done | bytes 262176 | tf_op jit(solution)/shard_map/all_to_all | solution.py:452
  33.8 0.1 select_select_fusion
  34.0 0.7 broadcast_in_dim.9
  34.6 6.0 %all-to-all-start.1 = ((f32[8,2,8,256]{3,2,1,0:T(8,128)}), f32[8,2,8,256]{3,2,1,0:T(8,128)S(1)}, u32[]{:S(2)}, u32[]{:S(2)}) async-start(f32[8,2,8,256]{3,2,1,0:T(8,128)} %broadcast_in_dim.9), calls=%async_computation.1 | async-start | bytes 262144 | tf_op jit(solution)/shard_map/all_to_all | solution.py:466
  40.6 5.3 %all-to-all-done.1 = f32[8,2,8,256]{3,2,1,0:T(8,128)S(1)} async-done(((f32[8,2,8,256]{3,2,1,0:T(8,128)}), f32[8,2,8,256]{3,2,1,0:T(8,128)S(1)}, u32[]{:S(2)}, u32[]{:S(2)}) %all-to-all-start.1) | async-done | bytes 131104 | tf_op jit(solution)/shard_map/all_to_all | solution.py:466
  45.9 0.8 broadcast_in_dim.20
  46.7 6.7 %all-to-all-start.2 = ((f32[32,3,8,128]{3,2,1,0:T(8,128)}), f32[32,3,8,128]{3,2,1,0:T(8,128)S(1)}, u32[]{:S(2)}, u32[]{:S(2)}) async-start(f32[32,3,8,128]{3,2,1,0:T(8,128)} %broadcast_in_dim.20), calls=%async_computation.2 | async-start | bytes 786432 | tf_op jit(solution)/shard_map/all_to_all | solution.py:470
  53.6 4.0 %collective-permute-start.5 = (f32[128,256]{1,0:T(8,128)S(1)}, f32[128,256]{1,0:T(8,128)S(1)}, u32[]{:S(2)}, u32[]{:S(2)}) collective-permute-start(f32[128,256]{1,0:T(8,128)S(1)} %get-tuple-element.53), channel_id=1, source_target_pairs={{0,2},{1,3},{8,10},{9,11},{16,18},{17,19},{24,26},{25,27},{32,34},... | collective-permute-start | bytes 393224 | tf_op jit(solution)/shard_map/ppermute | solution.py:32
  57.6 3.7 %collective-permute-start.4 = (f32[128,256]{1,0:T(8,128)S(1)}, f32[128,256]{1,0:T(8,128)S(1)}, u32[]{:S(2)}, u32[]{:S(2)}) collective-permute-start(f32[128,256]{1,0:T(8,128)S(1)} %get-tuple-element.54), channel_id=1, source_target_pairs={{0,4},{1,5},{8,12},{9,13},{16,20},{17,21},{24,28},{25,29},{32,36},... | collective-permute-start | bytes 393224 | tf_op jit(solution)/shard_map/ppermute | solution.py:32
  61.3 1.3 collective-permute-start.3
  62.6 0.8 collective-permute-done.5
  63.4 3.2 %collective-permute-done.4 = f32[128,256]{1,0:T(8,128)S(1)} collective-permute-done((f32[128,256]{1,0:T(8,128)S(1)}, f32[128,256]{1,0:T(8,128)S(1)}, u32[]{:S(2)}, u32[]{:S(2)}) %collective-permute-start.4) | collective-permute-done | bytes 131104 | tf_op jit(solution)/shard_map/ppermute | solution.py:32
  66.6 5.0 %collective-permute-done.3 = f32[128,256]{1,0:T(8,128)S(1)} collective-permute-done((f32[128,256]{1,0:T(8,128)S(1)}, f32[128,256]{1,0:T(8,128)S(1)}, u32[]{:S(2)}, u32[]{:S(2)}) %collective-permute-start.3) | collective-permute-done | bytes 131104 | tf_op jit(solution)/shard_map/ppermute | solution.py:32
  71.7 0.6 collective-permute-start.9
  72.3 4.4 %collective-permute-start.8 = (f32[128,256]{1,0:T(8,128)S(1)}, f32[128,256]{1,0:T(8,128)S(1)}, u32[]{:S(2)}, u32[]{:S(2)}) collective-permute-start(f32[128,256]{1,0:T(8,128)S(1)} %fusion.2.refs_0_), channel_id=1, source_target_pairs={{0,6},{1,7},{2,0},{3,1},{4,2},{5,3},{6,4},{7,5},{8,14},{9,15},{10,... | collective-permute-start | bytes 393224 | tf_op jit(solution)/shard_map/ppermute | solution.py:32
  76.7 2.1 %collective-permute-start.6 = (f32[128,256]{1,0:T(8,128)S(1)}, f32[128,256]{1,0:T(8,128)S(1)}, u32[]{:S(2)}, u32[]{:S(2)}) collective-permute-start(f32[128,256]{1,0:T(8,128)S(1)} %fusion.2.refs_0_), channel_id=1, source_target_pairs={{0,2},{1,3},{2,4},{3,5},{4,6},{5,7},{6,0},{7,1},{8,10},{9,11},{10,... | collective-permute-start | bytes 393224 | tf_op jit(solution)/shard_map/ppermute | solution.py:32
  78.7 8.6 %collective-permute-done.8.refs_3_ = f32[128,256]{1,0:T(8,128)S(1)} collective-permute-done((f32[128,256]{1,0:T(8,128)S(1)}, f32[128,256]{1,0:T(8,128)S(1)}, u32[]{:S(2)}, u32[]{:S(2)}) %collective-permute-start.8) | collective-permute-done | bytes 131104 | tf_op jit(solution)/shard_map/ppermute | solution.py:32
  87.4 1.8 %collective-permute-done.6.refs_1_ = f32[128,256]{1,0:T(8,128)S(1)} collective-permute-done((f32[128,256]{1,0:T(8,128)S(1)}, f32[128,256]{1,0:T(8,128)S(1)}, u32[]{:S(2)}, u32[]{:S(2)}) %collective-permute-start.6) | collective-permute-done | bytes 131104 | tf_op jit(solution)/shard_map/ppermute | solution.py:32
  89.2 2.2 %collective-permute-start.14 = (f32[512,256]{1,0:T(8,128)S(1)}, f32[512,256]{1,0:T(8,128)S(1)}, u32[]{:S(2)}, u32[]{:S(2)}) collective-permute-start(f32[512,256]{1,0:T(8,128)S(1)} %order.1.a0), channel_id=1, source_target_pairs={{0,24},{1,25},{2,26},{3,27},{4,28},{5,29},{6,30},{7,31},{8,0},{9,1... | collective-permute-start | bytes 1572872 | tf_op jit(solution)/shard_map/ppermute | solution.py:32
  91.5 0.5 collective-permute-start.13
  92.0 0.6 collective-permute-start.12
  92.6 0.8 collective-permute-start.11
  93.3 3.6 %collective-permute-start.10 = (f32[512,256]{1,0:T(8,128)S(1)}, f32[512,256]{1,0:T(8,128)S(1)}, u32[]{:S(2)}, u32[]{:S(2)}) collective-permute-start(f32[512,256]{1,0:T(8,128)S(1)} %order.1.a0), channel_id=1, source_target_pairs={{0,1},{1,0},{2,3},{3,2},{4,5},{5,4},{6,7},{7,6},{8,9},{9,8},{10,11... | collective-permute-start | bytes 1572872 | tf_op jit(solution)/shard_map/ppermute | solution.py:32
  97.0 21.9 %factor.1 = (f32[256,256]{1,0:T(8,128)}, f32[256,256]{1,0:T(8,128)}, f32[256,256]{1,0:T(8,128)}, f32[256,256]{1,0:T(8,128)}, f32[256,256]{1,0:T(8,128)}) custom-call(s32[1]{0:T(128)} %bitcast.19.core_ref, f32[32,3,8,128]{3,2,1,0:T(8,128)} %copy-done.10, f32[32,3,8,128]{3,2,1,0:T(8,128)} %copy-done.13), custom_call_target="tpu_custom_call" | custom-call | flops 1000000000 | bytes 62914560 | tf_op jit(solution)/shard_map/factor/pallas_call | solution.py:180
  119.0 1.1 slice.78
  120.1 1.0 slice.77
  121.1 1.7 %collective-permute-start.16 = (f32[768,256]{1,0:T(8,128)S(1)}, f32[768,256]{1,0:T(8,128)}, u32[]{:S(2)}, u32[]{:S(2)}) collective-permute-start(f32[768,256]{1,0:T(8,128)S(1)} %pad_maximum_fusion.1), channel_id=1, source_target_pairs={{0,1},{1,0},{2,3},{3,2},{4,5},{5,4},{6,7},{7,6},{8,9},{9,8},{10,11... | collective-permute-start | bytes 2359304 | tf_op jit(solution)/shard_map/ppermute | solution.py:32
  123.0 0.4 collective-permute-start.15
  123.4 1.0 collective-permute-start.19
  124.3 1.2 collective-permute-start.18
  125.6 0.6 stack.48.info_ref
  126.2 5.7 %solve_own.1 = (f32[4,512,256]{2,1,0:T(8,128)}, f32[256,256]{1,0:T(8,128)}) custom-call(s32[5]{0:T(128)} %stack.48.info_ref, f32[256,256]{1,0:T(8,128)} %get-tuple-element.40.w0_ref, f32[256,256]{1,0:T(8,128)} %get-tuple-element.41.p10_ref, f32[256,256]{1,0:T(8,128)} %get-tuple-element.42.w1_ref, f32[512,256]{1,0:T(8,128)} %copy-done.2, ...), custom_call_target="tpu_custom_call" | custom-call | flops 2000000000 | bytes 62914560 | tf_op jit(solution)/shard_map/solve_own/pallas_call | solution.py:281
  131.9 6.8 %collective-permute-done.17.u1 = f32[256,256]{1,0:T(8,128)} collective-permute-done((f32[256,256]{1,0:T(8,128)S(1)}, f32[256,256]{1,0:T(8,128)}, u32[]{:S(2)}, u32[]{:S(2)}) %collective-permute-start.17) | collective-permute-done | bytes 262176 | tf_op jit(solution)/shard_map/ppermute | solution.py:32
  138.6 0.7 collective-permute-done.16.lower_ref
  139.4 2.6 %collective-permute-start.20 = (f32[512,256]{1,0:T(8,128)S(1)}, f32[512,256]{1,0:T(8,128)S(1)}, u32[]{:S(2)}, u32[]{:S(2)}) collective-permute-start(f32[512,256]{1,0:T(8,128)S(1)} %broadcast_select_fusion.1), channel_id=1, source_target_pairs={{0,1},{1,0},{2,3},{3,2},{4,5},{5,4},{6,7},{7,6},{8,9},{9,8},{10,11... | collective-permute-start | bytes 1572872 | tf_op jit(solution)/shard_map/ppermute | solution.py:32
  142.0 10.3 %solve_rows.1.p_ref = f32[4,512,512]{2,1,0:T(8,128)} custom-call(s32[5]{0:T(128)} %stack.48.info_ref, f32[256,256]{1,0:T(8,128)} %get-tuple-element.40.w0_ref, f32[256,256]{1,0:T(8,128)} %get-tuple-element.42.w1_ref, f32[256,256]{1,0:T(8,128)} %get-tuple-element.47.turned_ref, f32[4,512,256]{2,1,0:T(8,128)} %get-tuple-element.43.part_ref, ...), custom_call_target="tpu_custom_call" | custom-call | flops 5000000000 | bytes 9437184 | tf_op jit(solution)/shard_map/solve_rows/pallas_call | solution.py:319
  152.4 0.2 collective-permute-done.20
  152.8 2.4 %collective-permute-start.21 = (f32[2,512,256]{2,1,0:T(8,128)S(1)}, f32[2,512,256]{2,1,0:T(8,128)S(1)}, u32[]{:S(2)}, u32[]{:S(2)}) collective-permute-start(f32[2,512,256]{2,1,0:T(8,128)S(1)} %pad_maximum_fusion.own_ref), channel_id=1, source_target_pairs={{0,32},{1,33},{2,34},{3,35},{4,36},{5,37},{6,38},{7,39},{8,40},{9,... | collective-permute-start | bytes 3145736 | tf_op jit(solution)/shard_map/ppermute | solution.py:32
  155.1 2.3 %collective-permute-done.21.other_ref = f32[2,512,256]{2,1,0:T(8,128)S(1)} collective-permute-done((f32[2,512,256]{2,1,0:T(8,128)S(1)}, f32[2,512,256]{2,1,0:T(8,128)S(1)}, u32[]{:S(2)}, u32[]{:S(2)}) %collective-permute-start.21) | collective-permute-done | bytes 1048608 | tf_op jit(solution)/shard_map/ppermute | solution.py:32
  157.5 2.2 %copy-done.4 = f32[4,512,512]{2,1,0:T(8,128)S(1)} copy-done((f32[4,512,512]{2,1,0:T(8,128)S(1)}, f32[4,512,512]{2,1,0:T(8,128)}, u32[]{:S(2)}) %copy-start.4) | copy-done | bytes 4194328
  159.6 6.2 %update.1 = f32[2,4096,128]{2,1,0:T(8,128)} custom-call(s32[5]{0:T(128)S(1)} %copy-done.3, f32[2,4096,128]{2,1,0:T(8,128)S(1)} %bitcast.42, f32[4,512,512]{2,1,0:T(8,128)S(1)} %copy-done.4, f32[2,512,256]{2,1,0:T(8,128)S(1)} %pad_maximum_fusion.own_ref, f32[2,512,256]{2,1,0:T(8,128)S(1)} %collective-permute-done.21.other_ref, f32[256,256]{1,0:T(8,128)S(1)} %copy-done.5, ...), custom_call_target="tpu_custom_call" | custom-call | flops 5000000000 | bytes 16777216 | tf_op jit(solution)/shard_map/update/pallas_call | solution.py:411
  (62 shorter events, 0.6 us)
Async XLA Ops:
  0.0 2.2 %copy-start = (f32[8,1,256,2,1,256]{5,4,3,2,1,0:T(1,128)S(1)}, f32[8,1,256,2,1,256]{5,4,3,2,1,0:T(1,128)}, u32[]{:S(2)}) copy-start(f32[8,1,256,2,1,256]{5,4,3,2,1,0:T(1,128)} %param.1) | copy-start | bytes 12582916
  2.6 31.2 %collective-permute-start = (f32[2,256,256]{2,1,0:T(8,128)S(1)}, f32[2,256,256]{2,1,0:T(8,128)S(1)}, u32[]{:S(2)}, u32[]{:S(2)}) collective-permute-start(f32[2,256,256]{2,1,0:T(8,128)S(1)} %get-tuple-element.28), channel_id=1, source_target_pairs={{0,24},{1,25},{32,56},{33,57},{64,88},{65,89},{96,120},{97,121},{1... | collective-permute-start | bytes 1572872 | tf_op jit(solution)/shard_map/ppermute | solution.py:32
  7.9 25.9 %collective-permute-start.1 = (f32[2,256,256]{2,1,0:T(8,128)S(1)}, f32[2,256,256]{2,1,0:T(8,128)S(1)}, u32[]{:S(2)}, u32[]{:S(2)}) collective-permute-start(f32[2,256,256]{2,1,0:T(8,128)S(1)} %get-tuple-element.29), channel_id=1, source_target_pairs={{0,16},{1,17},{32,48},{33,49},{64,80},{65,81},{96,112},{97,113},{1... | collective-permute-start | bytes 1572872 | tf_op jit(solution)/shard_map/ppermute | solution.py:32
  9.2 24.6 %collective-permute-start.2 = (f32[2,256,256]{2,1,0:T(8,128)S(1)}, f32[2,256,256]{2,1,0:T(8,128)}, u32[]{:S(2)}, u32[]{:S(2)}) collective-permute-start(f32[2,256,256]{2,1,0:T(8,128)S(1)} %get-tuple-element.30), channel_id=1, source_target_pairs={{0,8},{1,9},{32,40},{33,41},{64,72},{65,73},{96,104},{97,105},{128... | collective-permute-start | bytes 1572872 | tf_op jit(solution)/shard_map/ppermute | solution.py:32
  12.0 21.8 %all-to-all-start = ((f32[32,8,256]{2,1,0:T(8,128)}), f32[32,8,256]{2,1,0:T(8,128)S(1)}, u32[]{:S(2)}, u32[]{:S(2)}) async-start(f32[32,8,256]{2,1,0:T(8,128)} %slice_bitcast_fusion), calls=%async_computation | async-start | bytes 524288 | tf_op jit(solution)/shard_map/all_to_all | solution.py:452
  34.6 11.3 %all-to-all-start.1 = ((f32[8,2,8,256]{3,2,1,0:T(8,128)}), f32[8,2,8,256]{3,2,1,0:T(8,128)S(1)}, u32[]{:S(2)}, u32[]{:S(2)}) async-start(f32[8,2,8,256]{3,2,1,0:T(8,128)} %broadcast_in_dim.9), calls=%async_computation.1 | async-start | bytes 262144 | tf_op jit(solution)/shard_map/all_to_all | solution.py:466
  46.7 24.9 %all-to-all-start.2 = ((f32[32,3,8,128]{3,2,1,0:T(8,128)}), f32[32,3,8,128]{3,2,1,0:T(8,128)S(1)}, u32[]{:S(2)}, u32[]{:S(2)}) async-start(f32[32,3,8,128]{3,2,1,0:T(8,128)} %broadcast_in_dim.20), calls=%async_computation.2 | async-start | bytes 786432 | tf_op jit(solution)/shard_map/all_to_all | solution.py:470
  53.6 9.8 %collective-permute-start.5 = (f32[128,256]{1,0:T(8,128)S(1)}, f32[128,256]{1,0:T(8,128)S(1)}, u32[]{:S(2)}, u32[]{:S(2)}) collective-permute-start(f32[128,256]{1,0:T(8,128)S(1)} %get-tuple-element.53), channel_id=1, source_target_pairs={{0,2},{1,3},{8,10},{9,11},{16,18},{17,19},{24,26},{25,27},{32,34},... | collective-permute-start | bytes 393224 | tf_op jit(solution)/shard_map/ppermute | solution.py:32
  57.6 9.0 %collective-permute-start.4 = (f32[128,256]{1,0:T(8,128)S(1)}, f32[128,256]{1,0:T(8,128)S(1)}, u32[]{:S(2)}, u32[]{:S(2)}) collective-permute-start(f32[128,256]{1,0:T(8,128)S(1)} %get-tuple-element.54), channel_id=1, source_target_pairs={{0,4},{1,5},{8,12},{9,13},{16,20},{17,21},{24,28},{25,29},{32,36},... | collective-permute-start | bytes 393224 | tf_op jit(solution)/shard_map/ppermute | solution.py:32
  61.3 10.3 %collective-permute-start.3 = (f32[128,256]{1,0:T(8,128)S(1)}, f32[128,256]{1,0:T(8,128)S(1)}, u32[]{:S(2)}, u32[]{:S(2)}) collective-permute-start(f32[128,256]{1,0:T(8,128)S(1)} %get-tuple-element.55), channel_id=1, source_target_pairs={{0,6},{1,7},{8,14},{9,15},{16,22},{17,23},{24,30},{25,31},{32,38},... | collective-permute-start | bytes 393224 | tf_op jit(solution)/shard_map/ppermute | solution.py:32
  71.6 25.3 %copy-start.10 = (f32[32,3,8,128]{3,2,1,0:T(8,128)}, f32[32,3,8,128]{3,2,1,0:T(8,128)S(1)}, u32[]{:S(2)}) copy-start(f32[32,3,8,128]{3,2,1,0:T(8,128)S(1)} %all-to-all-done.2.own_ref) | copy-start | bytes 1179652
  71.7 17.6 %collective-permute-start.9 = (f32[32,3,8,128]{3,2,1,0:T(8,128)S(1)}, f32[32,3,8,128]{3,2,1,0:T(8,128)S(1)}, u32[]{:S(2)}, u32[]{:S(2)}) collective-permute-start(f32[32,3,8,128]{3,2,1,0:T(8,128)S(1)} %all-to-all-done.2.own_ref), channel_id=1, source_target_pairs={{0,32},{1,33},{2,34},{3,35},{4,36},{5,37},{6,38},{7,39},{8,40},{9,... | collective-permute-start | bytes 1179656 | tf_op jit(solution)/shard_map/ppermute | solution.py:32
  72.3 15.1 %collective-permute-start.8 = (f32[128,256]{1,0:T(8,128)S(1)}, f32[128,256]{1,0:T(8,128)S(1)}, u32[]{:S(2)}, u32[]{:S(2)}) collective-permute-start(f32[128,256]{1,0:T(8,128)S(1)} %fusion.2.refs_0_), channel_id=1, source_target_pairs={{0,6},{1,7},{2,0},{3,1},{4,2},{5,3},{6,4},{7,5},{8,14},{9,15},{10,... | collective-permute-start | bytes 393224 | tf_op jit(solution)/shard_map/ppermute | solution.py:32
  76.6 10.7 %collective-permute-start.7 = (f32[128,256]{1,0:T(8,128)S(1)}, f32[128,256]{1,0:T(8,128)S(1)}, u32[]{:S(2)}, u32[]{:S(2)}) collective-permute-start(f32[128,256]{1,0:T(8,128)S(1)} %fusion.2.refs_0_), channel_id=1, source_target_pairs={{0,4},{1,5},{2,6},{3,7},{4,0},{5,1},{6,2},{7,3},{8,12},{9,13},{10,... | collective-permute-start | bytes 393224 | tf_op jit(solution)/shard_map/ppermute | solution.py:32
  76.7 12.5 %collective-permute-start.6 = (f32[128,256]{1,0:T(8,128)S(1)}, f32[128,256]{1,0:T(8,128)S(1)}, u32[]{:S(2)}, u32[]{:S(2)}) collective-permute-start(f32[128,256]{1,0:T(8,128)S(1)} %fusion.2.refs_0_), channel_id=1, source_target_pairs={{0,2},{1,3},{2,4},{3,5},{4,6},{5,7},{6,0},{7,1},{8,10},{9,11},{10,... | collective-permute-start | bytes 393224 | tf_op jit(solution)/shard_map/ppermute | solution.py:32
  89.2 33.8 %copy-start.2 = (f32[512,256]{1,0:T(8,128)}, f32[512,256]{1,0:T(8,128)S(1)}, u32[]{:S(2)}) copy-start(f32[512,256]{1,0:T(8,128)S(1)} %order.1.a0) | copy-start | bytes 1572868
  89.2 7.7 %copy-start.13 = (f32[32,3,8,128]{3,2,1,0:T(8,128)}, f32[32,3,8,128]{3,2,1,0:T(8,128)S(1)}, u32[]{:S(2)}) copy-start(f32[32,3,8,128]{3,2,1,0:T(8,128)S(1)} %collective-permute-done.9.other_ref) | copy-start | bytes 1179652
  89.2 29.7 %collective-permute-start.14 = (f32[512,256]{1,0:T(8,128)S(1)}, f32[512,256]{1,0:T(8,128)S(1)}, u32[]{:S(2)}, u32[]{:S(2)}) collective-permute-start(f32[512,256]{1,0:T(8,128)S(1)} %order.1.a0), channel_id=1, source_target_pairs={{0,24},{1,25},{2,26},{3,27},{4,28},{5,29},{6,30},{7,31},{8,0},{9,1... | collective-permute-start | bytes 1572872 | tf_op jit(solution)/shard_map/ppermute | solution.py:32
  91.5 27.5 %collective-permute-start.13 = (f32[512,256]{1,0:T(8,128)S(1)}, f32[512,256]{1,0:T(8,128)}, u32[]{:S(2)}, u32[]{:S(2)}) collective-permute-start(f32[512,256]{1,0:T(8,128)S(1)} %order.1.a0), channel_id=1, source_target_pairs={{0,16},{1,17},{2,18},{3,19},{4,20},{5,21},{6,22},{7,23},{8,24},{9,... | collective-permute-start | bytes 1572872 | tf_op jit(solution)/shard_map/ppermute | solution.py:32
  92.0 28.1 %collective-permute-start.12 = (f32[512,256]{1,0:T(8,128)S(1)}, f32[512,256]{1,0:T(8,128)}, u32[]{:S(2)}, u32[]{:S(2)}) collective-permute-start(f32[512,256]{1,0:T(8,128)S(1)} %order.1.a0), channel_id=1, source_target_pairs={{0,8},{1,9},{2,10},{3,11},{4,12},{5,13},{6,14},{7,15},{8,16},{9,17... | collective-permute-start | bytes 1572872 | tf_op jit(solution)/shard_map/ppermute | solution.py:32
  92.6 30.3 %collective-permute-start.11 = (f32[512,256]{1,0:T(8,128)S(1)}, f32[512,256]{1,0:T(8,128)S(1)}, u32[]{:S(2)}, u32[]{:S(2)}) collective-permute-start(f32[512,256]{1,0:T(8,128)S(1)} %order.1.a0), channel_id=1, source_target_pairs={{0,128},{1,129},{2,130},{3,131},{4,132},{5,133},{6,134},{7,135},{8... | collective-permute-start | bytes 1572872 | tf_op jit(solution)/shard_map/ppermute | solution.py:32
  93.3 29.6 %collective-permute-start.10 = (f32[512,256]{1,0:T(8,128)S(1)}, f32[512,256]{1,0:T(8,128)S(1)}, u32[]{:S(2)}, u32[]{:S(2)}) collective-permute-start(f32[512,256]{1,0:T(8,128)S(1)} %order.1.a0), channel_id=1, source_target_pairs={{0,1},{1,0},{2,3},{3,2},{4,5},{5,4},{6,7},{7,6},{8,9},{9,8},{10,11... | collective-permute-start | bytes 1572872 | tf_op jit(solution)/shard_map/ppermute | solution.py:32
  118.9 1.2 copy-start.12
  121.1 18.2 %collective-permute-start.16 = (f32[768,256]{1,0:T(8,128)S(1)}, f32[768,256]{1,0:T(8,128)}, u32[]{:S(2)}, u32[]{:S(2)}) collective-permute-start(f32[768,256]{1,0:T(8,128)S(1)} %pad_maximum_fusion.1), channel_id=1, source_target_pairs={{0,1},{1,0},{2,3},{3,2},{4,5},{5,4},{6,7},{7,6},{8,9},{9,8},{10,11... | collective-permute-start | bytes 2359304 | tf_op jit(solution)/shard_map/ppermute | solution.py:32
  123.0 16.4 %copy-start.11 = (f32[512,256]{1,0:T(8,128)}, f32[512,256]{1,0:T(8,128)S(1)}, u32[]{:S(2)}) copy-start(f32[512,256]{1,0:T(8,128)S(1)} %collective-permute-done.10.others_ref) | copy-start | bytes 1572868
  123.0 15.7 %collective-permute-start.15 = (f32[512,256]{1,0:T(8,128)S(1)}, f32[512,256]{1,0:T(8,128)S(1)}, u32[]{:S(2)}, u32[]{:S(2)}) collective-permute-start(f32[512,256]{1,0:T(8,128)S(1)} %broadcast_select_fusion), channel_id=1, source_target_pairs={{0,64},{1,65},{2,66},{3,67},{4,68},{5,69},{6,70},{7,71},{8,72},{9,... | collective-permute-start | bytes 1572872 | tf_op jit(solution)/shard_map/ppermute | solution.py:32
  123.4 8.5 %collective-permute-start.19 = (f32[256,256]{1,0:T(8,128)S(1)}, f32[256,256]{1,0:T(8,128)S(1)}, u32[]{:S(2)}, u32[]{:S(2)}) collective-permute-start(f32[256,256]{1,0:T(8,128)S(1)} %slice.66), channel_id=1, source_target_pairs={{0,24},{1,25},{2,26},{3,27},{4,28},{5,29},{6,30},{7,31},{8,0},{9,1... | collective-permute-start | bytes 786440 | tf_op jit(solution)/shard_map/ppermute | solution.py:32
  124.3 7.5 %collective-permute-start.18 = (f32[256,256]{1,0:T(8,128)S(1)}, f32[256,256]{1,0:T(8,128)S(1)}, u32[]{:S(2)}, u32[]{:S(2)}) collective-permute-start(f32[256,256]{1,0:T(8,128)S(1)} %slice.66), channel_id=1, source_target_pairs={{0,16},{1,17},{2,18},{3,19},{4,20},{5,21},{6,22},{7,23},{8,24},{9,... | collective-permute-start | bytes 786440 | tf_op jit(solution)/shard_map/ppermute | solution.py:32
  125.6 13.1 %collective-permute-start.17 = (f32[256,256]{1,0:T(8,128)S(1)}, f32[256,256]{1,0:T(8,128)}, u32[]{:S(2)}, u32[]{:S(2)}) collective-permute-start(f32[256,256]{1,0:T(8,128)S(1)} %slice.66), channel_id=1, source_target_pairs={{0,8},{1,9},{2,10},{3,11},{4,12},{5,13},{6,14},{7,15},{8,16},{9,17... | collective-permute-start | bytes 786440 | tf_op jit(solution)/shard_map/ppermute | solution.py:32
  131.8 10.2 %copy-start.14 = (f32[256,256]{1,0:T(8,128)}, f32[256,256]{1,0:T(8,128)S(1)}, u32[]{:S(2)}) copy-start(f32[256,256]{1,0:T(8,128)S(1)} %collective-permute-done.19.u3) | copy-start | bytes 786436
  131.9 7.4 %copy-start.15 = (f32[256,256]{1,0:T(8,128)}, f32[256,256]{1,0:T(8,128)S(1)}, u32[]{:S(2)}) copy-start(f32[256,256]{1,0:T(8,128)S(1)} %collective-permute-done.18.u2) | copy-start | bytes 786436
  139.4 13.2 %collective-permute-start.20 = (f32[512,256]{1,0:T(8,128)S(1)}, f32[512,256]{1,0:T(8,128)S(1)}, u32[]{:S(2)}, u32[]{:S(2)}) collective-permute-start(f32[512,256]{1,0:T(8,128)S(1)} %broadcast_select_fusion.1), channel_id=1, source_target_pairs={{0,1},{1,0},{2,3},{3,2},{4,5},{5,4},{6,7},{7,6},{8,9},{9,8},{10,11... | collective-permute-start | bytes 1572872 | tf_op jit(solution)/shard_map/ppermute | solution.py:32
  142.0 15.4 %copy-start.5 = (f32[256,256]{1,0:T(8,128)S(1)}, f32[256,256]{1,0:T(8,128)}, u32[]{:S(2)}) copy-start(f32[256,256]{1,0:T(8,128)} %get-tuple-element.50.l0_ref) | copy-start | bytes 786436
  142.0 15.4 %copy-start.6 = (f32[256,256]{1,0:T(8,128)S(1)}, f32[256,256]{1,0:T(8,128)}, u32[]{:S(2)}) copy-start(f32[256,256]{1,0:T(8,128)} %get-tuple-element.40.w0_ref) | copy-start | bytes 786436
  142.0 15.4 %copy-start.7 = (f32[256,256]{1,0:T(8,128)S(1)}, f32[256,256]{1,0:T(8,128)}, u32[]{:S(2)}) copy-start(f32[256,256]{1,0:T(8,128)} %get-tuple-element.41.p10_ref) | copy-start | bytes 786436
  142.0 15.4 %copy-start.8 = (f32[256,256]{1,0:T(8,128)S(1)}, f32[256,256]{1,0:T(8,128)}, u32[]{:S(2)}) copy-start(f32[256,256]{1,0:T(8,128)} %get-tuple-element.38.l1_ref) | copy-start | bytes 786436
  142.0 15.4 %copy-start.9 = (f32[256,256]{1,0:T(8,128)S(1)}, f32[256,256]{1,0:T(8,128)}, u32[]{:S(2)}) copy-start(f32[256,256]{1,0:T(8,128)} %get-tuple-element.42.w1_ref) | copy-start | bytes 786436
  152.4 5.1 %copy-start.1 = (f32[8,1,256,2,1,256]{5,4,3,2,1,0:T(1,128)S(1)}, f32[8,1,256,2,1,256]{5,4,3,2,1,0:T(1,128)}, u32[]{:S(2)}) copy-start(f32[8,1,256,2,1,256]{5,4,3,2,1,0:T(1,128)} %param.1) | copy-start | bytes 12582916
  152.4 5.1 %copy-start.3 = (s32[5]{0:T(128)S(1)}, s32[5]{0:T(128)}, u32[]{:S(2)}) copy-start(s32[5]{0:T(128)} %stack.48.info_ref) | copy-start | bytes 64
  152.8 4.6 %collective-permute-start.21 = (f32[2,512,256]{2,1,0:T(8,128)S(1)}, f32[2,512,256]{2,1,0:T(8,128)S(1)}, u32[]{:S(2)}, u32[]{:S(2)}) collective-permute-start(f32[2,512,256]{2,1,0:T(8,128)S(1)} %pad_maximum_fusion.own_ref), channel_id=1, source_target_pairs={{0,32},{1,33},{2,34},{3,35},{4,36},{5,37},{6,38},{7,39},{8,40},{9,... | collective-permute-start | bytes 3145736 | tf_op jit(solution)/shard_map/ppermute | solution.py:32
  157.4 2.2 %copy-start.4 = (f32[4,512,512]{2,1,0:T(8,128)S(1)}, f32[4,512,512]{2,1,0:T(8,128)}, u32[]{:S(2)}) copy-start(f32[4,512,512]{2,1,0:T(8,128)} %solve_rows.1.p_ref) | copy-start | bytes 12582916
